TPU v7x, 512 devices: a whole 4x4x16 slice. The times are simulated.
512 devices in a mesh: section: 4 (over z_hi, core), ctx: 128 (over z_lo, x, y).
Axes of the slice: x: 4, y: 4, z: 16 (z_hi: 2, z_lo: 8; z = z_hi * 8 + z_lo), core: 2. Of those that a mesh axis runs over, the one named last changes fastest.
Arguments:
- query: bfloat16 [4, 2048, 6144], P('section', 'ctx'), may hold values from -96 to 96
- key: bfloat16 [4, 2048, 1024], P('section', 'ctx'), may hold values from -9.6 to 9.6
- value: bfloat16 [4, 2048, 1024], P('section', 'ctx'), may hold values from -6 to 6
- clean_key: bfloat16 [4, 2048, 1024], P('section', 'ctx'), may hold values from -9.5625 to 9.5625
- clean_value: bfloat16 [4, 2048, 1024], P('section', 'ctx'), may hold values from -6 to 6
- completing: int32 [1], replicated, may hold values from 0 to 2
- span_mask: int32 [4, 4], replicated, may hold values from 0 to 1, as said below
Outputs:
- attended: bfloat16 [4, 2048, 6144], P('section', 'ctx')
Inputs may be any that keep to these rules, and one draw needn't show every extreme that they name: span_mask is 1 on the diagonal and just below it, 0 above it, and 0 or 1 elsewhere below it.
All inputs are finite; a program needn't handle non-finite values.
Results may differ from a plain program's by a relative error of at most 0.0045.
Values may be sent and summed in bfloat16 or wider, within the bound.
No kernel may reach another device: no remote copies, remote signals or barrier semaphores. Data moves between devices by JAX's collectives and lax.ppermute only.
A program may use at most 64 MiB of HBM per device.

v0:
```python
import math

import jax
import jax.numpy as jnp
from jax import lax
from jax.sharding import PartitionSpec as P

HEAD_DIM = 128
HEADS = 48
KV_HEADS = 8


def from_root(array, axis, root):
    mine = lax.axis_index(axis) == root
    return lax.psum(jnp.where(mine, array, jnp.zeros_like(array)), axis)


def update_state(state, query_rows, block_keys, block_values, usable):
    largest, total, summed = state
    scale = query_rows.shape[-1] ** (-0.5)
    scores = (
        jnp.einsum("sgd,nd->gsn", query_rows, block_keys, preferred_element_type=jnp.float32)
        * scale
    )
    scores = jnp.where(usable, scores, -1e30)
    newest = jnp.maximum(largest, jnp.max(scores, axis=-1))
    factor = jnp.exp(largest - newest)
    weights = jnp.exp(scores - newest[..., None])
    total = total * factor + jnp.sum(weights, axis=-1)
    weights_b = weights.astype(jnp.bfloat16)
    summed = summed * factor[..., None] + jnp.einsum(
        "gsn,nd->gsd", weights_b, block_values, preferred_element_type=jnp.float32
    )
    return (newest, total, summed)


def attend_keys(state, query_rows, keys_rows, values_rows, usable):
    length = keys_rows.shape[0]
    width = math.gcd(length, 1024)
    key_blocks = keys_rows.reshape(length // width, width, keys_rows.shape[-1])
    value_blocks = values_rows.reshape(length // width, width, values_rows.shape[-1])

    def step_block(carry, blocks):
        return (update_state(carry, query_rows, blocks[0], blocks[1], usable), None)

    state, unused = lax.scan(step_block, state, (key_blocks, value_blocks))
    return state


def spread_heads(array, copies):
    tok_rows = array.shape[1]
    shaped = array.reshape(tok_rows, KV_HEADS, 1, HEAD_DIM)
    copied = jnp.broadcast_to(shaped, (tok_rows, KV_HEADS, copies, HEAD_DIM))
    return copied.reshape(tok_rows, KV_HEADS * copies, HEAD_DIM)


def shards(query, key, value, clean_key, clean_value, completing, span_mask):
    tok_rows = query.shape[1]
    group = HEADS // KV_HEADS
    devices_ctx = lax.axis_size("ctx")
    copies = devices_ctx // KV_HEADS
    sub_rows = tok_rows // copies
    section_now = lax.axis_index("section")
    finished = completing[0]
    seen = jnp.logical_and(section_now > finished, span_mask[section_now, finished] == 1)
    arranged_query = query.reshape(copies, sub_rows, KV_HEADS, group * HEAD_DIM)
    arranged_query = jnp.transpose(arranged_query, (2, 0, 1, 3)).reshape(
        devices_ctx, sub_rows, group * HEAD_DIM
    )
    served = lax.all_to_all(arranged_query, "ctx", split_axis=0, concat_axis=1, tiled=True)
    query_rows = served.reshape(devices_ctx * sub_rows, group, HEAD_DIM)
    handed_keys, handed_values = (
        from_root(clean_key, "section", finished),
        from_root(clean_value, "section", finished),
    )
    own_keys, own_values, far_keys, far_values = (
        lax.all_to_all(spread_heads(key, copies), "ctx", split_axis=1, concat_axis=0, tiled=True),
        lax.all_to_all(spread_heads(value, copies), "ctx", split_axis=1, concat_axis=0, tiled=True),
        lax.all_to_all(
            spread_heads(handed_keys, copies), "ctx", split_axis=1, concat_axis=0, tiled=True
        ),
        lax.all_to_all(
            spread_heads(handed_values, copies), "ctx", split_axis=1, concat_axis=0, tiled=True
        ),
    )
    own_keys = own_keys.reshape(-1, HEAD_DIM)
    own_values = own_values.reshape(-1, HEAD_DIM)
    far_keys = far_keys.reshape(-1, HEAD_DIM)
    far_values = far_values.reshape(-1, HEAD_DIM)
    served_rows = query_rows.shape[0]
    state = (
        jnp.full((group, served_rows), -1e30, jnp.float32),
        jnp.zeros((group, served_rows), jnp.float32),
        jnp.zeros((group, served_rows, HEAD_DIM), jnp.float32),
    )
    state = attend_keys(state, query_rows, own_keys, own_values, True)
    state = attend_keys(state, query_rows, far_keys, far_values, seen)
    largest, total, summed = state
    result = summed / total[..., None]
    result = jnp.transpose(result, (1, 0, 2)).astype(jnp.bfloat16)
    result = result.reshape(devices_ctx, sub_rows, group * HEAD_DIM)
    returned = lax.all_to_all(result, "ctx", split_axis=0, concat_axis=1, tiled=True)
    returned = returned.reshape(KV_HEADS, copies, sub_rows, group * HEAD_DIM)
    returned = jnp.transpose(returned, (1, 2, 0, 3))
    return returned.reshape(1, tok_rows, HEADS * HEAD_DIM)


def solution(mesh):
    placed = (
        P("section", "ctx", None),
        P("section", "ctx", None),
        P("section", "ctx", None),
        P("section", "ctx", None),
        P("section", "ctx", None),
        P(),
        P(),
    )
    return jax.shard_map(
        shards, mesh=mesh, in_specs=placed, out_specs=P("section", "ctx", None), check_vma=False
    )
```

profile of v0, /device:TPU:1, one launch (start us, length us, event | category | flops | bytes accessed | tf_op | source)
XLA Modules:
  0.0 301.7 jit_solution(3847588074964403546)
XLA Ops:
  6.5 1.0 copy.56
  8.2 0.8 reduce
  9.7 20.4 %all-to-all-start.1 = ((bf16[128,2,384]{2,1,0:T(2,128)(2,1)}), bf16[128,2,384]{2,1,0:T(2,128)(2,1)S(1)}, u32[]{:S(2)}, u32[]{:S(2)}) async-start(bf16[128,2,384]{2,1,0:T(2,128)(2,1)} %reshape.71), calls=%async_computation.1 | async-start | bytes 393216 | tf_op jit(solution)/shard_map/all_to_all | solution.py:70
  30.1 0.8 copy.55
  30.8 13.8 %all-to-all-done.1 = bf16[128,2,384]{2,1,0:T(2,128)(2,1)S(1)} async-done(((bf16[128,2,384]{2,1,0:T(2,128)(2,1)}), bf16[128,2,384]{2,1,0:T(2,128)(2,1)S(1)}, u32[]{:S(2)}, u32[]{:S(2)}) %all-to-all-start.1) | async-done | bytes 196640 | tf_op jit(solution)/shard_map/all_to_all | solution.py:70
  44.6 0.8 broadcast_in_dim.52
  45.5 10.9 %all-to-all-start = ((bf16[16,128,128]{2,0,1:T(8,128)(2,1)}), bf16[16,128,128]{2,0,1:T(8,128)(2,1)}, u32[]{:S(2)}, u32[]{:S(2)}) async-start(bf16[16,128,128]{2,0,1:T(8,128)(2,1)} %bitcast.5), calls=%async_computation | async-start | bytes 1048576 | tf_op jit(solution)/shard_map/all_to_all | solution.py:77
  56.5 28.8 %all-to-all-done = bf16[16,128,128]{2,0,1:T(8,128)(2,1)} async-done(((bf16[16,128,128]{2,0,1:T(8,128)(2,1)}), bf16[16,128,128]{2,0,1:T(8,128)(2,1)}, u32[]{:S(2)}, u32[]{:S(2)}) %all-to-all-start) | async-done | bytes 524320 | tf_op jit(solution)/shard_map/all_to_all | solution.py:77
  85.3 0.9 broadcast_in_dim.54
  86.2 9.9 %all-to-all-start.2 = ((bf16[16,128,128]{2,0,1:T(8,128)(2,1)}), bf16[16,128,128]{2,0,1:T(8,128)(2,1)}, u32[]{:S(2)}, u32[]{:S(2)}) async-start(bf16[16,128,128]{2,0,1:T(8,128)(2,1)} %bitcast.12), calls=%async_computation.2 | async-start | bytes 1048576 | tf_op jit(solution)/shard_map/all_to_all | solution.py:78
  98.1 79.9 %all-reduce.3.cloned.1.call-done = (bf16[16,8,128]{2,1,0:T(8,128)(2,1)}, bf16[16,8,128]{2,1,0:T(8,128)(2,1)}) async-done(((bf16[16,8,128]{2,1,0:T(8,128)(2,1)}, bf16[16,8,128]{2,1,0:T(8,128)(2,1)}), (bf16[16,8,128]{2,1,0:T(8,128)(2,1)}, bf16[16,8,128]{2,1,0:T(8,128)(2,1)})) %all-reduce.3.cloned.1.call-update) | async-done | bytes 65552 | tf_op jit(solution)/shard_map/psum | solution.py:15
  178.8 0.9 broadcast_in_dim.56
  179.7 9.3 %all-to-all-start.3 = ((bf16[16,128,128]{2,0,1:T(8,128)(2,1)}), bf16[16,128,128]{2,0,1:T(8,128)(2,1)S(1)}, u32[]{:S(2)}, u32[]{:S(2)}) async-start(bf16[16,128,128]{2,0,1:T(8,128)(2,1)} %bitcast.18), calls=%async_computation.3 | async-start | bytes 1048576 | tf_op jit(solution)/shard_map/all_to_all | solution.py:79
  189.0 1.3 dynamic_slice.16
  192.3 26.5 %all-to-all-done.3 = bf16[16,128,128]{2,0,1:T(8,128)(2,1)S(1)} async-done(((bf16[16,128,128]{2,0,1:T(8,128)(2,1)}), bf16[16,128,128]{2,0,1:T(8,128)(2,1)S(1)}, u32[]{:S(2)}, u32[]{:S(2)}) %all-to-all-start.3) | async-done | bytes 524320 | tf_op jit(solution)/shard_map/all_to_all | solution.py:79
  218.8 1.0 broadcast_in_dim.58
  219.8 9.6 %all-to-all-start.4 = ((bf16[16,128,128]{2,0,1:T(8,128)(2,1)}), bf16[16,128,128]{2,0,1:T(8,128)(2,1)}, u32[]{:S(2)}, u32[]{:S(2)}) async-start(bf16[16,128,128]{2,0,1:T(8,128)(2,1)} %bitcast.22), calls=%async_computation.4 | async-start | bytes 1048576 | tf_op jit(solution)/shard_map/all_to_all | solution.py:82
  229.4 10.0 %while.30 = (s32[]{:T(128)}, f32[6,128]{1,0:T(8,128)S(1)}, f32[6,128]{1,0:T(8,128)S(1)}, f32[6,128,128]{2,1,0:T(8,128)}, bf16[2,1024,128]{2,1,0:T(8,128)(2,1)}, ...) while((s32[]{:T(128)}, f32[6,128]{1,0:T(8,128)S(1)}, ...), condition=%wide.region_3.4_spmd.clone, body=%wide.region_0.3_spmd.clone.sunk | while | flops 409243392 | bytes 14139569 | solution.py:46
  229.4 1.5 bitcast_reduce_fusion.5
  232.0 1.7 fusion.60
  234.5 1.5 bitcast_reduce_fusion.5
  237.0 1.7 fusion.60
  239.5 18.6 %all-to-all-done.4 = bf16[16,128,128]{2,0,1:T(8,128)(2,1)} async-done(((bf16[16,128,128]{2,0,1:T(8,128)(2,1)}), bf16[16,128,128]{2,0,1:T(8,128)(2,1)}, u32[]{:S(2)}, u32[]{:S(2)}) %all-to-all-start.4) | async-done | bytes 524320 | tf_op jit(solution)/shard_map/all_to_all | solution.py:82
  258.1 9.9 %while.29 = (s32[]{:T(128)}, f32[6,128]{1,0:T(8,128)S(1)}, f32[6,128]{1,0:T(8,128)S(1)}, f32[6,128,128]{2,1,0:T(8,128)}, pred[]{:T(512)}, /*index=5*/bf16[2,1024...) while((s32[]{:T(128)}, f32[6,128]{1,0:T(8,128)S(1)}, ...), condition=%wide.region_9.10_spmd, body=%wide.region_6.9_spmd.sunk | while | flops 411502080 | bytes 14140582 | solution.py:46
  258.1 1.6 bitcast_reduce_fusion.4
  260.3 1.9 fusion.54
  263.0 1.6 bitcast_reduce_fusion.4
  265.3 1.9 fusion.54
  267.9 1.2 copy.49
  269.1 0.8 reduce.1
  270.2 23.7 %all_to_all.78 = bf16[128,2,384]{2,1,0:T(2,128)(2,1)S(1)} all-to-all(bf16[128,2,384]{2,1,0:T(2,128)(2,1)S(1)} %reshape.73), channel_id=1, replica_groups=mesh['section'=4,'ctx'=128] {'ctx'}, dimensions={0} | all-to-all | bytes 393216 | tf_op jit(solution)/shard_map/all_to_all | solution.py:102
  294.1 0.8 reshape.66
  (66 shorter events, 11.7 us)
Async XLA Ops:
  6.5 49.9 %copy-start.5 = (bf16[1,16,1024]{2,1,0:T(8,128)(2,1)S(1)}, bf16[1,16,1024]{2,1,0:T(8,128)(2,1)}, u32[]{:S(2)}) copy-start(bf16[1,16,1024]{2,1,0:T(8,128)(2,1)} %param.13) | copy-start | bytes 98308
  6.5 90.3 %copy-start.6 = (bf16[1,16,1024]{2,1,0:T(8,128)(2,1)S(1)}, bf16[1,16,1024]{2,1,0:T(8,128)(2,1)}, u32[]{:S(2)}) copy-start(bf16[1,16,1024]{2,1,0:T(8,128)(2,1)} %param.15) | copy-start | bytes 98308
  6.5 90.3 %copy-start.7 = (bf16[1,16,1024]{2,1,0:T(8,128)(2,1)S(1)}, bf16[1,16,1024]{2,1,0:T(8,128)(2,1)}, u32[]{:S(2)}) copy-start(bf16[1,16,1024]{2,1,0:T(8,128)(2,1)} %param.14) | copy-start | bytes 98308
  9.7 35.0 %all-to-all-start.1 = ((bf16[128,2,384]{2,1,0:T(2,128)(2,1)}), bf16[128,2,384]{2,1,0:T(2,128)(2,1)S(1)}, u32[]{:S(2)}, u32[]{:S(2)}) async-start(bf16[128,2,384]{2,1,0:T(2,128)(2,1)} %reshape.71), calls=%async_computation.1 | async-start | bytes 393216 | tf_op jit(solution)/shard_map/all_to_all | solution.py:70
  45.5 39.8 %all-to-all-start = ((bf16[16,128,128]{2,0,1:T(8,128)(2,1)}), bf16[16,128,128]{2,0,1:T(8,128)(2,1)}, u32[]{:S(2)}, u32[]{:S(2)}) async-start(bf16[16,128,128]{2,0,1:T(8,128)(2,1)} %bitcast.5), calls=%async_computation | async-start | bytes 1048576 | tf_op jit(solution)/shard_map/all_to_all | solution.py:77
  86.2 92.6 %all-to-all-start.2 = ((bf16[16,128,128]{2,0,1:T(8,128)(2,1)}), bf16[16,128,128]{2,0,1:T(8,128)(2,1)}, u32[]{:S(2)}, u32[]{:S(2)}) async-start(bf16[16,128,128]{2,0,1:T(8,128)(2,1)} %bitcast.12), calls=%async_computation.2 | async-start | bytes 1048576 | tf_op jit(solution)/shard_map/all_to_all | solution.py:78
  96.1 81.9 %all-reduce.3.cloned.1.call-start = ((), (), s32[]{:S(2)}) async-start(), calls=%async_computation.6 | async-start | bytes 131072 | tf_op jit(solution)/shard_map/psum | solution.py:15
  179.7 39.2 %all-to-all-start.3 = ((bf16[16,128,128]{2,0,1:T(8,128)(2,1)}), bf16[16,128,128]{2,0,1:T(8,128)(2,1)S(1)}, u32[]{:S(2)}, u32[]{:S(2)}) async-start(bf16[16,128,128]{2,0,1:T(8,128)(2,1)} %bitcast.18), calls=%async_computation.3 | async-start | bytes 1048576 | tf_op jit(solution)/shard_map/all_to_all | solution.py:79
  218.8 10.6 %copy-start.4 = (bf16[16,128,128]{2,0,1:T(8,128)(2,1)}, bf16[16,128,128]{2,0,1:T(8,128)(2,1)S(1)}, u32[]{:S(2)}) copy-start(bf16[16,128,128]{2,0,1:T(8,128)(2,1)S(1)} %all-to-all-done.3) | copy-start | bytes 1572868
  219.8 38.3 %all-to-all-start.4 = ((bf16[16,128,128]{2,0,1:T(8,128)(2,1)}), bf16[16,128,128]{2,0,1:T(8,128)(2,1)}, u32[]{:S(2)}, u32[]{:S(2)}) async-start(bf16[16,128,128]{2,0,1:T(8,128)(2,1)} %bitcast.22), calls=%async_computation.4 | async-start | bytes 1048576 | tf_op jit(solution)/shard_map/all_to_all | solution.py:82
  231.0 1.0 copy-start
  233.7 0.8 copy-start.1
  236.0 1.0 copy-start
  238.7 0.8 copy-start.1
  258.1 2.3 copy-start.2
  262.2 0.8 copy-start.3
  263.0 2.3 copy-start.2
  267.2 0.8 copy-start.3
Sparse Core Ops, SparseCore 0:
  99.9 78.0 all-reduce.2
where the time goes:
time: 305 us; the launch traced here: 302 us
  waiting for transfers between devices  168 us (55%)
  starting transfers between devices  60.2 us (20%)
  blocking collectives  23.7 us (8%)
  local copies, waits for them, and re-layouts  17.7 us (6%)
  between operations  14.9 us (5%)
  matrix products  13.4 us (4%)
  other arithmetic  3.99 us (1%)
    psum x1, waiting for transfers between devices, from_root(): return lax.psum(jnp.where(mine, array, jnp.zeros_like(array)), axis)  79.9 us
    all_to_all x1, waiting for transfers between devices, shards(): lax.all_to_all(spread_heads(key, copies), 'ctx', split_axis=1, concat_axi...  28.8 us
    all_to_all x1, waiting for transfers between devices, shards(): lax.all_to_all(spread_heads(handed_keys, copies), 'ctx', split_axis=1, co...  26.5 us
    all_to_all x1, blocking collectives, shards(): lax.all_to_all(result, 'ctx', split_axis=0, concat_axis=1, tiled=True)  23.7 us
    all_to_all x1, starting transfers between devices, shards(): lax.all_to_all(arranged_query, 'ctx', split_axis=0, concat_axis=1, tiled=...  20.4 us
    all_to_all x1, waiting for transfers between devices, shards(): lax.all_to_all(spread_heads(handed_values, copies), 'ctx', split_axis=1,...  18.6 us
    all_to_all x1, waiting for transfers between devices, shards(): lax.all_to_all(arranged_query, 'ctx', split_axis=0, concat_axis=1, tiled=...  13.8 us
    all_to_all x1, starting transfers between devices, shards(): lax.all_to_all(spread_heads(key, copies), 'ctx', split_axis=1, concat_axi...  10.9 us
  transfers between devices with their start and end apart: 6, of which 5 were waited for; matrix products, arithmetic and copies ran while one was open for 4% of the time, Pallas kernels for 0%

commit v1 on v0

v1 whole, which is shorter than its diff:
```python
import functools
import math

import jax
import jax.numpy as jnp
from jax import lax
from jax.experimental import pallas as pl
from jax.experimental.pallas import tpu as pltpu
from jax.sharding import Mesh
from jax.sharding import PartitionSpec as P

HEAD_DIM = 128
HEADS = 48
KV_HEADS = 8
GROUP = HEADS // KV_HEADS
WIDE = GROUP * HEAD_DIM
BASE = HEAD_DIM**-0.5 * math.log2(math.e)
VMEM = pl.BlockSpec(memory_space=pltpu.VMEM)
SMEM = pl.BlockSpec(memory_space=pltpu.SMEM)


def head_rows(q_ref, first, count):
    rows = q_ref.shape[0] * q_ref.shape[1]
    return jnp.concatenate(
        [
            q_ref[:, :, g * HEAD_DIM : (g + 1) * HEAD_DIM].reshape(rows, HEAD_DIM)
            for g in range(first, first + count)
        ],
        0,
    )


def attend(q, k, v_ones):
    scores = lax.dot_general(q, k, (((1,), (1,)), ((), ())), preferred_element_type=jnp.float32)
    largest = jnp.max(scores, axis=-1, keepdims=True)
    weights = jnp.exp2((scores - largest) * BASE).astype(jnp.bfloat16)
    return largest, jnp.dot(weights, v_ones, preferred_element_type=jnp.float32)


def with_ones(v):
    return jnp.concatenate([v, jnp.ones_like(v)], 1)


def own_kernel(count, q_ref, kv_ref, sums_ref, largest_ref):
    n = kv_ref.shape[0] * kv_ref.shape[1]
    rows = q_ref.shape[0] * q_ref.shape[1]
    k = kv_ref[:, :, :HEAD_DIM].reshape(n, HEAD_DIM)
    v_ones = with_ones(kv_ref[:, :, HEAD_DIM : 2 * HEAD_DIM].reshape(n, HEAD_DIM))
    for first in range(0, GROUP, count):
        at = slice(first * rows, (first + count) * rows)
        largest, sums = attend(head_rows(q_ref, first, count), k, v_ones)
        sums_ref[at, :] = sums
        largest_ref[at, :] = jnp.broadcast_to(largest, (count * rows, HEAD_DIM))


def far_kernel(count, flags_ref, q_ref, kv_ref, other_ref, sums_ref, largest_ref, out_ref):
    n = kv_ref.shape[0] * kv_ref.shape[1]
    blocks, rows_each = q_ref.shape[0], q_ref.shape[1]
    rows = blocks * rows_each

    def store(first, total):
        out = total[:, :HEAD_DIM] / total[:, HEAD_DIM:]
        for i in range(count):
            g = first + i
            out_ref[:, :, g * HEAD_DIM : (g + 1) * HEAD_DIM] = (
                out[i * rows : (i + 1) * rows].astype(out_ref.dtype).reshape(blocks, rows_each, HEAD_DIM)
            )

    @pl.when(flags_ref[0] == 1)
    def _():
        mine = kv_ref[:, :, 2 * HEAD_DIM :].reshape(n, HEAD_DIM)
        other = other_ref[...].reshape(n, HEAD_DIM)
        keys_here = flags_ref[1] == 0
        k = jnp.where(keys_here, mine, other)
        v_ones = with_ones(jnp.where(keys_here, other, mine))
        for first in range(0, GROUP, count):
            at = slice(first * rows, (first + count) * rows)
            largest, sums = attend(head_rows(q_ref, first, count), k, v_ones)
            before = largest_ref[at, :]
            after = jnp.maximum(before, largest)
            old = jnp.exp2((before - after) * BASE)
            new = jnp.exp2((largest - after) * BASE)
            old, new = jnp.concatenate([old, old], 1), jnp.concatenate([new, new], 1)
            store(first, sums_ref[at, :] * old + sums * new)

    @pl.when(flags_ref[0] == 0)
    def _():
        for first in range(0, GROUP, count):
            store(first, sums_ref[first * rows : (first + count) * rows, :])


def estimate(q_rows, n):
    return pl.CostEstimate(flops=4 * q_rows * n * HEAD_DIM, bytes_accessed=4 * 2**20, transcendentals=q_rows * n)


def own_attention(q, kv):
    rows, n = q.shape[0] * q.shape[1] * GROUP, kv.shape[0] * kv.shape[1]
    return pl.pallas_call(
        functools.partial(own_kernel, 3),
        out_shape=(
            jax.ShapeDtypeStruct((rows, 2 * HEAD_DIM), jnp.float32),
            jax.ShapeDtypeStruct((rows, HEAD_DIM), jnp.float32),
        ),
        in_specs=[VMEM] * 2,
        out_specs=(VMEM,) * 2,
        cost_estimate=estimate(rows, n),
        compiler_params=pltpu.CompilerParams(vmem_limit_bytes=40 * 2**20),
    )(q, kv)


def far_attention(flags, q, kv, other, sums, largest):
    rows, n = q.shape[0] * q.shape[1] * GROUP, kv.shape[0] * kv.shape[1]
    return pl.pallas_call(
        functools.partial(far_kernel, 3),
        out_shape=jax.ShapeDtypeStruct((q.shape[0], q.shape[1], WIDE), jnp.bfloat16),
        in_specs=[SMEM] + [VMEM] * 5,
        out_specs=VMEM,
        cost_estimate=estimate(rows, n),
        compiler_params=pltpu.CompilerParams(vmem_limit_bytes=40 * 2**20),
    )(flags, q, kv, other, sums, largest)


def shards(query, key, value, clean_key, clean_value, completing, span_mask):
    tok = query.shape[1]
    section = lax.axis_index("section")
    core, half = section % 2, section // 2
    finished = completing[0]
    seen = jnp.logical_and(section > finished, span_mask[section, finished] == 1)

    mine = jnp.where(core == 0, clean_key[0], clean_value[0])
    sent = jnp.where(core == 0, clean_value[0], clean_key[0])
    swapped = lax.ppermute(sent, "section", [(0, 1), (1, 0), (2, 3), (3, 2)])
    picked = jnp.where(finished % 2 == core, mine, swapped)
    handed = lax.ppermute(picked, "section", [(0, 2), (1, 3)])
    picked = jnp.where(jnp.logical_and(half == 1, finished < 2), handed, picked)

    def split(a):
        return a.reshape(tok, KV_HEADS, -1)

    packed = jnp.concatenate([split(query), split(key), split(value), split(picked)], -1)
    packed = jnp.transpose(packed, (1, 0, 2))
    served = lax.all_to_all(packed, "z", 0, 0, tiled=True)
    kv = served[:, :, WIDE:].reshape(1, KV_HEADS * tok, 3 * HEAD_DIM)
    plane = lax.axis_size("x") * lax.axis_size("y")
    kv = lax.all_to_all(jnp.broadcast_to(kv, (plane,) + kv.shape[1:]), ("x", "y"), 0, 0, tiled=True)
    other = lax.ppermute(kv[:, :, 2 * HEAD_DIM :], "section", [(0, 1), (1, 0), (2, 3), (3, 2)])
    sums, largest = own_attention(served, kv)
    flags = jnp.stack([seen.astype(jnp.int32), core.astype(jnp.int32)])
    out = far_attention(flags, served, kv, other, sums, largest)
    out = lax.all_to_all(out, "z", 0, 0, tiled=True)
    return jnp.transpose(out, (1, 0, 2)).reshape(1, tok, HEADS * HEAD_DIM)


def solution(mesh):
    grid = Mesh(mesh.devices.reshape(4, 8, 4, 4), ("section", "z", "x", "y"))
    rows = P("section", ("z", "x", "y"), None)
    return jax.shard_map(
        shards, mesh=grid, in_specs=(rows,) * 5 + (P(), P()), out_specs=rows, check_vma=False
    )
```

time: 305 us -> 104 us (0.34)
  the two profiles are of different devices: /device:TPU:1 before, /device:TPU:32 now
where the time goes in v1:
time: 104 us; the launch traced here: 103 us
  blocking collectives  72.5 us (70%)
  starting transfers between devices  18.6 us (18%)
  local copies, waits for them, and re-layouts  4.98 us (5%)
  Pallas kernels  3.39 us (3%)
  other arithmetic  1.66 us (2%)
  between operations  1.43 us (1%)
    all_to_all x1, blocking collectives, shards(): lax.all_to_all(jnp.broadcast_to(kv, (plane,) + kv.shape[1:]), ('x', 'y'),...  28 us
    all_to_all x1, blocking collectives, shards(): served = lax.all_to_all(packed, 'z', 0, 0, tiled=True)  23.5 us
    all_to_all x1, blocking collectives, shards(): out = lax.all_to_all(out, 'z', 0, 0, tiled=True)  21 us
    ppermute x1, starting transfers between devices, shards(): handed = lax.ppermute(picked, 'section', [(0, 2), (1, 3)])  14.8 us
    pallas_call x1, Pallas kernels, own_attention(): pl.pallas_call(functools.partial(own_kernel, 3), out_shape=(jax.ShapeDtyp...  2.78 us
    unnamed x3, local copies, waits for them, and re-layouts  2.5 us
  transfers between devices with their start and end apart: 3, of which 1 were waited for; matrix products, arithmetic and copies ran while one was open for 4% of the time, Pallas kernels for 3%

profile of v1, /device:TPU:32, one launch (start us, length us, event | category | flops | bytes accessed | tf_op | source)
XLA Modules:
  0.0 103.1 jit_solution(11476942190384474760)
XLA Ops:
  0.0 0.8 select_bitcast_fusion.1
  0.8 1.9 %collective-permute-start = (bf16[16,1024]{1,0:T(8,128)(2,1)S(1)}, bf16[16,1024]{1,0:T(8,128)(2,1)S(1)}, u32[]{:S(2)}, u32[]{:S(2)}) collective-permute-start(bf16[16,1024]{1,0:T(8,128)(2,1)S(1)} %select_bitcast_fusion.1), channel_id=1, source_target_pairs={{0,128},{128,0},{256,384},{384,256},{1,129},{129,1},{257,385},{385... | collective-permute-start | bytes 98312 | tf_op jit(solution)/shard_map/ppermute | solution.py:132
  3.4 0.5 collective-permute-done
  3.9 0.8 bitcast_select_fusion
  4.6 14.8 %collective-permute-start.1 = (bf16[16,1024]{1,0:T(8,128)(2,1)S(1)}, bf16[16,1024]{1,0:T(8,128)(2,1)S(1)}, u32[]{:S(2)}, u32[]{:S(2)}) collective-permute-start(bf16[16,1024]{1,0:T(8,128)(2,1)S(1)} %bitcast_select_fusion), channel_id=1, source_target_pairs={{0,256},{128,384},{1,257},{129,385},{2,258},{130,386},{3,259},{131... | collective-permute-start | bytes 98312 | tf_op jit(solution)/shard_map/ppermute | solution.py:134
  19.5 0.8 copy.15
  20.2 0.8 copy.16
  21.0 1.0 copy.14
  22.0 0.0 collective-permute-done.1
  22.1 23.5 %all_to_all.15.q_ref = bf16[8,16,1152]{2,1,0:T(8,128)(2,1)S(1)} all-to-all(bf16[8,16,1152]{2,1,0:T(8,128)(2,1)S(1)} %maximum_bitcast_fusion), channel_id=1, replica_groups=mesh['section'=4,'z'=8,'x'=4,'y'=4] {'z'}, dimensions={0} | all-to-all | bytes 589824 | tf_op jit(solution)/shard_map/all_to_all | solution.py:142
  45.6 0.2 broadcast_in_dim.8
  45.8 28.0 %all_to_all.16.kv_ref = bf16[16,128,384]{2,1,0:T(8,128)(2,1)S(1)} all-to-all(bf16[16,128,384]{2,1,0:T(8,128)(2,1)S(1)} %broadcast_in_dim.8), channel_id=1, replica_groups=mesh['section'=4,'z'=8,'x'=4,'y'=4] {'x','y'}, dimensions={0} | all-to-all | bytes 3145728 | tf_op jit(solution)/shard_map/all_to_all | solution.py:145
  73.8 0.1 slice.9
  73.9 1.9 %collective-permute-start.2 = (bf16[16,128,128]{2,1,0:T(8,128)(2,1)S(1)}, bf16[16,128,128]{2,1,0:T(8,128)(2,1)S(1)}, u32[]{:S(2)}, u32[]{:S(2)}) collective-permute-start(bf16[16,128,128]{2,1,0:T(8,128)(2,1)S(1)} %slice.9), channel_id=1, source_target_pairs={{0,128},{128,0},{256,384},{384,256},{1,129},{129,1},{257,385},{385... | collective-permute-start | bytes 1572872 | tf_op jit(solution)/shard_map/ppermute | solution.py:146
  75.9 1.3 %dynamic_slice.3 = s32[1,1]{1,0:T(1,128)} dynamic-slice(s32[4,4]{1,0:T(4,128)} %param.13, s32[]{:T(128)S(6)} %select_n.51, s32[]{:T(128)S(6)} %select_n.52), dynamic_slice_sizes={1,1} | dynamic-slice | bytes 12 | tf_op jit(solution)/shard_map/dynamic_slice | solution.py:128
  77.8 0.1 pad_add_fusion.flags_ref
  77.8 2.8 %shard_map.73 = (f32[768,256]{1,0:T(8,128)S(1)}, f32[768,128]{1,0:T(8,128)S(1)}) custom-call(bf16[8,16,1152]{2,1,0:T(8,128)(2,1)S(1)} %all_to_all.15.q_ref, bf16[16,128,384]{2,1,0:T(8,128)(2,1)S(1)} %all_to_all.16.kv_ref), custom_call_target="tpu_custom_call" | custom-call | flops 805306368 | bytes 4194304 | tf_op jit(solution)/shard_map/pallas_call | solution.py:98
  80.6 0.0 collective-permute-done.2.other_ref
  80.6 0.6 shard_map.74
  81.3 21.0 %all_to_all.17 = bf16[8,16,768]{2,1,0:T(8,128)(2,1)S(1)} all-to-all(bf16[8,16,768]{2,1,0:T(8,128)(2,1)S(1)} %shard_map.74), channel_id=1, replica_groups=mesh['section'=4,'z'=8,'x'=4,'y'=4] {'z'}, dimensions={0} | all-to-all | bytes 393216 | tf_op jit(solution)/shard_map/all_to_all | solution.py:150
  102.3 0.1 copy.12
  102.4 0.8 reshape.27
  (6 shorter events, 0.1 us)
Async XLA Ops:
  0.8 3.1 %collective-permute-start = (bf16[16,1024]{1,0:T(8,128)(2,1)S(1)}, bf16[16,1024]{1,0:T(8,128)(2,1)S(1)}, u32[]{:S(2)}, u32[]{:S(2)}) collective-permute-start(bf16[16,1024]{1,0:T(8,128)(2,1)S(1)} %select_bitcast_fusion.1), channel_id=1, source_target_pairs={{0,128},{128,0},{256,384},{384,256},{1,129},{129,1},{257,385},{385... | collective-permute-start | bytes 98312 | tf_op jit(solution)/shard_map/ppermute | solution.py:132
  4.6 17.4 %collective-permute-start.1 = (bf16[16,1024]{1,0:T(8,128)(2,1)S(1)}, bf16[16,1024]{1,0:T(8,128)(2,1)S(1)}, u32[]{:S(2)}, u32[]{:S(2)}) collective-permute-start(bf16[16,1024]{1,0:T(8,128)(2,1)S(1)} %bitcast_select_fusion), channel_id=1, source_target_pairs={{0,256},{128,384},{1,257},{129,385},{2,258},{130,386},{3,259},{131... | collective-permute-start | bytes 98312 | tf_op jit(solution)/shard_map/ppermute | solution.py:134
  73.9 6.7 %collective-permute-start.2 = (bf16[16,128,128]{2,1,0:T(8,128)(2,1)S(1)}, bf16[16,128,128]{2,1,0:T(8,128)(2,1)S(1)}, u32[]{:S(2)}, u32[]{:S(2)}) collective-permute-start(bf16[16,128,128]{2,1,0:T(8,128)(2,1)S(1)} %slice.9), channel_id=1, source_target_pairs={{0,128},{128,0},{256,384},{384,256},{1,129},{129,1},{257,385},{385... | collective-permute-start | bytes 1572872 | tf_op jit(solution)/shard_map/ppermute | solution.py:146

commit v2 on v1

v2 whole, which is shorter than its diff:
```python
import functools
import math

import jax
import jax.numpy as jnp
from jax import lax
from jax.experimental import pallas as pl
from jax.experimental.pallas import tpu as pltpu
from jax.sharding import Mesh
from jax.sharding import PartitionSpec as P

HEAD_DIM = 128
HEADS = 48
KV_HEADS = 8
GROUP = HEADS // KV_HEADS
WIDE = GROUP * HEAD_DIM
BASE = HEAD_DIM**-0.5 * math.log2(math.e)
VMEM = pl.BlockSpec(memory_space=pltpu.VMEM)
SMEM = pl.BlockSpec(memory_space=pltpu.SMEM)


def head_rows(q_ref, first, count):
    rows = q_ref.shape[0] * q_ref.shape[1]
    return jnp.concatenate(
        [
            q_ref[:, :, g * HEAD_DIM : (g + 1) * HEAD_DIM].reshape(rows, HEAD_DIM)
            for g in range(first, first + count)
        ],
        0,
    )


def attend(q, k, v_ones):
    scores = lax.dot_general(q, k, (((1,), (1,)), ((), ())), preferred_element_type=jnp.float32)
    largest = jnp.max(scores, axis=-1, keepdims=True)
    weights = jnp.exp2((scores - largest) * BASE).astype(jnp.bfloat16)
    return largest, jnp.dot(weights, v_ones, preferred_element_type=jnp.float32)


def with_ones(v):
    return jnp.concatenate([v, jnp.ones_like(v)], 1)


def own_kernel(count, q_ref, kv_ref, sums_ref, largest_ref):
    n = kv_ref.shape[0] * kv_ref.shape[1]
    rows = q_ref.shape[0] * q_ref.shape[1]
    k = kv_ref[:, :, :HEAD_DIM].reshape(n, HEAD_DIM)
    v_ones = with_ones(kv_ref[:, :, HEAD_DIM : 2 * HEAD_DIM].reshape(n, HEAD_DIM))
    for first in range(0, GROUP, count):
        at = slice(first * rows, (first + count) * rows)
        largest, sums = attend(head_rows(q_ref, first, count), k, v_ones)
        sums_ref[at, :] = sums
        largest_ref[at, :] = jnp.broadcast_to(largest, (count * rows, HEAD_DIM))


def far_kernel(count, completing_ref, mask_ref, q_ref, kv_ref, other_ref, sums_ref, largest_ref, out_ref):
    n = kv_ref.shape[0] * kv_ref.shape[1]
    blocks, rows_each = q_ref.shape[0], q_ref.shape[1]
    rows = blocks * rows_each
    core = lax.axis_index("core")
    section = lax.axis_index("half") * 2 + core
    finished = completing_ref[0]
    seen = jnp.logical_and(section > finished, mask_ref[section, finished] == 1)

    def store(first, total):
        out = total[:, :HEAD_DIM] / total[:, HEAD_DIM:]
        for i in range(count):
            g = first + i
            out_ref[:, :, g * HEAD_DIM : (g + 1) * HEAD_DIM] = (
                out[i * rows : (i + 1) * rows].astype(out_ref.dtype).reshape(blocks, rows_each, HEAD_DIM)
            )

    @pl.when(seen)
    def _():
        mine = kv_ref[:, :, 2 * HEAD_DIM :].reshape(n, HEAD_DIM)
        other = other_ref[...].reshape(n, HEAD_DIM)
        keys_here = core == 0
        k = jnp.where(keys_here, mine, other)
        v_ones = with_ones(jnp.where(keys_here, other, mine))
        for first in range(0, GROUP, count):
            at = slice(first * rows, (first + count) * rows)
            largest, sums = attend(head_rows(q_ref, first, count), k, v_ones)
            before = largest_ref[at, :]
            after = jnp.maximum(before, largest)
            old = jnp.exp2((before - after) * BASE)
            new = jnp.exp2((largest - after) * BASE)
            old, new = jnp.concatenate([old, old], 1), jnp.concatenate([new, new], 1)
            store(first, sums_ref[at, :] * old + sums * new)

    @pl.when(jnp.logical_not(seen))
    def _():
        for first in range(0, GROUP, count):
            store(first, sums_ref[first * rows : (first + count) * rows, :])


def stage_kernel(
    query_ref, key_ref, value_ref, clean_key_ref, clean_value_ref, out_ref, near_ref, mine_ref, sent_ref, sems
):
    core = lax.axis_index("core")
    copies = [
        pltpu.make_async_copy(query_ref.at[0, :, pl.ds(h * WIDE, WIDE)], out_ref.at[h], sems.at[h])
        for h in range(KV_HEADS)
    ]
    copies.append(pltpu.make_async_copy(key_ref.at[0], near_ref.at[0], sems.at[KV_HEADS]))
    copies.append(pltpu.make_async_copy(value_ref.at[0], near_ref.at[1], sems.at[KV_HEADS + 1]))
    for here, kept, given in ((0, clean_key_ref, clean_value_ref), (1, clean_value_ref, clean_key_ref)):

        @pl.when(core == here)
        def _():
            pltpu.make_async_copy(given.at[0], sent_ref, sems.at[KV_HEADS + 2]).start()
            pltpu.make_async_copy(kept.at[0], mine_ref, sems.at[KV_HEADS + 3]).start()

    for copy in copies:
        copy.start()
    for copy in copies:
        copy.wait()
    pltpu.make_async_copy(clean_key_ref.at[0], sent_ref, sems.at[KV_HEADS + 2]).wait()
    pltpu.make_async_copy(clean_key_ref.at[0], mine_ref, sems.at[KV_HEADS + 3]).wait()


def pack_keys_kernel(completing_ref, near_ref, picked_ref, handed_ref, after_ref, out_ref):
    del after_ref
    handed = jnp.logical_and(lax.axis_index("half") == 1, completing_ref[0] < 2)
    clean = jnp.where(handed, handed_ref[...], picked_ref[...])
    for h in range(KV_HEADS):
        at = slice(h * HEAD_DIM, (h + 1) * HEAD_DIM)
        first = (h % 2) * 3 * HEAD_DIM
        for z in (h // 2, h // 2 + KV_HEADS // 2):
            for i, part in enumerate((near_ref[0, :, at], near_ref[1, :, at], clean[:, at])):
                out_ref[z, :, first + i * HEAD_DIM : first + (i + 1) * HEAD_DIM] = part


def spread_kernel(served_ref, out_ref):
    rows = served_ref.shape[0] * served_ref.shape[1]
    each = 3 * HEAD_DIM
    for i in range(out_ref.shape[0]):
        head = (i // 4) % 2
        out_ref[i] = served_ref[:, :, head * each : (head + 1) * each].reshape(rows, each)


def estimate(q_rows, n):
    return pl.CostEstimate(flops=4 * q_rows * n * HEAD_DIM, bytes_accessed=4 * 2**20, transcendentals=q_rows * n)


def call(kernel, out_shape, specs, *operands, cost=None):
    outs = (VMEM,) * len(out_shape) if isinstance(out_shape, tuple) else VMEM
    return pl.pallas_call(
        kernel,
        out_shape=out_shape,
        in_specs=specs,
        out_specs=outs,
        cost_estimate=cost,
        compiler_params=pltpu.CompilerParams(vmem_limit_bytes=40 * 2**20),
    )(*operands)


def shaped(*shape, dtype=jnp.bfloat16):
    return jax.ShapeDtypeStruct(shape, dtype)


def shards(query, key, value, clean_key, clean_value, completing, span_mask):
    tok = query.shape[1]
    heads = KV_HEADS
    z_all, served_by, plane_axes = ("zq", "zc"), ("zc", "xb"), ("xa", "xb", "y")
    depth, plane = 8, 16
    anywhere = pl.BlockSpec(memory_space=pl.ANY)

    width = heads * HEAD_DIM
    packed, near, mine, sent = pl.pallas_call(
        stage_kernel,
        out_shape=(shaped(heads, tok, WIDE), shaped(2, tok, width), shaped(tok, width), shaped(tok, width)),
        in_specs=[anywhere] * 5,
        out_specs=(VMEM,) * 4,
        scratch_shapes=[pltpu.SemaphoreType.DMA((heads + 4,))],
    )(query, key, value, clean_key, clean_value)
    served = lax.all_to_all(packed, served_by, 0, 0, tiled=True)

    swapped = lax.ppermute(sent, "core", [(0, 1), (1, 0)])
    picked = jnp.where(completing[0] % 2 == lax.axis_index("core"), mine, swapped)
    handed = lax.ppermute(
        picked, ("half",) + z_all, [(z, depth + (z + depth // 2) % depth) for z in range(depth)]
    )

    kv = call(
        pack_keys_kernel,
        shaped(depth, tok, 6 * HEAD_DIM),
        [SMEM] + [VMEM] * 3 + [anywhere],
        completing,
        near,
        picked,
        handed,
        served,
    )
    kv = lax.all_to_all(kv, z_all, 0, 0, tiled=True)
    kv = call(spread_kernel, shaped(plane, depth * tok, 3 * HEAD_DIM), [VMEM], kv)
    kv = lax.all_to_all(kv, plane_axes, 0, 0, tiled=True)
    other = lax.ppermute(kv[:, :, 2 * HEAD_DIM :], "core", [(0, 1), (1, 0)])

    rows, n = heads * tok * GROUP, plane * depth * tok
    sums, largest = call(
        functools.partial(own_kernel, 3),
        (shaped(rows, 2 * HEAD_DIM, dtype=jnp.float32), shaped(rows, HEAD_DIM, dtype=jnp.float32)),
        [VMEM] * 2,
        served,
        kv,
        cost=estimate(rows, n),
    )
    out = call(
        functools.partial(far_kernel, 3),
        shaped(heads, tok, WIDE),
        [SMEM] * 2 + [VMEM] * 5,
        completing,
        span_mask,
        served,
        kv,
        other,
        sums,
        largest,
        cost=estimate(rows, n),
    )
    out = lax.all_to_all(out, served_by, 0, 0, tiled=True)
    return jnp.transpose(out, (1, 0, 2)).reshape(1, tok, HEADS * HEAD_DIM)


def solution(mesh):
    grid = Mesh(mesh.devices.reshape(2, 2, 2, 4, 2, 2, 4), ("half", "core", "zq", "zc", "xa", "xb", "y"))
    rows = P(("half", "core"), ("zq", "zc", "xa", "xb", "y"), None)
    return jax.shard_map(
        shards, mesh=grid, in_specs=(rows,) * 5 + (P(), P()), out_specs=rows, check_vma=False
    )
```

time: 104 us -> 93.1 us (0.90)
  the two profiles are of different devices: /device:TPU:32 before, /device:TPU:1 now
where the time goes in v2:
time: 93.1 us; the launch traced here: 92.5 us
  blocking collectives  52.2 us (56%)
  starting transfers between devices  28.1 us (30%)
  Pallas kernels  8.2 us (9%)
  local copies, waits for them, and re-layouts  1.77 us (2%)
  waiting for transfers between devices  1.39 us (1%)
    all_to_all x1, blocking collectives, shards(): kv = lax.all_to_all(kv, plane_axes, 0, 0, tiled=True)  24.1 us
    all_to_all x1, blocking collectives, shards(): kv = lax.all_to_all(kv, z_all, 0, 0, tiled=True)  19.1 us
    all_to_all x1, blocking collectives, shards(): out = lax.all_to_all(out, served_by, 0, 0, tiled=True)  9.04 us
    ppermute x1, starting transfers between devices, shards(): other = lax.ppermute(kv[:, :, 2 * HEAD_DIM:], 'core', [(0, 1), (1, 0)])  8.15 us
    ppermute x1, starting transfers between devices, shards(): lax.ppermute(picked, ('half',) + z_all, [(z, depth + (z + depth // 2) % d...  7.8 us
    all_to_all x1, starting transfers between devices, shards(): served = lax.all_to_all(packed, served_by, 0, 0, tiled=True)  7.39 us
    pallas_call x4, Pallas kernels, call(): pl.pallas_call(kernel, out_shape=out_shape, in_specs=specs, out_specs=out...  6.47 us
    ppermute x1, starting transfers between devices, shards(): swapped = lax.ppermute(sent, 'core', [(0, 1), (1, 0)])  4.81 us
  transfers between devices with their start and end apart: 4, of which 2 were waited for; matrix products, arithmetic and copies ran while one was open for 0% of the time, Pallas kernels for 3%

profile of v2, /device:TPU:1, one launch (start us, length us, event | category | flops | bytes accessed | tf_op | source)
XLA Modules:
  0.0 92.5 jit_solution(5780341844238462476)
XLA Ops:
  0.0 1.7 %shard_map.73 = (bf16[8,16,768]{2,1,0:T(8,128)(2,1)}, bf16[2,16,1024]{2,1,0:T(8,128)(2,1)}, bf16[16,1024]{1,0:T(8,128)(2,1)}, bf16[16,1024]{1,0:T(8,128)(2,1)}) custom-call(bf16[1,16,6144]{2,1,0:T(8,128)(2,1)} %query_ref.1, bf16[1,16,1024]{2,1,0:T(8,128)(2,1)} %key_ref.1, bf16[1,16,1024]{2,1,0:T(8,128)(2,1)} %value_ref.1, ...), custom_call_target="tpu_custom_call" | custom-call | tf_op jit(solution)/shard_map/pallas_call | solution.py:169
  1.7 7.4 %all-to-all-start = ((bf16[8,16,768]{2,1,0:T(8,128)(2,1)}), bf16[8,16,768]{2,1,0:T(8,128)(2,1)S(1)}, u32[]{:S(2)}, u32[]{:S(2)}) async-start(bf16[8,16,768]{2,1,0:T(8,128)(2,1)} %get-tuple-element.11), calls=%async_computation | async-start | bytes 393216 | tf_op jit(solution)/shard_map/all_to_all | solution.py:176
  9.1 4.8 %collective-permute-start = (bf16[16,1024]{1,0:T(8,128)(2,1)}, bf16[16,1024]{1,0:T(8,128)(2,1)S(1)}, u32[]{:S(2)}, u32[]{:S(2)}) collective-permute-start(bf16[16,1024]{1,0:T(8,128)(2,1)} %get-tuple-element.14), channel_id=1, source_target_pairs={{0,128},{128,0},{1,129},{129,1},{2,130},{130,2},{3,131},{131,3},{4... | collective-permute-start | bytes 98312 | tf_op jit(solution)/shard_map/ppermute | solution.py:178
  14.6 0.4 collective-permute-done
  15.0 7.8 %collective-permute-start.1 = (bf16[16,1024]{1,0:T(8,128)(2,1)S(1)}, bf16[16,1024]{1,0:T(8,128)(2,1)S(1)}, u32[]{:S(2)}, u32[]{:S(2)}) collective-permute-start(bf16[16,1024]{1,0:T(8,128)(2,1)S(1)} %broadcast_select_fusion.picked_ref), channel_id=1, source_target_pairs={{0,320},{16,336},{32,352},{48,368},{64,256},{80,272},{96,288},{112... | collective-permute-start | bytes 98312 | tf_op jit(solution)/shard_map/ppermute | solution.py:180
  22.8 1.0 %collective-permute-done.1.handed_ref = bf16[16,1024]{1,0:T(8,128)(2,1)S(1)} collective-permute-done((bf16[16,1024]{1,0:T(8,128)(2,1)S(1)}, bf16[16,1024]{1,0:T(8,128)(2,1)S(1)}, u32[]{:S(2)}, u32[]{:S(2)}) %collective-permute-start.1) | collective-permute-done | bytes 32800 | tf_op jit(solution)/shard_map/ppermute | solution.py:180
  23.8 0.0 all-to-all-done.after_ref.q_ref
  23.8 0.0 copy-start
  23.8 0.8 copy-done
  24.7 19.1 %all_to_all.20.served_ref = bf16[8,16,768]{2,1,0:T(8,128)(2,1)S(1)} all-to-all(bf16[8,16,768]{2,1,0:T(8,128)(2,1)S(1)} %shard_map.74), channel_id=1, replica_groups=mesh['half'=2,'core'=2,'zq'=2,'zc'=4,'xa'=2,'xb'=2,'y'=4] {'zq','zc'}, dimensions={0} | all-to-all | bytes 393216 | tf_op jit(solution)/shard_map/all_to_all | solution.py:194
  43.8 0.1 shard_map.75
  44.0 24.1 %all_to_all.21.kv_ref = bf16[16,128,384]{2,1,0:T(8,128)(2,1)S(1)} all-to-all(bf16[16,128,384]{2,1,0:T(8,128)(2,1)S(1)} %shard_map.75), channel_id=1, replica_groups=mesh['half'=2,'core'=2,'zq'=2,'zc'=4,'xa'=2,'xb'=2,'y'=4] {'xa','xb','y'}, dimensions={0} | all-to-all | bytes 3145728 | tf_op jit(solution)/shard_map/all_to_all | solution.py:196
  68.0 0.1 slice.4
  68.1 0.0 copy-start.1
  68.1 8.1 %collective-permute-start.2 = (bf16[16,128,128]{2,1,0:T(8,128)(2,1)S(1)}, bf16[16,128,128]{2,1,0:T(8,128)(2,1)S(1)}, u32[]{:S(2)}, u32[]{:S(2)}) collective-permute-start(bf16[16,128,128]{2,1,0:T(8,128)(2,1)S(1)} %slice.4), channel_id=1, source_target_pairs={{0,128},{128,0},{1,129},{129,1},{2,130},{130,2},{3,131},{131,3},{4... | collective-permute-start | bytes 1572872 | tf_op jit(solution)/shard_map/ppermute | solution.py:197
  76.3 2.9 %shard_map.76 = (f32[768,256]{1,0:T(8,128)S(1)}, f32[768,128]{1,0:T(8,128)S(1)}) custom-call(bf16[8,16,768]{2,1,0:T(8,128)(2,1)S(1)} %all-to-all-done.after_ref.q_ref, bf16[16,128,384]{2,1,0:T(8,128)(2,1)S(1)} %all_to_all.21.kv_ref), custom_call_target="tpu_custom_call" | custom-call | flops 805306368 | bytes 4194304 | tf_op jit(solution)/shard_map/pallas_call | solution.py:147
  79.2 0.0 collective-permute-done.2.other_ref
  79.2 0.0 copy-done.1
  79.2 3.4 %shard_map.77 = bf16[8,16,768]{2,1,0:T(8,128)(2,1)S(1)} custom-call(s32[1]{0:T(128)} %copy.9.completing_ref, s32[4,4]{1,0:T(4,128)S(1)} %copy-done.1, bf16[8,16,768]{2,1,0:T(8,128)(2,1)S(1)} %all-to-all-done.after_ref.q_ref, bf16[16,128,384]{2,1,0:T(8,128)(2,1)S(1)} %all_to_all.21.kv_ref, bf16[16,128,128]{2,1,0:T(8,128)(2,1)S(1)} %collective-permute-done.2.other_ref, ...), custom_call_target="tpu_custom_call" | custom-call | flops 805306368 | bytes 4194304 | tf_op jit(solution)/shard_map/pallas_call | solution.py:147
  82.6 9.0 %all_to_all.22 = bf16[8,16,768]{2,1,0:T(8,128)(2,1)S(1)} all-to-all(bf16[8,16,768]{2,1,0:T(8,128)(2,1)S(1)} %shard_map.77), channel_id=1, replica_groups=mesh['half'=2,'core'=2,'zq'=2,'zc'=4,'xa'=2,'xb'=2,'y'=4] {'zc','xb'}, dimensions={0} | all-to-all | bytes 393216 | tf_op jit(solution)/shard_map/all_to_all | solution.py:221
  91.7 0.1 copy.8
  91.7 0.8 reshape.3
  (2 shorter events, 0.0 us)
Async XLA Ops:
  1.7 22.1 %all-to-all-start = ((bf16[8,16,768]{2,1,0:T(8,128)(2,1)}), bf16[8,16,768]{2,1,0:T(8,128)(2,1)S(1)}, u32[]{:S(2)}, u32[]{:S(2)}) async-start(bf16[8,16,768]{2,1,0:T(8,128)(2,1)} %get-tuple-element.11), calls=%async_computation | async-start | bytes 393216 | tf_op jit(solution)/shard_map/all_to_all | solution.py:176
  9.1 5.9 %collective-permute-start = (bf16[16,1024]{1,0:T(8,128)(2,1)}, bf16[16,1024]{1,0:T(8,128)(2,1)S(1)}, u32[]{:S(2)}, u32[]{:S(2)}) collective-permute-start(bf16[16,1024]{1,0:T(8,128)(2,1)} %get-tuple-element.14), channel_id=1, source_target_pairs={{0,128},{128,0},{1,129},{129,1},{2,130},{130,2},{3,131},{131,3},{4... | collective-permute-start | bytes 98312 | tf_op jit(solution)/shard_map/ppermute | solution.py:178
  15.0 8.8 %collective-permute-start.1 = (bf16[16,1024]{1,0:T(8,128)(2,1)S(1)}, bf16[16,1024]{1,0:T(8,128)(2,1)S(1)}, u32[]{:S(2)}, u32[]{:S(2)}) collective-permute-start(bf16[16,1024]{1,0:T(8,128)(2,1)S(1)} %broadcast_select_fusion.picked_ref), channel_id=1, source_target_pairs={{0,320},{16,336},{32,352},{48,368},{64,256},{80,272},{96,288},{112... | collective-permute-start | bytes 98312 | tf_op jit(solution)/shard_map/ppermute | solution.py:180
  23.8 0.8 copy-start
  68.1 11.1 %copy-start.1 = (s32[4,4]{1,0:T(4,128)S(1)}, s32[4,4]{1,0:T(4,128)}, u32[]{:S(2)}) copy-start(s32[4,4]{1,0:T(4,128)} %mask_ref.1) | copy-start | bytes 196
  68.1 11.0 %collective-permute-start.2 = (bf16[16,128,128]{2,1,0:T(8,128)(2,1)S(1)}, bf16[16,128,128]{2,1,0:T(8,128)(2,1)S(1)}, u32[]{:S(2)}, u32[]{:S(2)}) collective-permute-start(bf16[16,128,128]{2,1,0:T(8,128)(2,1)S(1)} %slice.4), channel_id=1, source_target_pairs={{0,128},{128,0},{1,129},{129,1},{2,130},{130,2},{3,131},{131,3},{4... | collective-permute-start | bytes 1572872 | tf_op jit(solution)/shard_map/ppermute | solution.py:197

commit v3 on v2

--- a/solution.py
+++ b/solution.py
@@ -30,8 +30,11 @@
     )
 
 
-def attend(q, k, v_ones):
-    scores = lax.dot_general(q, k, (((1,), (1,)), ((), ())), preferred_element_type=jnp.float32)
+def scores_of(q, k):
+    return lax.dot_general(q, k, (((1,), (1,)), ((), ())), preferred_element_type=jnp.float32)
+
+
+def weigh(scores, v_ones):
     largest = jnp.max(scores, axis=-1, keepdims=True)
     weights = jnp.exp2((scores - largest) * BASE).astype(jnp.bfloat16)
     return largest, jnp.dot(weights, v_ones, preferred_element_type=jnp.float32)
@@ -46,9 +49,11 @@
     rows = q_ref.shape[0] * q_ref.shape[1]
     k = kv_ref[:, :, :HEAD_DIM].reshape(n, HEAD_DIM)
     v_ones = with_ones(kv_ref[:, :, HEAD_DIM : 2 * HEAD_DIM].reshape(n, HEAD_DIM))
-    for first in range(0, GROUP, count):
+    firsts = range(0, GROUP, count)
+    scores = [scores_of(head_rows(q_ref, first, count), k) for first in firsts]
+    for first, block in zip(firsts, scores):
         at = slice(first * rows, (first + count) * rows)
-        largest, sums = attend(head_rows(q_ref, first, count), k, v_ones)
+        largest, sums = weigh(block, v_ones)
         sums_ref[at, :] = sums
         largest_ref[at, :] = jnp.broadcast_to(largest, (count * rows, HEAD_DIM))
 
@@ -77,9 +82,11 @@
         keys_here = core == 0
         k = jnp.where(keys_here, mine, other)
         v_ones = with_ones(jnp.where(keys_here, other, mine))
-        for first in range(0, GROUP, count):
+        firsts = range(0, GROUP, count)
+        scores = [scores_of(head_rows(q_ref, first, count), k) for first in firsts]
+        for first, block in zip(firsts, scores):
             at = slice(first * rows, (first + count) * rows)
-            largest, sums = attend(head_rows(q_ref, first, count), k, v_ones)
+            largest, sums = weigh(block, v_ones)
             before = largest_ref[at, :]
             after = jnp.maximum(before, largest)
             old = jnp.exp2((before - after) * BASE)
@@ -93,41 +100,53 @@
             store(first, sums_ref[first * rows : (first + count) * rows, :])
 
 
-def stage_kernel(
-    query_ref, key_ref, value_ref, clean_key_ref, clean_value_ref, out_ref, near_ref, mine_ref, sent_ref, sems
-):
+def stage_kernel(query_ref, clean_key_ref, clean_value_ref, out_ref, mine_ref, sent_ref, sems):
     core = lax.axis_index("core")
     copies = [
         pltpu.make_async_copy(query_ref.at[0, :, pl.ds(h * WIDE, WIDE)], out_ref.at[h], sems.at[h])
         for h in range(KV_HEADS)
     ]
-    copies.append(pltpu.make_async_copy(key_ref.at[0], near_ref.at[0], sems.at[KV_HEADS]))
-    copies.append(pltpu.make_async_copy(value_ref.at[0], near_ref.at[1], sems.at[KV_HEADS + 1]))
     for here, kept, given in ((0, clean_key_ref, clean_value_ref), (1, clean_value_ref, clean_key_ref)):
 
         @pl.when(core == here)
         def _():
-            pltpu.make_async_copy(given.at[0], sent_ref, sems.at[KV_HEADS + 2]).start()
-            pltpu.make_async_copy(kept.at[0], mine_ref, sems.at[KV_HEADS + 3]).start()
+            pltpu.make_async_copy(given.at[0], sent_ref, sems.at[KV_HEADS]).start()
+            pltpu.make_async_copy(kept.at[0], mine_ref, sems.at[KV_HEADS + 1]).start()
 
     for copy in copies:
         copy.start()
     for copy in copies:
         copy.wait()
-    pltpu.make_async_copy(clean_key_ref.at[0], sent_ref, sems.at[KV_HEADS + 2]).wait()
-    pltpu.make_async_copy(clean_key_ref.at[0], mine_ref, sems.at[KV_HEADS + 3]).wait()
-
-
-def pack_keys_kernel(completing_ref, near_ref, picked_ref, handed_ref, after_ref, out_ref):
+    pltpu.make_async_copy(clean_key_ref.at[0], sent_ref, sems.at[KV_HEADS]).wait()
+    pltpu.make_async_copy(clean_key_ref.at[0], mine_ref, sems.at[KV_HEADS + 1]).wait()
+
+
+def pair_kernel(key_ref, value_ref, out_ref, key_buf, value_buf, sems):
+    copies = [
+        pltpu.make_async_copy(key_ref.at[0], key_buf, sems.at[0]),
+        pltpu.make_async_copy(value_ref.at[0], value_buf, sems.at[1]),
+    ]
+    for copy in copies:
+        copy.start()
+    for copy in copies:
+        copy.wait()
+    for h in range(KV_HEADS):
+        at = slice(h * HEAD_DIM, (h + 1) * HEAD_DIM)
+        first = (h % 2) * 2 * HEAD_DIM
+        out_ref[h // 2, :, first : first + HEAD_DIM] = key_buf[:, at]
+        out_ref[h // 2, :, first + HEAD_DIM : first + 2 * HEAD_DIM] = value_buf[:, at]
+
+
+def pack_keys_kernel(completing_ref, pairs_ref, picked_ref, handed_ref, after_ref, out_ref):
     del after_ref
     handed = jnp.logical_and(lax.axis_index("half") == 1, completing_ref[0] < 2)
     clean = jnp.where(handed, handed_ref[...], picked_ref[...])
     for h in range(KV_HEADS):
-        at = slice(h * HEAD_DIM, (h + 1) * HEAD_DIM)
         first = (h % 2) * 3 * HEAD_DIM
+        near = pairs_ref[h // 2, :, (h % 2) * 2 * HEAD_DIM : (h % 2 + 1) * 2 * HEAD_DIM]
         for z in (h // 2, h // 2 + KV_HEADS // 2):
-            for i, part in enumerate((near_ref[0, :, at], near_ref[1, :, at], clean[:, at])):
-                out_ref[z, :, first + i * HEAD_DIM : first + (i + 1) * HEAD_DIM] = part
+            out_ref[z, :, first : first + 2 * HEAD_DIM] = near
+            out_ref[z, :, first + 2 * HEAD_DIM : first + 3 * HEAD_DIM] = clean[:, h * HEAD_DIM : (h + 1) * HEAD_DIM]
 
 
 def spread_kernel(served_ref, out_ref):
@@ -166,13 +185,21 @@
     anywhere = pl.BlockSpec(memory_space=pl.ANY)
 
     width = heads * HEAD_DIM
-    packed, near, mine, sent = pl.pallas_call(
+    packed, mine, sent = pl.pallas_call(
         stage_kernel,
-        out_shape=(shaped(heads, tok, WIDE), shaped(2, tok, width), shaped(tok, width), shaped(tok, width)),
-        in_specs=[anywhere] * 5,
-        out_specs=(VMEM,) * 4,
-        scratch_shapes=[pltpu.SemaphoreType.DMA((heads + 4,))],
-    )(query, key, value, clean_key, clean_value)
+        out_shape=(shaped(heads, tok, WIDE), shaped(tok, width), shaped(tok, width)),
+        in_specs=[anywhere] * 3,
+        out_specs=(VMEM,) * 3,
+        scratch_shapes=[pltpu.SemaphoreType.DMA((heads + 2,))],
+    )(query, clean_key, clean_value)
+    pairs = pl.pallas_call(
+        pair_kernel,
+        out_shape=shaped(heads // 2, tok, 4 * HEAD_DIM),
+        in_specs=[anywhere] * 2,
+        out_specs=VMEM,
+        scratch_shapes=[pltpu.VMEM((tok, width), jnp.bfloat16)] * 2 + [pltpu.SemaphoreType.DMA((2,))],
+        compiler_params=pltpu.CompilerParams(vmem_limit_bytes=40 * 2**20),
+    )(key, value)
     served = lax.all_to_all(packed, served_by, 0, 0, tiled=True)
 
     swapped = lax.ppermute(sent, "core", [(0, 1), (1, 0)])
@@ -186,7 +213,7 @@
         shaped(depth, tok, 6 * HEAD_DIM),
         [SMEM] + [VMEM] * 3 + [anywhere],
         completing,
-        near,
+        pairs,
         picked,
         handed,
         served,

time: 93.1 us -> 92.6 us (level)
  blocking collectives: 52.2 us -> 56 us
  Pallas kernels: 8.2 us -> 4.59 us
  starting transfers between devices: 28.1 us -> 26.9 us
  waiting for transfers between devices: 1.39 us -> 0.39 us
    pallas_call x4, Pallas kernels: 6.47 us -> 2.84 us  [call(): pl.pallas_call(kernel, out_shape=out_shape, in_specs=specs, out_specs=out...]
    all_to_all x1, blocking collectives: 9.04 us -> 10.8 us  [shards(): out = lax.all_to_all(out, served_by, 0, 0, tiled=True)]
    all_to_all x1, blocking collectives: 24.1 us -> 25.5 us  [shards(): kv = lax.all_to_all(kv, plane_axes, 0, 0, tiled=True)]
    ppermute x1, starting transfers between devices: 8.15 us -> 6.9 us  [shards(): other = lax.ppermute(kv[:, :, 2 * HEAD_DIM:], 'core', [(0, 1), (1, 0)])]
    ppermute x1, waiting for transfers between devices: 1 us -> 0.01 us  [shards(): lax.ppermute(picked, ('half',) + z_all, [(z, depth + (z + depth // 2) % d...]
  transfers between devices with their start and end apart: 4 -> 4, of which waited for: 2 -> 1; matrix products, arithmetic and copies ran while one was open for 0% -> 1% of each run, Pallas kernels for 3% -> 2%
where the time goes in v3:
time: 92.6 us; the launch traced here: 91.9 us
  blocking collectives  56 us (60%)
  starting transfers between devices  26.9 us (29%)
  Pallas kernels  4.59 us (5%)
  local copies, waits for them, and re-layouts  2.44 us (3%)
    all_to_all x1, blocking collectives, shards(): kv = lax.all_to_all(kv, plane_axes, 0, 0, tiled=True)  25.5 us
    all_to_all x1, blocking collectives, shards(): kv = lax.all_to_all(kv, z_all, 0, 0, tiled=True)  19.8 us
    all_to_all x1, blocking collectives, shards(): out = lax.all_to_all(out, served_by, 0, 0, tiled=True)  10.8 us
    ppermute x1, starting transfers between devices, shards(): lax.ppermute(picked, ('half',) + z_all, [(z, depth + (z + depth // 2) % d...  7.79 us
    all_to_all x1, starting transfers between devices, shards(): served = lax.all_to_all(packed, served_by, 0, 0, tiled=True)  7.39 us
    ppermute x1, starting transfers between devices, shards(): other = lax.ppermute(kv[:, :, 2 * HEAD_DIM:], 'core', [(0, 1), (1, 0)])  6.9 us
    ppermute x1, starting transfers between devices, shards(): swapped = lax.ppermute(sent, 'core', [(0, 1), (1, 0)])  4.81 us
    pallas_call x4, Pallas kernels, call(): pl.pallas_call(kernel, out_shape=out_shape, in_specs=specs, out_specs=out...  2.84 us
  transfers between devices with their start and end apart: 4, of which 1 were waited for; matrix products, arithmetic and copies ran while one was open for 1% of the time, Pallas kernels for 2%

profile of v3, /device:TPU:1, one launch (start us, length us, event | category | flops | bytes accessed | tf_op | source)
XLA Modules:
  0.0 91.9 jit_solution(14668505222406359849)
XLA Ops:
  0.0 1.7 %shard_map.73 = (bf16[8,16,768]{2,1,0:T(8,128)(2,1)}, bf16[16,1024]{1,0:T(8,128)(2,1)}, bf16[16,1024]{1,0:T(8,128)(2,1)}) custom-call(bf16[1,16,6144]{2,1,0:T(8,128)(2,1)} %query_ref.1, bf16[1,16,1024]{2,1,0:T(8,128)(2,1)} %clean_key_ref.1, bf16[1,16,1024]{2,1,0:T(8,128)(2,1)} %clean_value_ref.1), custom_call_target="tpu_custom_call" | custom-call | tf_op jit(solution)/shard_map/pallas_call | solution.py:188
  1.7 7.4 %all-to-all-start = ((bf16[8,16,768]{2,1,0:T(8,128)(2,1)}), bf16[8,16,768]{2,1,0:T(8,128)(2,1)S(1)}, u32[]{:S(2)}, u32[]{:S(2)}) async-start(bf16[8,16,768]{2,1,0:T(8,128)(2,1)} %get-tuple-element.10), calls=%async_computation | async-start | bytes 393216 | tf_op jit(solution)/shard_map/all_to_all | solution.py:203
  9.1 4.8 %collective-permute-start = (bf16[16,1024]{1,0:T(8,128)(2,1)}, bf16[16,1024]{1,0:T(8,128)(2,1)S(1)}, u32[]{:S(2)}, u32[]{:S(2)}) collective-permute-start(bf16[16,1024]{1,0:T(8,128)(2,1)} %get-tuple-element.12), channel_id=1, source_target_pairs={{0,128},{128,0},{1,129},{129,1},{2,130},{130,2},{3,131},{131,3},{4... | collective-permute-start | bytes 98312 | tf_op jit(solution)/shard_map/ppermute | solution.py:205
  14.5 0.4 collective-permute-done
  14.9 0.8 broadcast_select_fusion.picked_ref
  15.7 7.8 %collective-permute-start.1 = (bf16[16,1024]{1,0:T(8,128)(2,1)S(1)}, bf16[16,1024]{1,0:T(8,128)(2,1)S(1)}, u32[]{:S(2)}, u32[]{:S(2)}) collective-permute-start(bf16[16,1024]{1,0:T(8,128)(2,1)S(1)} %broadcast_select_fusion.picked_ref), channel_id=1, source_target_pairs={{0,320},{16,336},{32,352},{48,368},{64,256},{80,272},{96,288},{112... | collective-permute-start | bytes 98312 | tf_op jit(solution)/shard_map/ppermute | solution.py:207
  23.5 0.0 copy-start
  23.5 0.7 copy-done
  24.2 0.0 copy-start.1
  24.2 0.8 copy-done.1
  25.0 0.1 shard_map.74.pairs_ref
  25.1 0.0 collective-permute-done.1.handed_ref
  25.1 0.0 all-to-all-done.after_ref.q_ref
  25.1 19.8 %all_to_all.20.served_ref = bf16[8,16,768]{2,1,0:T(8,128)(2,1)S(1)} all-to-all(bf16[8,16,768]{2,1,0:T(8,128)(2,1)S(1)} %shard_map.75), channel_id=1, replica_groups=mesh['half'=2,'core'=2,'zq'=2,'zc'=4,'xa'=2,'xb'=2,'y'=4] {'zq','zc'}, dimensions={0} | all-to-all | bytes 393216 | tf_op jit(solution)/shard_map/all_to_all | solution.py:221
  44.9 0.1 shard_map.76
  45.1 25.5 %all_to_all.21.kv_ref = bf16[16,128,384]{2,1,0:T(8,128)(2,1)S(1)} all-to-all(bf16[16,128,384]{2,1,0:T(8,128)(2,1)S(1)} %shard_map.76), channel_id=1, replica_groups=mesh['half'=2,'core'=2,'zq'=2,'zc'=4,'xa'=2,'xb'=2,'y'=4] {'xa','xb','y'}, dimensions={0} | all-to-all | bytes 3145728 | tf_op jit(solution)/shard_map/all_to_all | solution.py:223
  70.6 0.1 slice.4
  70.7 0.0 copy-start.2
  70.7 6.9 %collective-permute-start.2 = (bf16[16,128,128]{2,1,0:T(8,128)(2,1)S(1)}, bf16[16,128,128]{2,1,0:T(8,128)(2,1)S(1)}, u32[]{:S(2)}, u32[]{:S(2)}) collective-permute-start(bf16[16,128,128]{2,1,0:T(8,128)(2,1)S(1)} %slice.4), channel_id=1, source_target_pairs={{0,128},{128,0},{1,129},{129,1},{2,130},{130,2},{3,131},{131,3},{4... | collective-permute-start | bytes 1572872 | tf_op jit(solution)/shard_map/ppermute | solution.py:224
  77.6 2.0 %shard_map.77 = (f32[768,256]{1,0:T(8,128)S(1)}, f32[768,128]{1,0:T(8,128)S(1)}) custom-call(bf16[8,16,768]{2,1,0:T(8,128)(2,1)S(1)} %all-to-all-done.after_ref.q_ref, bf16[16,128,384]{2,1,0:T(8,128)(2,1)S(1)} %all_to_all.21.kv_ref), custom_call_target="tpu_custom_call" | custom-call | flops 805306368 | bytes 4194304 | tf_op jit(solution)/shard_map/pallas_call | solution.py:166
  79.6 0.0 collective-permute-done.2.other_ref
  79.6 0.0 copy-done.2
  79.6 0.6 shard_map.78
  80.3 10.8 %all_to_all.22 = bf16[8,16,768]{2,1,0:T(8,128)(2,1)S(1)} all-to-all(bf16[8,16,768]{2,1,0:T(8,128)(2,1)S(1)} %shard_map.78), channel_id=1, replica_groups=mesh['half'=2,'core'=2,'zq'=2,'zc'=4,'xa'=2,'xb'=2,'y'=4] {'zc','xb'}, dimensions={0} | all-to-all | bytes 393216 | tf_op jit(solution)/shard_map/all_to_all | solution.py:248
  91.1 0.1 copy.8
  91.1 0.8 reshape.3
  (1 shorter events, 0.0 us)
Async XLA Ops:
  1.7 23.4 %all-to-all-start = ((bf16[8,16,768]{2,1,0:T(8,128)(2,1)}), bf16[8,16,768]{2,1,0:T(8,128)(2,1)S(1)}, u32[]{:S(2)}, u32[]{:S(2)}) async-start(bf16[8,16,768]{2,1,0:T(8,128)(2,1)} %get-tuple-element.10), calls=%async_computation | async-start | bytes 393216 | tf_op jit(solution)/shard_map/all_to_all | solution.py:203
  9.1 5.9 %collective-permute-start = (bf16[16,1024]{1,0:T(8,128)(2,1)}, bf16[16,1024]{1,0:T(8,128)(2,1)S(1)}, u32[]{:S(2)}, u32[]{:S(2)}) collective-permute-start(bf16[16,1024]{1,0:T(8,128)(2,1)} %get-tuple-element.12), channel_id=1, source_target_pairs={{0,128},{128,0},{1,129},{129,1},{2,130},{130,2},{3,131},{131,3},{4... | collective-permute-start | bytes 98312 | tf_op jit(solution)/shard_map/ppermute | solution.py:205
  15.7 9.4 %collective-permute-start.1 = (bf16[16,1024]{1,0:T(8,128)(2,1)S(1)}, bf16[16,1024]{1,0:T(8,128)(2,1)S(1)}, u32[]{:S(2)}, u32[]{:S(2)}) collective-permute-start(bf16[16,1024]{1,0:T(8,128)(2,1)S(1)} %broadcast_select_fusion.picked_ref), channel_id=1, source_target_pairs={{0,320},{16,336},{32,352},{48,368},{64,256},{80,272},{96,288},{112... | collective-permute-start | bytes 98312 | tf_op jit(solution)/shard_map/ppermute | solution.py:207
  23.5 0.8 copy-start
  24.2 0.8 copy-start.1
  70.7 9.0 %copy-start.2 = (s32[4,4]{1,0:T(4,128)S(1)}, s32[4,4]{1,0:T(4,128)}, u32[]{:S(2)}) copy-start(s32[4,4]{1,0:T(4,128)} %mask_ref.1) | copy-start | bytes 196
  70.7 9.0 %collective-permute-start.2 = (bf16[16,128,128]{2,1,0:T(8,128)(2,1)S(1)}, bf16[16,128,128]{2,1,0:T(8,128)(2,1)S(1)}, u32[]{:S(2)}, u32[]{:S(2)}) collective-permute-start(bf16[16,128,128]{2,1,0:T(8,128)(2,1)S(1)} %slice.4), channel_id=1, source_target_pairs={{0,128},{128,0},{1,129},{129,1},{2,130},{130,2},{3,131},{131,3},{4... | collective-permute-start | bytes 1572872 | tf_op jit(solution)/shard_map/ppermute | solution.py:224

commit v4 on v3

--- a/solution.py
+++ b/solution.py
@@ -100,12 +100,13 @@
             store(first, sums_ref[first * rows : (first + count) * rows, :])
 
 
-def stage_kernel(query_ref, clean_key_ref, clean_value_ref, out_ref, mine_ref, sent_ref, sems):
-    core = lax.axis_index("core")
-    copies = [
-        pltpu.make_async_copy(query_ref.at[0, :, pl.ds(h * WIDE, WIDE)], out_ref.at[h], sems.at[h])
-        for h in range(KV_HEADS)
-    ]
+def stage_kernel(query_ref, clean_key_ref, clean_value_ref, keep_ref, send_ref, mine_ref, sent_ref, sems):
+    core, xb = lax.axis_index("core"), lax.axis_index("xb")
+    copies = []
+    for z in range(KV_HEADS // 2):
+        for i, (target, x) in enumerate(((keep_ref, xb), (send_ref, 1 - xb))):
+            at = pl.ds(pl.multiple_of((2 * z + x) * WIDE, WIDE), WIDE)
+            copies.append(pltpu.make_async_copy(query_ref.at[0, :, at], target.at[z], sems.at[2 * z + i]))
     for here, kept, given in ((0, clean_key_ref, clean_value_ref), (1, clean_value_ref, clean_key_ref)):
 
         @pl.when(core == here)
@@ -119,6 +120,31 @@
         copy.wait()
     pltpu.make_async_copy(clean_key_ref.at[0], sent_ref, sems.at[KV_HEADS]).wait()
     pltpu.make_async_copy(clean_key_ref.at[0], mine_ref, sems.at[KV_HEADS + 1]).wait()
+
+
+def second_kernel(kept_ref, got_ref, keep_ref, send_ref):
+    xb, low = lax.axis_index("xb"), lax.rem(lax.axis_index("zc"), 2)
+    for source, x in ((kept_ref, xb), (got_ref, 1 - xb)):
+        for high in range(2):
+            keep_ref[x, high] = source[2 * high + low]
+            send_ref[x, high] = source[2 * high + 1 - low]
+
+
+def third_kernel(kept_ref, got_ref, keep_ref, send_ref):
+    zc = lax.axis_index("zc")
+    low, high = lax.rem(zc, 2), lax.div(zc, 2)
+    for source, z in ((kept_ref, low), (got_ref, 1 - low)):
+        for x in range(2):
+            keep_ref[z, x] = source[x, high]
+            send_ref[z, x] = source[x, 1 - high]
+
+
+def last_kernel(kept_ref, got_ref, out_ref):
+    high = lax.div(lax.axis_index("zc"), 2)
+    for source, z in ((kept_ref, high), (got_ref, 1 - high)):
+        for low in range(2):
+            for x in range(2):
+                out_ref[4 * z + 2 * low + x] = source[low, x]
 
 
 def pair_kernel(key_ref, value_ref, out_ref, key_buf, value_buf, sems):
@@ -137,8 +163,7 @@
         out_ref[h // 2, :, first + HEAD_DIM : first + 2 * HEAD_DIM] = value_buf[:, at]
 
 
-def pack_keys_kernel(completing_ref, pairs_ref, picked_ref, handed_ref, after_ref, out_ref):
-    del after_ref
+def pack_keys_kernel(completing_ref, pairs_ref, picked_ref, handed_ref, out_ref):
     handed = jnp.logical_and(lax.axis_index("half") == 1, completing_ref[0] < 2)
     clean = jnp.where(handed, handed_ref[...], picked_ref[...])
     for h in range(KV_HEADS):
@@ -149,12 +174,18 @@
             out_ref[z, :, first + 2 * HEAD_DIM : first + 3 * HEAD_DIM] = clean[:, h * HEAD_DIM : (h + 1) * HEAD_DIM]
 
 
-def spread_kernel(served_ref, out_ref):
+def spread_kernel(served_ref, after_ref, out_ref):
+    del after_ref
     rows = served_ref.shape[0] * served_ref.shape[1]
     each = 3 * HEAD_DIM
     for i in range(out_ref.shape[0]):
         head = (i // 4) % 2
         out_ref[i] = served_ref[:, :, head * each : (head + 1) * each].reshape(rows, each)
+
+
+def clean_kernel(kv_ref, after_ref, out_ref):
+    del after_ref
+    out_ref[...] = kv_ref[:, :, 2 * HEAD_DIM :]
 
 
 def estimate(q_rows, n):
@@ -185,13 +216,23 @@
     anywhere = pl.BlockSpec(memory_space=pl.ANY)
 
     width = heads * HEAD_DIM
-    packed, mine, sent = pl.pallas_call(
+    part = heads // 2
+    keep, send, mine, sent = pl.pallas_call(
         stage_kernel,
-        out_shape=(shaped(heads, tok, WIDE), shaped(tok, width), shaped(tok, width)),
+        out_shape=(shaped(part, tok, WIDE),) * 2 + (shaped(tok, width),) * 2,
         in_specs=[anywhere] * 3,
-        out_specs=(VMEM,) * 3,
+        out_specs=(VMEM,) * 4,
         scratch_shapes=[pltpu.SemaphoreType.DMA((heads + 2,))],
     )(query, clean_key, clean_value)
+    got = lax.ppermute(send, "xb", [(0, 1), (1, 0)])
+    halves = (shaped(2, 2, tok, WIDE),) * 2
+    keep, send = call(second_kernel, halves, [VMEM] * 2, keep, got)
+    after_first = keep
+    got = lax.ppermute(send, "zc", [(z, z ^ 1) for z in range(4)])
+    keep, send = call(third_kernel, halves, [VMEM] * 2, keep, got)
+    got = lax.ppermute(send, "zc", [(z, z ^ 2) for z in range(4)])
+    served = call(last_kernel, shaped(heads, tok, WIDE), [VMEM] * 2, keep, got)
+
     pairs = pl.pallas_call(
         pair_kernel,
         out_shape=shaped(heads // 2, tok, 4 * HEAD_DIM),
@@ -200,7 +241,6 @@
         scratch_shapes=[pltpu.VMEM((tok, width), jnp.bfloat16)] * 2 + [pltpu.SemaphoreType.DMA((2,))],
         compiler_params=pltpu.CompilerParams(vmem_limit_bytes=40 * 2**20),
     )(key, value)
-    served = lax.all_to_all(packed, served_by, 0, 0, tiled=True)
 
     swapped = lax.ppermute(sent, "core", [(0, 1), (1, 0)])
     picked = jnp.where(completing[0] % 2 == lax.axis_index("core"), mine, swapped)
@@ -211,17 +251,17 @@
     kv = call(
         pack_keys_kernel,
         shaped(depth, tok, 6 * HEAD_DIM),
-        [SMEM] + [VMEM] * 3 + [anywhere],
+        [SMEM] + [VMEM] * 3,
         completing,
         pairs,
         picked,
         handed,
-        served,
     )
     kv = lax.all_to_all(kv, z_all, 0, 0, tiled=True)
-    kv = call(spread_kernel, shaped(plane, depth * tok, 3 * HEAD_DIM), [VMEM], kv)
+    kv = call(spread_kernel, shaped(plane, depth * tok, 3 * HEAD_DIM), [VMEM, anywhere], kv, after_first)
     kv = lax.all_to_all(kv, plane_axes, 0, 0, tiled=True)
-    other = lax.ppermute(kv[:, :, 2 * HEAD_DIM :], "core", [(0, 1), (1, 0)])
+    clean = call(clean_kernel, shaped(plane, depth * tok, HEAD_DIM), [VMEM, anywhere], kv, served)
+    other = lax.ppermute(clean, "core", [(0, 1), (1, 0)])
 
     rows, n = heads * tok * GROUP, plane * depth * tok
     sums, largest = call(

time: 92.6 us -> 89.2 us (0.963)
  blocking collectives: 56 us -> 10.4 us
  waiting for transfers between devices: 0.39 us -> 19.8 us
  starting transfers between devices: 26.9 us -> 45.7 us
  Pallas kernels: 4.59 us -> 8.43 us
    all_to_all x2 -> x0, blocking collectives: 45.3 us -> none  [the longest x1 25.5 us: shards(): kv = lax.all_to_all(kv, plane_axes, 0, 0, tiled=True)]
    all_to_all x1 -> x2, waiting for transfers between devices: 0.01 us -> 10.4 us  [the longest x1 5.84 us: shards(): kv = lax.all_to_all(kv, plane_axes, 0, 0, tiled=True)]
    ppermute x1 -> x4, starting transfers between devices: 6.9 us -> 17.2 us  [the longest x1 7.59 us: shards(): other = lax.ppermute(clean, 'core', [(0, 1), (1, 0)])]
    ppermute x1 -> x4, waiting for transfers between devices: 0.01 us -> 9.07 us  [the longest x1 3.43 us: shards(): got = lax.ppermute(send, 'zc', [(z, z ^ 1) for z in range(4)])]
    all_to_all x1 -> x2, starting transfers between devices: 7.39 us -> 12.7 us  [the longest x1 6.75 us: shards(): kv = lax.all_to_all(kv, plane_axes, 0, 0, tiled=True)]
    ppermute x1, starting transfers between devices: 4.81 us -> 8.79 us  [shards(): swapped = lax.ppermute(sent, 'core', [(0, 1), (1, 0)])]
    pallas_call x4 -> x8, Pallas kernels: 2.84 us -> 6.69 us  [call(): pl.pallas_call(kernel, out_shape=out_shape, in_specs=specs, out_specs=out...]
    unnamed x6 -> x8, local copies, waits for them, and re-layouts: 1.52 us -> 2.41 us
  transfers between devices with their start and end apart: 4 -> 8, of which waited for: 1 -> 6; matrix products, arithmetic and copies ran while one was open for 1% -> 0% of each run, Pallas kernels for 2% -> 2%
where the time goes in v4:
time: 89.2 us; the launch traced here: 88.4 us
  starting transfers between devices  45.7 us (51%)
  waiting for transfers between devices  19.8 us (22%)
  blocking collectives  10.4 us (12%)
  Pallas kernels  8.43 us (9%)
  local copies, waits for them, and re-layouts  3.24 us (4%)
    all_to_all x1, blocking collectives, shards(): out = lax.all_to_all(out, served_by, 0, 0, tiled=True)  10.4 us
    ppermute x1, starting transfers between devices, shards(): swapped = lax.ppermute(sent, 'core', [(0, 1), (1, 0)])  8.79 us
    ppermute x1, starting transfers between devices, shards(): other = lax.ppermute(clean, 'core', [(0, 1), (1, 0)])  7.59 us
    ppermute x1, starting transfers between devices, shards(): lax.ppermute(picked, ('half',) + z_all, [(z, depth + (z + depth // 2) % d...  7.08 us
    all_to_all x1, starting transfers between devices, shards(): kv = lax.all_to_all(kv, plane_axes, 0, 0, tiled=True)  6.75 us
    pallas_call x8, Pallas kernels, call(): pl.pallas_call(kernel, out_shape=out_shape, in_specs=specs, out_specs=out...  6.69 us
    all_to_all x1, starting transfers between devices, shards(): kv = lax.all_to_all(kv, z_all, 0, 0, tiled=True)  5.91 us
    all_to_all x1, waiting for transfers between devices, shards(): kv = lax.all_to_all(kv, plane_axes, 0, 0, tiled=True)  5.84 us
  transfers between devices with their start and end apart: 8, of which 6 were waited for; matrix products, arithmetic and copies ran while one was open for 0% of the time, Pallas kernels for 2%

profile of v4, /device:TPU:1, one launch (start us, length us, event | category | flops | bytes accessed | tf_op | source)
XLA Modules:
  0.0 88.4 jit_solution(17417679718373508505)
XLA Ops:
  0.0 1.7 %shard_map.73 = (bf16[4,16,768]{2,1,0:T(8,128)(2,1)}, bf16[4,16,768]{2,1,0:T(8,128)(2,1)}, bf16[16,1024]{1,0:T(8,128)(2,1)}, bf16[16,1024]{1,0:T(8,128)(2,1)}) custom-call(bf16[1,16,6144]{2,1,0:T(8,128)(2,1)} %query_ref.1, bf16[1,16,1024]{2,1,0:T(8,128)(2,1)} %clean_key_ref.1, bf16[1,16,1024]{2,1,0:T(8,128)(2,1)} %clean_value_ref.1), custom_call_target="tpu_custom_call" | custom-call | tf_op jit(solution)/shard_map/pallas_call | solution.py:220
  1.7 8.8 %collective-permute-start.3 = (bf16[16,1024]{1,0:T(8,128)(2,1)}, bf16[16,1024]{1,0:T(8,128)(2,1)S(1)}, u32[]{:S(2)}, u32[]{:S(2)}) collective-permute-start(bf16[16,1024]{1,0:T(8,128)(2,1)} %get-tuple-element.22), channel_id=1, source_target_pairs={{0,128},{128,0},{1,129},{129,1},{2,130},{130,2},{3,131},{131,3},{4... | collective-permute-start | bytes 98312 | tf_op jit(solution)/shard_map/ppermute | solution.py:245
  11.1 0.4 collective-permute-done.3
  11.5 7.1 %collective-permute-start.4 = (bf16[16,1024]{1,0:T(8,128)(2,1)S(1)}, bf16[16,1024]{1,0:T(8,128)(2,1)S(1)}, u32[]{:S(2)}, u32[]{:S(2)}) collective-permute-start(bf16[16,1024]{1,0:T(8,128)(2,1)S(1)} %broadcast_select_fusion.picked_ref), channel_id=1, source_target_pairs={{0,320},{16,336},{32,352},{48,368},{64,256},{80,272},{96,288},{112... | collective-permute-start | bytes 98312 | tf_op jit(solution)/shard_map/ppermute | solution.py:247
  18.6 0.0 copy-start.1
  18.6 0.7 copy-done.1
  19.4 0.8 copy-done.2
  20.1 0.1 shard_map.77.pairs_ref
  20.2 0.0 collective-permute-done.4.handed_ref
  20.2 0.7 shard_map.78
  20.9 5.9 %all-to-all-start = ((bf16[8,16,768]{2,1,0:T(8,128)(2,1)}), bf16[8,16,768]{2,1,0:T(8,128)(2,1)S(1)}, u32[]{:S(2)}, u32[]{:S(2)}) async-start(bf16[8,16,768]{2,1,0:T(8,128)(2,1)} %shard_map.78), calls=%async_computation | async-start | bytes 393216 | tf_op jit(solution)/shard_map/all_to_all | solution.py:260
  26.8 3.1 %collective-permute-start = (bf16[4,16,768]{2,1,0:T(8,128)(2,1)}, bf16[4,16,768]{2,1,0:T(8,128)(2,1)S(1)}, u32[]{:S(2)}, u32[]{:S(2)}) collective-permute-start(bf16[4,16,768]{2,1,0:T(8,128)(2,1)} %get-tuple-element.16), channel_id=1, source_target_pairs={{0,4},{4,0},{1,5},{5,1},{2,6},{6,2},{3,7},{7,3},{8,12},{12,8},{9,1... | collective-permute-start | bytes 294920 | tf_op jit(solution)/shard_map/ppermute | solution.py:227
  30.0 2.4 %collective-permute-done.got_ref = bf16[4,16,768]{2,1,0:T(8,128)(2,1)S(1)} collective-permute-done((bf16[4,16,768]{2,1,0:T(8,128)(2,1)}, bf16[4,16,768]{2,1,0:T(8,128)(2,1)S(1)}, u32[]{:S(2)}, u32[]{:S(2)}) %collective-permute-start) | collective-permute-done | bytes 98336 | tf_op jit(solution)/shard_map/ppermute | solution.py:227
  32.4 0.9 %copy-done = bf16[4,16,768]{2,1,0:T(8,128)(2,1)S(1)} copy-done((bf16[4,16,768]{2,1,0:T(8,128)(2,1)S(1)}, bf16[4,16,768]{2,1,0:T(8,128)(2,1)}, u32[]{:S(2)}) %copy-start) | copy-done | bytes 98328
  33.3 4.5 %all-to-all-done.served_ref = bf16[8,16,768]{2,1,0:T(8,128)(2,1)S(1)} async-done(((bf16[8,16,768]{2,1,0:T(8,128)(2,1)}), bf16[8,16,768]{2,1,0:T(8,128)(2,1)S(1)}, u32[]{:S(2)}, u32[]{:S(2)}) %all-to-all-start) | async-done | bytes 196640 | tf_op jit(solution)/shard_map/all_to_all | solution.py:260
  37.8 1.3 %shard_map.79 = bf16[16,128,384]{2,1,0:T(8,128)(2,1)} custom-call(bf16[8,16,768]{2,1,0:T(8,128)(2,1)S(1)} %all-to-all-done.served_ref, bf16[2,2,16,768]{3,2,1,0:T(8,128)(2,1)S(1)} %get-tuple-element.17.kept_ref.after_ref), custom_call_target="tpu_custom_call" | custom-call | tf_op jit(solution)/shard_map/pallas_call | solution.py:197
  39.1 6.8 %all-to-all-start.1 = ((bf16[16,128,384]{2,1,0:T(8,128)(2,1)}), bf16[16,128,384]{2,1,0:T(8,128)(2,1)S(1)}, u32[]{:S(2)}, u32[]{:S(2)}) async-start(bf16[16,128,384]{2,1,0:T(8,128)(2,1)} %shard_map.79), calls=%async_computation.1 | async-start | bytes 3145728 | tf_op jit(solution)/shard_map/all_to_all | solution.py:262
  45.9 1.9 %collective-permute-start.1 = (bf16[2,2,16,768]{3,2,1,0:T(8,128)(2,1)S(1)}, bf16[2,2,16,768]{3,2,1,0:T(8,128)(2,1)S(1)}, u32[]{:S(2)}, u32[]{:S(2)}) collective-permute-start(bf16[2,2,16,768]{3,2,1,0:T(8,128)(2,1)S(1)} %get-tuple-element.18), channel_id=1, source_target_pairs={{0,16},{16,0},{32,48},{48,32},{1,17},{17,1},{33,49},{49,33},{2,18}... | collective-permute-start | bytes 294920 | tf_op jit(solution)/shard_map/ppermute | solution.py:231
  47.8 3.4 %collective-permute-done.1.got_ref = bf16[2,2,16,768]{3,2,1,0:T(8,128)(2,1)S(1)} collective-permute-done((bf16[2,2,16,768]{3,2,1,0:T(8,128)(2,1)S(1)}, bf16[2,2,16,768]{3,2,1,0:T(8,128)(2,1)S(1)}, u32[]{:S(2)}, u32[]{:S(2)}) %collective-permute-start.1) | collective-permute-done | bytes 98336 | tf_op jit(solution)/shard_map/ppermute | solution.py:231
  51.3 4.6 %collective-permute-start.2 = (bf16[2,2,16,768]{3,2,1,0:T(8,128)(2,1)S(1)}, bf16[2,2,16,768]{3,2,1,0:T(8,128)(2,1)S(1)}, u32[]{:S(2)}, u32[]{:S(2)}) collective-permute-start(bf16[2,2,16,768]{3,2,1,0:T(8,128)(2,1)S(1)} %get-tuple-element.20), channel_id=1, source_target_pairs={{0,32},{16,48},{32,0},{48,16},{1,33},{17,49},{33,1},{49,17},{2,34}... | collective-permute-start | bytes 294920 | tf_op jit(solution)/shard_map/ppermute | solution.py:233
  55.9 3.2 %collective-permute-done.2.got_ref = bf16[2,2,16,768]{3,2,1,0:T(8,128)(2,1)S(1)} collective-permute-done((bf16[2,2,16,768]{3,2,1,0:T(8,128)(2,1)S(1)}, bf16[2,2,16,768]{3,2,1,0:T(8,128)(2,1)S(1)}, u32[]{:S(2)}, u32[]{:S(2)}) %collective-permute-start.2) | collective-permute-done | bytes 98336 | tf_op jit(solution)/shard_map/ppermute | solution.py:233
  59.1 5.8 %all-to-all-done.1.kv_ref = bf16[16,128,384]{2,1,0:T(8,128)(2,1)S(1)} async-done(((bf16[16,128,384]{2,1,0:T(8,128)(2,1)}), bf16[16,128,384]{2,1,0:T(8,128)(2,1)S(1)}, u32[]{:S(2)}, u32[]{:S(2)}) %all-to-all-start.1) | async-done | bytes 1572896 | tf_op jit(solution)/shard_map/all_to_all | solution.py:262
  64.9 0.1 shard_map.80
  65.0 0.0 copy-start.3
  65.0 7.6 %collective-permute-start.5 = (bf16[16,128,128]{2,1,0:T(8,128)(2,1)S(1)}, bf16[16,128,128]{2,1,0:T(8,128)(2,1)S(1)}, u32[]{:S(2)}, u32[]{:S(2)}) collective-permute-start(bf16[16,128,128]{2,1,0:T(8,128)(2,1)S(1)} %shard_map.80), channel_id=1, source_target_pairs={{0,128},{128,0},{1,129},{129,1},{2,130},{130,2},{3,131},{131,3},{4... | collective-permute-start | bytes 1572872 | tf_op jit(solution)/shard_map/ppermute | solution.py:264
  72.6 1.9 %shard_map.81 = (f32[768,256]{1,0:T(8,128)S(1)}, f32[768,128]{1,0:T(8,128)S(1)}) custom-call(bf16[8,16,768]{2,1,0:T(8,128)(2,1)S(1)} %shard_map.76.after_ref.q_ref, bf16[16,128,384]{2,1,0:T(8,128)(2,1)S(1)} %all-to-all-done.1.kv_ref), custom_call_target="tpu_custom_call" | custom-call | flops 805306368 | bytes 4194304 | tf_op jit(solution)/shard_map/pallas_call | solution.py:197
  74.6 0.0 collective-permute-done.5.other_ref
  74.6 0.0 copy-done.3
  74.6 2.6 %shard_map.82 = bf16[8,16,768]{2,1,0:T(8,128)(2,1)S(1)} custom-call(s32[1]{0:T(128)} %copy.9.completing_ref, s32[4,4]{1,0:T(4,128)S(1)} %copy-done.3, bf16[8,16,768]{2,1,0:T(8,128)(2,1)S(1)} %shard_map.76.after_ref.q_ref, bf16[16,128,384]{2,1,0:T(8,128)(2,1)S(1)} %all-to-all-done.1.kv_ref, bf16[16,128,128]{2,1,0:T(8,128)(2,1)S(1)} %collective-permute-done.5.other_ref, ...), custom_call_target="tpu_custom_call" | custom-call | flops 805306368 | bytes 4194304 | tf_op jit(solution)/shard_map/pallas_call | solution.py:197
  77.2 10.4 %all_to_all.15 = bf16[8,16,768]{2,1,0:T(8,128)(2,1)S(1)} all-to-all(bf16[8,16,768]{2,1,0:T(8,128)(2,1)S(1)} %shard_map.82), channel_id=1, replica_groups=mesh['half'=2,'core'=2,'zq'=2,'zc'=4,'xa'=2,'xb'=2,'y'=4] {'zc','xb'}, dimensions={0} | all-to-all | bytes 393216 | tf_op jit(solution)/shard_map/all_to_all | solution.py:288
  87.6 0.1 copy.8
  87.6 0.8 reshape.3
  (6 shorter events, 0.1 us)
Async XLA Ops:
  1.7 9.8 %collective-permute-start.3 = (bf16[16,1024]{1,0:T(8,128)(2,1)}, bf16[16,1024]{1,0:T(8,128)(2,1)S(1)}, u32[]{:S(2)}, u32[]{:S(2)}) collective-permute-start(bf16[16,1024]{1,0:T(8,128)(2,1)} %get-tuple-element.22), channel_id=1, source_target_pairs={{0,128},{128,0},{1,129},{129,1},{2,130},{130,2},{3,131},{131,3},{4... | collective-permute-start | bytes 98312 | tf_op jit(solution)/shard_map/ppermute | solution.py:245
  11.5 8.7 %collective-permute-start.4 = (bf16[16,1024]{1,0:T(8,128)(2,1)S(1)}, bf16[16,1024]{1,0:T(8,128)(2,1)S(1)}, u32[]{:S(2)}, u32[]{:S(2)}) collective-permute-start(bf16[16,1024]{1,0:T(8,128)(2,1)S(1)} %broadcast_select_fusion.picked_ref), channel_id=1, source_target_pairs={{0,320},{16,336},{32,352},{48,368},{64,256},{80,272},{96,288},{112... | collective-permute-start | bytes 98312 | tf_op jit(solution)/shard_map/ppermute | solution.py:247
  18.6 0.8 copy-start.1
  19.4 0.8 copy-start.2
  20.9 16.9 %all-to-all-start = ((bf16[8,16,768]{2,1,0:T(8,128)(2,1)}), bf16[8,16,768]{2,1,0:T(8,128)(2,1)S(1)}, u32[]{:S(2)}, u32[]{:S(2)}) async-start(bf16[8,16,768]{2,1,0:T(8,128)(2,1)} %shard_map.78), calls=%async_computation | async-start | bytes 393216 | tf_op jit(solution)/shard_map/all_to_all | solution.py:260
  26.8 5.6 %collective-permute-start = (bf16[4,16,768]{2,1,0:T(8,128)(2,1)}, bf16[4,16,768]{2,1,0:T(8,128)(2,1)S(1)}, u32[]{:S(2)}, u32[]{:S(2)}) collective-permute-start(bf16[4,16,768]{2,1,0:T(8,128)(2,1)} %get-tuple-element.16), channel_id=1, source_target_pairs={{0,4},{4,0},{1,5},{5,1},{2,6},{6,2},{3,7},{7,3},{8,12},{12,8},{9,1... | collective-permute-start | bytes 294920 | tf_op jit(solution)/shard_map/ppermute | solution.py:227
  32.4 0.9 %copy-start = (bf16[4,16,768]{2,1,0:T(8,128)(2,1)S(1)}, bf16[4,16,768]{2,1,0:T(8,128)(2,1)}, u32[]{:S(2)}) copy-start(bf16[4,16,768]{2,1,0:T(8,128)(2,1)} %get-tuple-element.15.kept_ref) | copy-start | bytes 294916
  39.1 25.8 %all-to-all-start.1 = ((bf16[16,128,384]{2,1,0:T(8,128)(2,1)}), bf16[16,128,384]{2,1,0:T(8,128)(2,1)S(1)}, u32[]{:S(2)}, u32[]{:S(2)}) async-start(bf16[16,128,384]{2,1,0:T(8,128)(2,1)} %shard_map.79), calls=%async_computation.1 | async-start | bytes 3145728 | tf_op jit(solution)/shard_map/all_to_all | solution.py:262
  45.9 5.4 %collective-permute-start.1 = (bf16[2,2,16,768]{3,2,1,0:T(8,128)(2,1)S(1)}, bf16[2,2,16,768]{3,2,1,0:T(8,128)(2,1)S(1)}, u32[]{:S(2)}, u32[]{:S(2)}) collective-permute-start(bf16[2,2,16,768]{3,2,1,0:T(8,128)(2,1)S(1)} %get-tuple-element.18), channel_id=1, source_target_pairs={{0,16},{16,0},{32,48},{48,32},{1,17},{17,1},{33,49},{49,33},{2,18}... | collective-permute-start | bytes 294920 | tf_op jit(solution)/shard_map/ppermute | solution.py:231
  51.3 7.8 %collective-permute-start.2 = (bf16[2,2,16,768]{3,2,1,0:T(8,128)(2,1)S(1)}, bf16[2,2,16,768]{3,2,1,0:T(8,128)(2,1)S(1)}, u32[]{:S(2)}, u32[]{:S(2)}) collective-permute-start(bf16[2,2,16,768]{3,2,1,0:T(8,128)(2,1)S(1)} %get-tuple-element.20), channel_id=1, source_target_pairs={{0,32},{16,48},{32,0},{48,16},{1,33},{17,49},{33,1},{49,17},{2,34}... | collective-permute-start | bytes 294920 | tf_op jit(solution)/shard_map/ppermute | solution.py:233
  65.0 9.6 %copy-start.3 = (s32[4,4]{1,0:T(4,128)S(1)}, s32[4,4]{1,0:T(4,128)}, u32[]{:S(2)}) copy-start(s32[4,4]{1,0:T(4,128)} %mask_ref.1) | copy-start | bytes 196
  65.0 9.5 %collective-permute-start.5 = (bf16[16,128,128]{2,1,0:T(8,128)(2,1)S(1)}, bf16[16,128,128]{2,1,0:T(8,128)(2,1)S(1)}, u32[]{:S(2)}, u32[]{:S(2)}) collective-permute-start(bf16[16,128,128]{2,1,0:T(8,128)(2,1)S(1)} %shard_map.80), channel_id=1, source_target_pairs={{0,128},{128,0},{1,129},{129,1},{2,130},{130,2},{3,131},{131,3},{4... | collective-permute-start | bytes 1572872 | tf_op jit(solution)/shard_map/ppermute | solution.py:264

commit v5 on v4

--- a/solution.py
+++ b/solution.py
@@ -100,26 +100,18 @@
             store(first, sums_ref[first * rows : (first + count) * rows, :])
 
 
-def stage_kernel(query_ref, clean_key_ref, clean_value_ref, keep_ref, send_ref, mine_ref, sent_ref, sems):
-    core, xb = lax.axis_index("core"), lax.axis_index("xb")
+def stage_kernel(query_ref, after_ref, keep_ref, send_ref, sems):
+    del after_ref
+    xb = lax.axis_index("xb")
     copies = []
     for z in range(KV_HEADS // 2):
         for i, (target, x) in enumerate(((keep_ref, xb), (send_ref, 1 - xb))):
             at = pl.ds(pl.multiple_of((2 * z + x) * WIDE, WIDE), WIDE)
             copies.append(pltpu.make_async_copy(query_ref.at[0, :, at], target.at[z], sems.at[2 * z + i]))
-    for here, kept, given in ((0, clean_key_ref, clean_value_ref), (1, clean_value_ref, clean_key_ref)):
-
-        @pl.when(core == here)
-        def _():
-            pltpu.make_async_copy(given.at[0], sent_ref, sems.at[KV_HEADS]).start()
-            pltpu.make_async_copy(kept.at[0], mine_ref, sems.at[KV_HEADS + 1]).start()
-
     for copy in copies:
         copy.start()
     for copy in copies:
         copy.wait()
-    pltpu.make_async_copy(clean_key_ref.at[0], sent_ref, sems.at[KV_HEADS]).wait()
-    pltpu.make_async_copy(clean_key_ref.at[0], mine_ref, sems.at[KV_HEADS + 1]).wait()
 
 
 def second_kernel(kept_ref, got_ref, keep_ref, send_ref):
@@ -147,7 +139,9 @@
                 out_ref[4 * z + 2 * low + x] = source[low, x]
 
 
-def pair_kernel(key_ref, value_ref, out_ref, key_buf, value_buf, sems):
+def pair_kernel(key_ref, value_ref, sent_ref, after_ref, out_ref, late_ref, key_buf, value_buf, sems):
+    del after_ref
+    late_ref[...] = sent_ref[...]
     copies = [
         pltpu.make_async_copy(key_ref.at[0], key_buf, sems.at[0]),
         pltpu.make_async_copy(value_ref.at[0], value_buf, sems.at[1]),
@@ -163,9 +157,11 @@
         out_ref[h // 2, :, first + HEAD_DIM : first + 2 * HEAD_DIM] = value_buf[:, at]
 
 
-def pack_keys_kernel(completing_ref, pairs_ref, picked_ref, handed_ref, out_ref):
-    handed = jnp.logical_and(lax.axis_index("half") == 1, completing_ref[0] < 2)
-    clean = jnp.where(handed, handed_ref[...], picked_ref[...])
+def pack_keys_kernel(completing_ref, pairs_ref, picked_ref, late_ref, handed_ref, out_ref):
+    upper = lax.axis_index("half") == 1
+    handed = jnp.logical_and(upper, completing_ref[0] < 2)
+    late = jnp.logical_and(upper, lax.axis_index("core") == 1)
+    clean = jnp.where(handed, handed_ref[...], jnp.where(late, late_ref[...], picked_ref[...]))
     for h in range(KV_HEADS):
         first = (h % 2) * 3 * HEAD_DIM
         near = pairs_ref[h // 2, :, (h % 2) * 2 * HEAD_DIM : (h % 2 + 1) * 2 * HEAD_DIM]
@@ -192,7 +188,7 @@
     return pl.CostEstimate(flops=4 * q_rows * n * HEAD_DIM, bytes_accessed=4 * 2**20, transcendentals=q_rows * n)
 
 
-def call(kernel, out_shape, specs, *operands, cost=None):
+def call(kernel, out_shape, specs, *operands, cost=None, mib=16):
     outs = (VMEM,) * len(out_shape) if isinstance(out_shape, tuple) else VMEM
     return pl.pallas_call(
         kernel,
@@ -200,7 +196,7 @@
         in_specs=specs,
         out_specs=outs,
         cost_estimate=cost,
-        compiler_params=pltpu.CompilerParams(vmem_limit_bytes=40 * 2**20),
+        compiler_params=pltpu.CompilerParams(vmem_limit_bytes=mib * 2**20),
     )(*operands)
 
 
@@ -216,14 +212,43 @@
     anywhere = pl.BlockSpec(memory_space=pl.ANY)
 
     width = heads * HEAD_DIM
+    core = lax.axis_index("core")
+    mine = jnp.where(core == 0, clean_key[0], clean_value[0])
+    sent = jnp.where(core == 0, clean_value[0], clean_key[0])
+    swapped = lax.ppermute(sent, ("half", "core"), [(0, 1), (1, 0)])
+    picked = jnp.where(completing[0] % 2 == core, mine, swapped)
+    handed = lax.ppermute(
+        picked, ("half",) + z_all, [(z, depth + (z + depth // 2) % depth) for z in range(depth)]
+    )
+    pairs, late = pl.pallas_call(
+        pair_kernel,
+        out_shape=(shaped(heads // 2, tok, 4 * HEAD_DIM), shaped(tok, width)),
+        in_specs=[anywhere] * 2 + [VMEM, anywhere],
+        out_specs=(VMEM,) * 2,
+        scratch_shapes=[pltpu.VMEM((tok, width), jnp.bfloat16)] * 2 + [pltpu.SemaphoreType.DMA((2,))],
+        compiler_params=pltpu.CompilerParams(vmem_limit_bytes=16 * 2**20),
+    )(key, value, sent, picked)
+    late = lax.ppermute(late, ("half", "core"), [(2, 3)])
+
+    kv = call(
+        pack_keys_kernel,
+        shaped(depth, tok, 6 * HEAD_DIM),
+        [SMEM] + [VMEM] * 4,
+        completing,
+        pairs,
+        picked,
+        late,
+        handed,
+    )
     part = heads // 2
-    keep, send, mine, sent = pl.pallas_call(
+    keep, send = pl.pallas_call(
         stage_kernel,
-        out_shape=(shaped(part, tok, WIDE),) * 2 + (shaped(tok, width),) * 2,
-        in_specs=[anywhere] * 3,
-        out_specs=(VMEM,) * 4,
-        scratch_shapes=[pltpu.SemaphoreType.DMA((heads + 2,))],
-    )(query, clean_key, clean_value)
+        out_shape=(shaped(part, tok, WIDE),) * 2,
+        in_specs=[anywhere] * 2,
+        out_specs=(VMEM,) * 2,
+        scratch_shapes=[pltpu.SemaphoreType.DMA((heads,))],
+        compiler_params=pltpu.CompilerParams(vmem_limit_bytes=16 * 2**20),
+    )(query, kv)
     got = lax.ppermute(send, "xb", [(0, 1), (1, 0)])
     halves = (shaped(2, 2, tok, WIDE),) * 2
     keep, send = call(second_kernel, halves, [VMEM] * 2, keep, got)
@@ -233,30 +258,7 @@
     got = lax.ppermute(send, "zc", [(z, z ^ 2) for z in range(4)])
     served = call(last_kernel, shaped(heads, tok, WIDE), [VMEM] * 2, keep, got)
 
-    pairs = pl.pallas_call(
-        pair_kernel,
-        out_shape=shaped(heads // 2, tok, 4 * HEAD_DIM),
-        in_specs=[anywhere] * 2,
-        out_specs=VMEM,
-        scratch_shapes=[pltpu.VMEM((tok, width), jnp.bfloat16)] * 2 + [pltpu.SemaphoreType.DMA((2,))],
-        compiler_params=pltpu.CompilerParams(vmem_limit_bytes=40 * 2**20),
-    )(key, value)
-
-    swapped = lax.ppermute(sent, "core", [(0, 1), (1, 0)])
-    picked = jnp.where(completing[0] % 2 == lax.axis_index("core"), mine, swapped)
-    handed = lax.ppermute(
-        picked, ("half",) + z_all, [(z, depth + (z + depth // 2) % depth) for z in range(depth)]
-    )
-
-    kv = call(
-        pack_keys_kernel,
-        shaped(depth, tok, 6 * HEAD_DIM),
-        [SMEM] + [VMEM] * 3,
-        completing,
-        pairs,
-        picked,
-        handed,
-    )
+
     kv = lax.all_to_all(kv, z_all, 0, 0, tiled=True)
     kv = call(spread_kernel, shaped(plane, depth * tok, 3 * HEAD_DIM), [VMEM, anywhere], kv, after_first)
     kv = lax.all_to_all(kv, plane_axes, 0, 0, tiled=True)
@@ -271,6 +273,7 @@
         served,
         kv,
         cost=estimate(rows, n),
+        mib=40,
     )
     out = call(
         functools.partial(far_kernel, 3),
@@ -284,6 +287,7 @@
         sums,
         largest,
         cost=estimate(rows, n),
+        mib=40,
     )
     out = lax.all_to_all(out, served_by, 0, 0, tiled=True)
     return jnp.transpose(out, (1, 0, 2)).reshape(1, tok, HEADS * HEAD_DIM)

time: 89.2 us -> 85.7 us (0.961)
  Pallas kernels: 8.43 us -> 5.04 us
  other arithmetic: 0.01 us -> 1.53 us
  starting transfers between devices: 45.7 us -> 44.3 us
    ppermute x1, starting transfers between devices: 7.08 us -> 5 us  [shards(): lax.ppermute(picked, ('half',) + z_all, [(z, depth + (z + depth // 2) % d...]
    pallas_call x8, Pallas kernels: 6.69 us -> 4.74 us  [call(): pl.pallas_call(kernel, out_shape=out_shape, in_specs=specs, out_specs=out...]
    select_n x1 -> x2, other arithmetic: 0.01 us -> 1.53 us  [the longest x1 0.77 us: shards(): picked = jnp.where(completing[0] % 2 == core, mine, swapped)]
    pallas_call x2, Pallas kernels: 1.74 us -> 0.29 us  [the longest x1 0.2 us: shards(): pl.pallas_call(stage_kernel, out_shape=(shaped(part, tok, WIDE),) * 2, in...]
    ppermute x1 -> x2, starting transfers between devices: 8.79 us -> 9.44 us  [the longest x1 8.78 us: shards(): swapped = lax.ppermute(sent, ('half', 'core'), [(0, 1), (1, 0)])]
  transfers between devices with their start and end apart: 8 -> 9, of which waited for: 6 -> 6; matrix products, arithmetic and copies ran while one was open for 0% -> 0% of each run, Pallas kernels for 2% -> 3%
where the time goes in v5:
time: 85.7 us; the launch traced here: 84.9 us
  starting transfers between devices  44.3 us (52%)
  waiting for transfers between devices  19.4 us (23%)
  blocking collectives  10.6 us (12%)
  Pallas kernels  5.04 us (6%)
  local copies, waits for them, and re-layouts  3.27 us (4%)
  other arithmetic  1.53 us (2%)
    all_to_all x1, blocking collectives, shards(): out = lax.all_to_all(out, served_by, 0, 0, tiled=True)  10.6 us
    ppermute x1, starting transfers between devices, shards(): swapped = lax.ppermute(sent, ('half', 'core'), [(0, 1), (1, 0)])  8.78 us
    ppermute x1, starting transfers between devices, shards(): other = lax.ppermute(clean, 'core', [(0, 1), (1, 0)])  7.59 us
    all_to_all x1, starting transfers between devices, shards(): kv = lax.all_to_all(kv, plane_axes, 0, 0, tiled=True)  6.75 us
    all_to_all x1, starting transfers between devices, shards(): kv = lax.all_to_all(kv, z_all, 0, 0, tiled=True)  5.91 us
    all_to_all x1, waiting for transfers between devices, shards(): kv = lax.all_to_all(kv, plane_axes, 0, 0, tiled=True)  5.84 us
    ppermute x1, starting transfers between devices, shards(): lax.ppermute(picked, ('half',) + z_all, [(z, depth + (z + depth // 2) % d...  5 us
    pallas_call x8, Pallas kernels, call(): pl.pallas_call(kernel, out_shape=out_shape, in_specs=specs, out_specs=out...  4.74 us
  transfers between devices with their start and end apart: 9, of which 6 were waited for; matrix products, arithmetic and copies ran while one was open for 0% of the time, Pallas kernels for 3%

profile of v5, /device:TPU:1, one launch (start us, length us, event | category | flops | bytes accessed | tf_op | source)
XLA Modules:
  0.0 84.9 jit_solution(2385869565236488040)
XLA Ops:
  0.0 0.8 select_bitcast_fusion.sent_ref
  0.8 8.8 %collective-permute-start = (bf16[16,1024]{1,0:T(8,128)(2,1)S(1)}, bf16[16,1024]{1,0:T(8,128)(2,1)S(1)}, u32[]{:S(2)}, u32[]{:S(2)}) collective-permute-start(bf16[16,1024]{1,0:T(8,128)(2,1)S(1)} %select_bitcast_fusion.sent_ref), channel_id=1, source_target_pairs={{0,128},{128,0},{1,129},{129,1},{2,130},{130,2},{3,131},{131,3},{4... | collective-permute-start | bytes 98312 | tf_op jit(solution)/shard_map/ppermute | solution.py:218
  10.2 0.2 collective-permute-done
  10.4 0.8 bitcast_select_fusion.after_ref.picked_ref
  11.2 5.0 %collective-permute-start.2 = (bf16[16,1024]{1,0:T(8,128)(2,1)S(1)}, bf16[16,1024]{1,0:T(8,128)(2,1)S(1)}, u32[]{:S(2)}, u32[]{:S(2)}) collective-permute-start(bf16[16,1024]{1,0:T(8,128)(2,1)S(1)} %bitcast_select_fusion.after_ref.picked_ref), channel_id=1, source_target_pairs={{0,320},{16,336},{32,352},{48,368},{64,256},{80,272},{96,288},{112... | collective-permute-start | bytes 98312 | tf_op jit(solution)/shard_map/ppermute | solution.py:220
  16.2 0.0 copy-start.1
  16.2 0.7 copy-done.1
  16.9 0.8 copy-done.2
  17.7 0.1 shard_map.73
  17.8 0.7 collective-permute-start.1
  18.5 0.7 shard_map.74.after_ref
  19.2 5.9 %all-to-all-start = ((bf16[8,16,768]{2,1,0:T(8,128)(2,1)}), bf16[8,16,768]{2,1,0:T(8,128)(2,1)S(1)}, u32[]{:S(2)}, u32[]{:S(2)}) async-start(bf16[8,16,768]{2,1,0:T(8,128)(2,1)} %shard_map.74.after_ref), calls=%async_computation | async-start | bytes 393216 | tf_op jit(solution)/shard_map/all_to_all | solution.py:262
  25.1 0.9 %copy-done = bf16[1,16,6144]{2,1,0:T(8,128)(2,1)S(1)} copy-done((bf16[1,16,6144]{2,1,0:T(8,128)(2,1)S(1)}, bf16[1,16,6144]{2,1,0:T(8,128)(2,1)}, u32[]{:S(2)}) %copy-start) | copy-done | bytes 196632
  26.0 0.2 shard_map.75
  26.2 3.1 %collective-permute-start.3 = (bf16[4,16,768]{2,1,0:T(8,128)(2,1)S(1)}, bf16[4,16,768]{2,1,0:T(8,128)(2,1)S(1)}, u32[]{:S(2)}, u32[]{:S(2)}) collective-permute-start(bf16[4,16,768]{2,1,0:T(8,128)(2,1)S(1)} %get-tuple-element.18), channel_id=1, source_target_pairs={{0,4},{4,0},{1,5},{5,1},{2,6},{6,2},{3,7},{7,3},{8,12},{12,8},{9,1... | collective-permute-start | bytes 294920 | tf_op jit(solution)/shard_map/ppermute | solution.py:252
  29.4 2.2 %collective-permute-done.3.got_ref = bf16[4,16,768]{2,1,0:T(8,128)(2,1)S(1)} collective-permute-done((bf16[4,16,768]{2,1,0:T(8,128)(2,1)S(1)}, bf16[4,16,768]{2,1,0:T(8,128)(2,1)S(1)}, u32[]{:S(2)}, u32[]{:S(2)}) %collective-permute-start.3) | collective-permute-done | bytes 98336 | tf_op jit(solution)/shard_map/ppermute | solution.py:252
  31.6 4.5 %all-to-all-done.served_ref = bf16[8,16,768]{2,1,0:T(8,128)(2,1)S(1)} async-done(((bf16[8,16,768]{2,1,0:T(8,128)(2,1)}), bf16[8,16,768]{2,1,0:T(8,128)(2,1)S(1)}, u32[]{:S(2)}, u32[]{:S(2)}) %all-to-all-start) | async-done | bytes 196640 | tf_op jit(solution)/shard_map/all_to_all | solution.py:262
  36.1 1.3 %shard_map.79 = bf16[16,128,384]{2,1,0:T(8,128)(2,1)} custom-call(bf16[8,16,768]{2,1,0:T(8,128)(2,1)S(1)} %all-to-all-done.served_ref, bf16[2,2,16,768]{3,2,1,0:T(8,128)(2,1)S(1)} %get-tuple-element.19.kept_ref.after_ref), custom_call_target="tpu_custom_call" | custom-call | tf_op jit(solution)/shard_map/pallas_call | solution.py:193
  37.4 6.8 %all-to-all-start.1 = ((bf16[16,128,384]{2,1,0:T(8,128)(2,1)}), bf16[16,128,384]{2,1,0:T(8,128)(2,1)S(1)}, u32[]{:S(2)}, u32[]{:S(2)}) async-start(bf16[16,128,384]{2,1,0:T(8,128)(2,1)} %shard_map.79), calls=%async_computation.1 | async-start | bytes 3145728 | tf_op jit(solution)/shard_map/all_to_all | solution.py:264
  44.2 1.9 %collective-permute-start.4 = (bf16[2,2,16,768]{3,2,1,0:T(8,128)(2,1)S(1)}, bf16[2,2,16,768]{3,2,1,0:T(8,128)(2,1)S(1)}, u32[]{:S(2)}, u32[]{:S(2)}) collective-permute-start(bf16[2,2,16,768]{3,2,1,0:T(8,128)(2,1)S(1)} %get-tuple-element.20), channel_id=1, source_target_pairs={{0,16},{16,0},{32,48},{48,32},{1,17},{17,1},{33,49},{49,33},{2,18}... | collective-permute-start | bytes 294920 | tf_op jit(solution)/shard_map/ppermute | solution.py:256
  46.1 3.4 %collective-permute-done.4.got_ref = bf16[2,2,16,768]{3,2,1,0:T(8,128)(2,1)S(1)} collective-permute-done((bf16[2,2,16,768]{3,2,1,0:T(8,128)(2,1)S(1)}, bf16[2,2,16,768]{3,2,1,0:T(8,128)(2,1)S(1)}, u32[]{:S(2)}, u32[]{:S(2)}) %collective-permute-start.4) | collective-permute-done | bytes 98336 | tf_op jit(solution)/shard_map/ppermute | solution.py:256
  49.6 4.6 %collective-permute-start.5 = (bf16[2,2,16,768]{3,2,1,0:T(8,128)(2,1)S(1)}, bf16[2,2,16,768]{3,2,1,0:T(8,128)(2,1)S(1)}, u32[]{:S(2)}, u32[]{:S(2)}) collective-permute-start(bf16[2,2,16,768]{3,2,1,0:T(8,128)(2,1)S(1)} %get-tuple-element.22), channel_id=1, source_target_pairs={{0,32},{16,48},{32,0},{48,16},{1,33},{17,49},{33,1},{49,17},{2,34}... | collective-permute-start | bytes 294920 | tf_op jit(solution)/shard_map/ppermute | solution.py:258
  54.1 3.2 %collective-permute-done.5.got_ref = bf16[2,2,16,768]{3,2,1,0:T(8,128)(2,1)S(1)} collective-permute-done((bf16[2,2,16,768]{3,2,1,0:T(8,128)(2,1)S(1)}, bf16[2,2,16,768]{3,2,1,0:T(8,128)(2,1)S(1)}, u32[]{:S(2)}, u32[]{:S(2)}) %collective-permute-start.5) | collective-permute-done | bytes 98336 | tf_op jit(solution)/shard_map/ppermute | solution.py:258
  57.3 5.8 %all-to-all-done.1.kv_ref = bf16[16,128,384]{2,1,0:T(8,128)(2,1)S(1)} async-done(((bf16[16,128,384]{2,1,0:T(8,128)(2,1)}), bf16[16,128,384]{2,1,0:T(8,128)(2,1)S(1)}, u32[]{:S(2)}, u32[]{:S(2)}) %all-to-all-start.1) | async-done | bytes 1572896 | tf_op jit(solution)/shard_map/all_to_all | solution.py:264
  63.2 0.1 shard_map.80
  63.3 0.0 copy-start.3
  63.3 7.6 %collective-permute-start.6 = (bf16[16,128,128]{2,1,0:T(8,128)(2,1)S(1)}, bf16[16,128,128]{2,1,0:T(8,128)(2,1)S(1)}, u32[]{:S(2)}, u32[]{:S(2)}) collective-permute-start(bf16[16,128,128]{2,1,0:T(8,128)(2,1)S(1)} %shard_map.80), channel_id=1, source_target_pairs={{0,128},{128,0},{1,129},{129,1},{2,130},{130,2},{3,131},{131,3},{4... | collective-permute-start | bytes 1572872 | tf_op jit(solution)/shard_map/ppermute | solution.py:266
  70.9 1.9 %shard_map.81 = (f32[768,256]{1,0:T(8,128)S(1)}, f32[768,128]{1,0:T(8,128)S(1)}) custom-call(bf16[8,16,768]{2,1,0:T(8,128)(2,1)S(1)} %shard_map.78.after_ref.q_ref, bf16[16,128,384]{2,1,0:T(8,128)(2,1)S(1)} %all-to-all-done.1.kv_ref), custom_call_target="tpu_custom_call" | custom-call | flops 805306368 | bytes 4194304 | tf_op jit(solution)/shard_map/pallas_call | solution.py:193
  72.8 0.6 shard_map.82
  73.5 10.6 %all_to_all.15 = bf16[8,16,768]{2,1,0:T(8,128)(2,1)S(1)} all-to-all(bf16[8,16,768]{2,1,0:T(8,128)(2,1)S(1)} %shard_map.82), channel_id=1, replica_groups=mesh['half'=2,'core'=2,'zq'=2,'zc'=4,'xa'=2,'xb'=2,'y'=4] {'zc','xb'}, dimensions={0} | all-to-all | bytes 393216 | tf_op jit(solution)/shard_map/all_to_all | solution.py:292
  84.1 0.1 copy.8
  84.2 0.8 reshape.7
  (9 shorter events, 0.1 us)
Async XLA Ops:
  0.8 9.6 %collective-permute-start = (bf16[16,1024]{1,0:T(8,128)(2,1)S(1)}, bf16[16,1024]{1,0:T(8,128)(2,1)S(1)}, u32[]{:S(2)}, u32[]{:S(2)}) collective-permute-start(bf16[16,1024]{1,0:T(8,128)(2,1)S(1)} %select_bitcast_fusion.sent_ref), channel_id=1, source_target_pairs={{0,128},{128,0},{1,129},{129,1},{2,130},{130,2},{3,131},{131,3},{4... | collective-permute-start | bytes 98312 | tf_op jit(solution)/shard_map/ppermute | solution.py:218
  11.2 7.3 %collective-permute-start.2 = (bf16[16,1024]{1,0:T(8,128)(2,1)S(1)}, bf16[16,1024]{1,0:T(8,128)(2,1)S(1)}, u32[]{:S(2)}, u32[]{:S(2)}) collective-permute-start(bf16[16,1024]{1,0:T(8,128)(2,1)S(1)} %bitcast_select_fusion.after_ref.picked_ref), channel_id=1, source_target_pairs={{0,320},{16,336},{32,352},{48,368},{64,256},{80,272},{96,288},{112... | collective-permute-start | bytes 98312 | tf_op jit(solution)/shard_map/ppermute | solution.py:220
  16.2 0.8 copy-start.1
  16.9 0.8 copy-start.2
  17.8 0.7 collective-permute-start.1
  19.2 16.9 %all-to-all-start = ((bf16[8,16,768]{2,1,0:T(8,128)(2,1)}), bf16[8,16,768]{2,1,0:T(8,128)(2,1)S(1)}, u32[]{:S(2)}, u32[]{:S(2)}) async-start(bf16[8,16,768]{2,1,0:T(8,128)(2,1)} %shard_map.74.after_ref), calls=%async_computation | async-start | bytes 393216 | tf_op jit(solution)/shard_map/all_to_all | solution.py:262
  25.1 0.9 %copy-start = (bf16[1,16,6144]{2,1,0:T(8,128)(2,1)S(1)}, bf16[1,16,6144]{2,1,0:T(8,128)(2,1)}, u32[]{:S(2)}) copy-start(bf16[1,16,6144]{2,1,0:T(8,128)(2,1)} %query_ref.1) | copy-start | bytes 589828
  26.2 5.4 %collective-permute-start.3 = (bf16[4,16,768]{2,1,0:T(8,128)(2,1)S(1)}, bf16[4,16,768]{2,1,0:T(8,128)(2,1)S(1)}, u32[]{:S(2)}, u32[]{:S(2)}) collective-permute-start(bf16[4,16,768]{2,1,0:T(8,128)(2,1)S(1)} %get-tuple-element.18), channel_id=1, source_target_pairs={{0,4},{4,0},{1,5},{5,1},{2,6},{6,2},{3,7},{7,3},{8,12},{12,8},{9,1... | collective-permute-start | bytes 294920 | tf_op jit(solution)/shard_map/ppermute | solution.py:252
  37.4 25.8 %all-to-all-start.1 = ((bf16[16,128,384]{2,1,0:T(8,128)(2,1)}), bf16[16,128,384]{2,1,0:T(8,128)(2,1)S(1)}, u32[]{:S(2)}, u32[]{:S(2)}) async-start(bf16[16,128,384]{2,1,0:T(8,128)(2,1)} %shard_map.79), calls=%async_computation.1 | async-start | bytes 3145728 | tf_op jit(solution)/shard_map/all_to_all | solution.py:264
  44.2 5.4 %collective-permute-start.4 = (bf16[2,2,16,768]{3,2,1,0:T(8,128)(2,1)S(1)}, bf16[2,2,16,768]{3,2,1,0:T(8,128)(2,1)S(1)}, u32[]{:S(2)}, u32[]{:S(2)}) collective-permute-start(bf16[2,2,16,768]{3,2,1,0:T(8,128)(2,1)S(1)} %get-tuple-element.20), channel_id=1, source_target_pairs={{0,16},{16,0},{32,48},{48,32},{1,17},{17,1},{33,49},{49,33},{2,18}... | collective-permute-start | bytes 294920 | tf_op jit(solution)/shard_map/ppermute | solution.py:256
  49.6 7.8 %collective-permute-start.5 = (bf16[2,2,16,768]{3,2,1,0:T(8,128)(2,1)S(1)}, bf16[2,2,16,768]{3,2,1,0:T(8,128)(2,1)S(1)}, u32[]{:S(2)}, u32[]{:S(2)}) collective-permute-start(bf16[2,2,16,768]{3,2,1,0:T(8,128)(2,1)S(1)} %get-tuple-element.22), channel_id=1, source_target_pairs={{0,32},{16,48},{32,0},{48,16},{1,33},{17,49},{33,1},{49,17},{2,34}... | collective-permute-start | bytes 294920 | tf_op jit(solution)/shard_map/ppermute | solution.py:258
  63.3 9.6 %copy-start.3 = (s32[4,4]{1,0:T(4,128)S(1)}, s32[4,4]{1,0:T(4,128)}, u32[]{:S(2)}) copy-start(s32[4,4]{1,0:T(4,128)} %mask_ref.1) | copy-start | bytes 196
  63.3 9.5 %collective-permute-start.6 = (bf16[16,128,128]{2,1,0:T(8,128)(2,1)S(1)}, bf16[16,128,128]{2,1,0:T(8,128)(2,1)S(1)}, u32[]{:S(2)}, u32[]{:S(2)}) collective-permute-start(bf16[16,128,128]{2,1,0:T(8,128)(2,1)S(1)} %shard_map.80), channel_id=1, source_target_pairs={{0,128},{128,0},{1,129},{129,1},{2,130},{130,2},{3,131},{131,3},{4... | collective-permute-start | bytes 1572872 | tf_op jit(solution)/shard_map/ppermute | solution.py:266

commit v6 on v5

--- a/solution.py
+++ b/solution.py
@@ -122,7 +122,8 @@
             send_ref[x, high] = source[2 * high + 1 - low]
 
 
-def third_kernel(kept_ref, got_ref, keep_ref, send_ref):
+def third_kernel(completing_ref, kept_ref, got_ref, keep_ref, send_ref):
+    del completing_ref
     zc = lax.axis_index("zc")
     low, high = lax.rem(zc, 2), lax.div(zc, 2)
     for source, z in ((kept_ref, low), (got_ref, 1 - low)):
@@ -139,27 +140,24 @@
                 out_ref[4 * z + 2 * low + x] = source[low, x]
 
 
-def pair_kernel(key_ref, value_ref, sent_ref, after_ref, out_ref, late_ref, key_buf, value_buf, sems):
+def pair_kernel(near_ref, sent_ref, after_ref, out_ref, late_ref):
     del after_ref
     late_ref[...] = sent_ref[...]
-    copies = [
-        pltpu.make_async_copy(key_ref.at[0], key_buf, sems.at[0]),
-        pltpu.make_async_copy(value_ref.at[0], value_buf, sems.at[1]),
-    ]
-    for copy in copies:
-        copy.start()
-    for copy in copies:
-        copy.wait()
     for h in range(KV_HEADS):
         at = slice(h * HEAD_DIM, (h + 1) * HEAD_DIM)
         first = (h % 2) * 2 * HEAD_DIM
-        out_ref[h // 2, :, first : first + HEAD_DIM] = key_buf[:, at]
-        out_ref[h // 2, :, first + HEAD_DIM : first + 2 * HEAD_DIM] = value_buf[:, at]
+        for i in range(2):
+            out_ref[h // 2, :, first + i * HEAD_DIM : first + (i + 1) * HEAD_DIM] = near_ref[i, :, at]
+
+
+def pick_kernel(completing_ref, mine_ref, swapped_ref, out_ref):
+    other = lax.bitwise_and(completing_ref[...], 1) != lax.axis_index("core")
+    out_ref[...] = jnp.where(jnp.broadcast_to(other, out_ref.shape), swapped_ref[...], mine_ref[...])
 
 
 def pack_keys_kernel(completing_ref, pairs_ref, picked_ref, late_ref, handed_ref, out_ref):
     upper = lax.axis_index("half") == 1
-    handed = jnp.logical_and(upper, completing_ref[0] < 2)
+    handed = jnp.broadcast_to(jnp.where(upper, completing_ref[...], 2) < 2, handed_ref.shape)
     late = jnp.logical_and(upper, lax.axis_index("core") == 1)
     clean = jnp.where(handed, handed_ref[...], jnp.where(late, late_ref[...], picked_ref[...]))
     for h in range(KV_HEADS):
@@ -214,27 +212,29 @@
     width = heads * HEAD_DIM
     core = lax.axis_index("core")
     mine = jnp.where(core == 0, clean_key[0], clean_value[0])
+    near = jnp.stack([key[0], value[0]])
     sent = jnp.where(core == 0, clean_value[0], clean_key[0])
     swapped = lax.ppermute(sent, ("half", "core"), [(0, 1), (1, 0)])
-    picked = jnp.where(completing[0] % 2 == core, mine, swapped)
+    finished = completing.reshape(1, 1)
+    picked = call(pick_kernel, shaped(tok, width), [VMEM] * 3, finished, mine, swapped)
     handed = lax.ppermute(
         picked, ("half",) + z_all, [(z, depth + (z + depth // 2) % depth) for z in range(depth)]
     )
-    pairs, late = pl.pallas_call(
+    pairs, late = call(
         pair_kernel,
-        out_shape=(shaped(heads // 2, tok, 4 * HEAD_DIM), shaped(tok, width)),
-        in_specs=[anywhere] * 2 + [VMEM, anywhere],
-        out_specs=(VMEM,) * 2,
-        scratch_shapes=[pltpu.VMEM((tok, width), jnp.bfloat16)] * 2 + [pltpu.SemaphoreType.DMA((2,))],
-        compiler_params=pltpu.CompilerParams(vmem_limit_bytes=16 * 2**20),
-    )(key, value, sent, picked)
+        (shaped(heads // 2, tok, 4 * HEAD_DIM), shaped(tok, width)),
+        [VMEM] * 2 + [anywhere],
+        near,
+        sent,
+        picked,
+    )
     late = lax.ppermute(late, ("half", "core"), [(2, 3)])
 
     kv = call(
         pack_keys_kernel,
         shaped(depth, tok, 6 * HEAD_DIM),
-        [SMEM] + [VMEM] * 4,
-        completing,
+        [VMEM] * 5,
+        finished,
         pairs,
         picked,
         late,
@@ -254,7 +254,7 @@
     keep, send = call(second_kernel, halves, [VMEM] * 2, keep, got)
     after_first = keep
     got = lax.ppermute(send, "zc", [(z, z ^ 1) for z in range(4)])
-    keep, send = call(third_kernel, halves, [VMEM] * 2, keep, got)
+    keep, send = call(third_kernel, halves, [SMEM] + [VMEM] * 2, completing, keep, got)
     got = lax.ppermute(send, "zc", [(z, z ^ 2) for z in range(4)])
     served = call(last_kernel, shaped(heads, tok, WIDE), [VMEM] * 2, keep, got)
 

time: 85.7 us -> 84.9 us (level)
  Pallas kernels: 5.04 us -> 7.05 us
  waiting for transfers between devices: 19.4 us -> 21.2 us
  local copies, waits for them, and re-layouts: 3.27 us -> 1.76 us
  starting transfers between devices: 44.3 us -> 42.8 us
  blocking collectives: 10.6 us -> 9.14 us
    pallas_call x8 -> x10, Pallas kernels: 4.74 us -> 6.85 us  [call(): pl.pallas_call(kernel, out_shape=out_shape, in_specs=specs, out_specs=out...]
    ppermute x1, starting transfers between devices: 4.56 us -> 2.81 us  [shards(): got = lax.ppermute(send, 'zc', [(z, z ^ 2) for z in range(4)])]
    unnamed x8 -> x4, local copies, waits for them, and re-layouts: 2.44 us -> 0.93 us
    ppermute x1, waiting for transfers between devices: 3.19 us -> 4.65 us  [shards(): got = lax.ppermute(send, 'zc', [(z, z ^ 2) for z in range(4)])]
    all_to_all x1, blocking collectives: 10.6 us -> 9.14 us  [shards(): out = lax.all_to_all(out, served_by, 0, 0, tiled=True)]
  transfers between devices with their start and end apart: 9 -> 9, of which waited for: 6 -> 6; matrix products, arithmetic and copies ran while one was open for 0% -> 1% of each run, Pallas kernels for 3% -> 3%
where the time goes in v6:
time: 84.9 us; the launch traced here: 84.3 us
  starting transfers between devices  42.8 us (50%)
  waiting for transfers between devices  21.2 us (25%)
  blocking collectives  9.14 us (11%)
  Pallas kernels  7.05 us (8%)
  local copies, waits for them, and re-layouts  1.76 us (2%)
  other arithmetic  1.57 us (2%)
    all_to_all x1, blocking collectives, shards(): out = lax.all_to_all(out, served_by, 0, 0, tiled=True)  9.14 us
    ppermute x1, starting transfers between devices, shards(): swapped = lax.ppermute(sent, ('half', 'core'), [(0, 1), (1, 0)])  8.78 us
    ppermute x1, starting transfers between devices, shards(): other = lax.ppermute(clean, 'core', [(0, 1), (1, 0)])  7.66 us
    pallas_call x10, Pallas kernels, call(): pl.pallas_call(kernel, out_shape=out_shape, in_specs=specs, out_specs=out...  6.85 us
    all_to_all x1, starting transfers between devices, shards(): kv = lax.all_to_all(kv, plane_axes, 0, 0, tiled=True)  6.75 us
    all_to_all x1, waiting for transfers between devices, shards(): kv = lax.all_to_all(kv, plane_axes, 0, 0, tiled=True)  6.1 us
    all_to_all x1, starting transfers between devices, shards(): kv = lax.all_to_all(kv, z_all, 0, 0, tiled=True)  5.91 us
    ppermute x1, starting transfers between devices, shards(): lax.ppermute(picked, ('half',) + z_all, [(z, depth + (z + depth // 2) % d...  5.15 us
  transfers between devices with their start and end apart: 9, of which 6 were waited for; matrix products, arithmetic and copies ran while one was open for 1% of the time, Pallas kernels for 3%

profile of v6, /device:TPU:1, one launch (start us, length us, event | category | flops | bytes accessed | tf_op | source)
XLA Modules:
  0.0 84.3 jit_solution(13478622537839946209)
XLA Ops:
  0.0 0.8 select_bitcast_fusion
  0.8 8.8 %collective-permute-start = (bf16[16,1024]{1,0:T(8,128)(2,1)S(1)}, bf16[16,1024]{1,0:T(8,128)(2,1)S(1)}, u32[]{:S(2)}, u32[]{:S(2)}) collective-permute-start(bf16[16,1024]{1,0:T(8,128)(2,1)S(1)} %get-tuple-element.26.sent_ref), channel_id=1, source_target_pairs={{0,128},{128,0},{1,129},{129,1},{2,130},{130,2},{3,131},{131,3},{4... | collective-permute-start | bytes 98312 | tf_op jit(solution)/shard_map/ppermute | solution.py:217
  9.6 0.8 pad_maximum_fusion.near_ref
  11.0 0.0 collective-permute-done.swapped_ref
  11.0 0.1 shard_map.73.after_ref.picked_ref
  11.1 5.1 %collective-permute-start.2 = (bf16[16,1024]{1,0:T(8,128)(2,1)S(1)}, bf16[16,1024]{1,0:T(8,128)(2,1)S(1)}, u32[]{:S(2)}, u32[]{:S(2)}) collective-permute-start(bf16[16,1024]{1,0:T(8,128)(2,1)S(1)} %shard_map.73.after_ref.picked_ref), channel_id=1, source_target_pairs={{0,320},{16,336},{32,352},{48,368},{64,256},{80,272},{96,288},{112... | collective-permute-start | bytes 98312 | tf_op jit(solution)/shard_map/ppermute | solution.py:220
  16.3 0.7 collective-permute-start.1
  17.0 0.3 collective-permute-done.2.handed_ref
  17.3 0.0 collective-permute-done.1.late_ref
  17.3 0.8 shard_map.75.after_ref
  18.0 5.9 %all-to-all-start = ((bf16[8,16,768]{2,1,0:T(8,128)(2,1)}), bf16[8,16,768]{2,1,0:T(8,128)(2,1)S(1)}, u32[]{:S(2)}, u32[]{:S(2)}) async-start(bf16[8,16,768]{2,1,0:T(8,128)(2,1)} %shard_map.75.after_ref), calls=%async_computation | async-start | bytes 393216 | tf_op jit(solution)/shard_map/all_to_all | solution.py:262
  24.0 0.9 %copy-done = bf16[1,16,6144]{2,1,0:T(8,128)(2,1)S(1)} copy-done((bf16[1,16,6144]{2,1,0:T(8,128)(2,1)S(1)}, bf16[1,16,6144]{2,1,0:T(8,128)(2,1)}, u32[]{:S(2)}) %copy-start) | copy-done | bytes 196632
  24.9 0.2 shard_map.76
  25.1 3.1 %collective-permute-start.3 = (bf16[4,16,768]{2,1,0:T(8,128)(2,1)S(1)}, bf16[4,16,768]{2,1,0:T(8,128)(2,1)S(1)}, u32[]{:S(2)}, u32[]{:S(2)}) collective-permute-start(bf16[4,16,768]{2,1,0:T(8,128)(2,1)S(1)} %get-tuple-element.18), channel_id=1, source_target_pairs={{0,4},{4,0},{1,5},{5,1},{2,6},{6,2},{3,7},{7,3},{8,12},{12,8},{9,1... | collective-permute-start | bytes 294920 | tf_op jit(solution)/shard_map/ppermute | solution.py:252
  28.2 2.2 %collective-permute-done.3.got_ref = bf16[4,16,768]{2,1,0:T(8,128)(2,1)S(1)} collective-permute-done((bf16[4,16,768]{2,1,0:T(8,128)(2,1)S(1)}, bf16[4,16,768]{2,1,0:T(8,128)(2,1)S(1)}, u32[]{:S(2)}, u32[]{:S(2)}) %collective-permute-start.3) | collective-permute-done | bytes 98336 | tf_op jit(solution)/shard_map/ppermute | solution.py:252
  30.5 4.5 %all-to-all-done.served_ref = bf16[8,16,768]{2,1,0:T(8,128)(2,1)S(1)} async-done(((bf16[8,16,768]{2,1,0:T(8,128)(2,1)}), bf16[8,16,768]{2,1,0:T(8,128)(2,1)S(1)}, u32[]{:S(2)}, u32[]{:S(2)}) %all-to-all-start) | async-done | bytes 196640 | tf_op jit(solution)/shard_map/all_to_all | solution.py:262
  34.9 1.3 %shard_map.80 = bf16[16,128,384]{2,1,0:T(8,128)(2,1)} custom-call(bf16[8,16,768]{2,1,0:T(8,128)(2,1)S(1)} %all-to-all-done.served_ref, bf16[2,2,16,768]{3,2,1,0:T(8,128)(2,1)S(1)} %get-tuple-element.19.kept_ref.after_ref), custom_call_target="tpu_custom_call" | custom-call | tf_op jit(solution)/shard_map/pallas_call | solution.py:191
  36.2 6.8 %all-to-all-start.1 = ((bf16[16,128,384]{2,1,0:T(8,128)(2,1)}), bf16[16,128,384]{2,1,0:T(8,128)(2,1)S(1)}, u32[]{:S(2)}, u32[]{:S(2)}) async-start(bf16[16,128,384]{2,1,0:T(8,128)(2,1)} %shard_map.80), calls=%async_computation.1 | async-start | bytes 3145728 | tf_op jit(solution)/shard_map/all_to_all | solution.py:264
  43.0 1.9 %collective-permute-start.4 = (bf16[2,2,16,768]{3,2,1,0:T(8,128)(2,1)S(1)}, bf16[2,2,16,768]{3,2,1,0:T(8,128)(2,1)S(1)}, u32[]{:S(2)}, u32[]{:S(2)}) collective-permute-start(bf16[2,2,16,768]{3,2,1,0:T(8,128)(2,1)S(1)} %get-tuple-element.20), channel_id=1, source_target_pairs={{0,16},{16,0},{32,48},{48,32},{1,17},{17,1},{33,49},{49,33},{2,18}... | collective-permute-start | bytes 294920 | tf_op jit(solution)/shard_map/ppermute | solution.py:256
  44.9 3.4 %collective-permute-done.4.got_ref = bf16[2,2,16,768]{3,2,1,0:T(8,128)(2,1)S(1)} collective-permute-done((bf16[2,2,16,768]{3,2,1,0:T(8,128)(2,1)S(1)}, bf16[2,2,16,768]{3,2,1,0:T(8,128)(2,1)S(1)}, u32[]{:S(2)}, u32[]{:S(2)}) %collective-permute-start.4) | collective-permute-done | bytes 98336 | tf_op jit(solution)/shard_map/ppermute | solution.py:256
  48.4 2.8 %collective-permute-start.5 = (bf16[2,2,16,768]{3,2,1,0:T(8,128)(2,1)S(1)}, bf16[2,2,16,768]{3,2,1,0:T(8,128)(2,1)S(1)}, u32[]{:S(2)}, u32[]{:S(2)}) collective-permute-start(bf16[2,2,16,768]{3,2,1,0:T(8,128)(2,1)S(1)} %get-tuple-element.22), channel_id=1, source_target_pairs={{0,32},{16,48},{32,0},{48,16},{1,33},{17,49},{33,1},{49,17},{2,34}... | collective-permute-start | bytes 294920 | tf_op jit(solution)/shard_map/ppermute | solution.py:258
  51.2 4.7 %collective-permute-done.5.got_ref = bf16[2,2,16,768]{3,2,1,0:T(8,128)(2,1)S(1)} collective-permute-done((bf16[2,2,16,768]{3,2,1,0:T(8,128)(2,1)S(1)}, bf16[2,2,16,768]{3,2,1,0:T(8,128)(2,1)S(1)}, u32[]{:S(2)}, u32[]{:S(2)}) %collective-permute-start.5) | collective-permute-done | bytes 98336 | tf_op jit(solution)/shard_map/ppermute | solution.py:258
  55.9 6.1 %all-to-all-done.1.kv_ref = bf16[16,128,384]{2,1,0:T(8,128)(2,1)S(1)} async-done(((bf16[16,128,384]{2,1,0:T(8,128)(2,1)}), bf16[16,128,384]{2,1,0:T(8,128)(2,1)S(1)}, u32[]{:S(2)}, u32[]{:S(2)}) %all-to-all-start.1) | async-done | bytes 1572896 | tf_op jit(solution)/shard_map/all_to_all | solution.py:264
  62.0 0.1 shard_map.81
  62.1 0.0 copy-start.1
  62.1 7.7 %collective-permute-start.6 = (bf16[16,128,128]{2,1,0:T(8,128)(2,1)S(1)}, bf16[16,128,128]{2,1,0:T(8,128)(2,1)S(1)}, u32[]{:S(2)}, u32[]{:S(2)}) collective-permute-start(bf16[16,128,128]{2,1,0:T(8,128)(2,1)S(1)} %shard_map.81), channel_id=1, source_target_pairs={{0,128},{128,0},{1,129},{129,1},{2,130},{130,2},{3,131},{131,3},{4... | collective-permute-start | bytes 1572872 | tf_op jit(solution)/shard_map/ppermute | solution.py:266
  69.7 1.9 %shard_map.82 = (f32[768,256]{1,0:T(8,128)S(1)}, f32[768,128]{1,0:T(8,128)S(1)}) custom-call(bf16[8,16,768]{2,1,0:T(8,128)(2,1)S(1)} %shard_map.79.after_ref.q_ref, bf16[16,128,384]{2,1,0:T(8,128)(2,1)S(1)} %all-to-all-done.1.kv_ref), custom_call_target="tpu_custom_call" | custom-call | flops 805306368 | bytes 4194304 | tf_op jit(solution)/shard_map/pallas_call | solution.py:191
  71.7 0.0 collective-permute-done.6.other_ref
  71.7 2.6 %shard_map.83 = bf16[8,16,768]{2,1,0:T(8,128)(2,1)S(1)} custom-call(s32[1]{0:T(128)} %copy.9.completing_ref, s32[4,4]{1,0:T(4,128)S(1)} %copy-done.1, bf16[8,16,768]{2,1,0:T(8,128)(2,1)S(1)} %shard_map.79.after_ref.q_ref, bf16[16,128,384]{2,1,0:T(8,128)(2,1)S(1)} %all-to-all-done.1.kv_ref, bf16[16,128,128]{2,1,0:T(8,128)(2,1)S(1)} %collective-permute-done.6.other_ref, ...), custom_call_target="tpu_custom_call" | custom-call | flops 805306368 | bytes 4194304 | tf_op jit(solution)/shard_map/pallas_call | solution.py:191
  74.3 9.1 %all_to_all.15 = bf16[8,16,768]{2,1,0:T(8,128)(2,1)S(1)} all-to-all(bf16[8,16,768]{2,1,0:T(8,128)(2,1)S(1)} %shard_map.83), channel_id=1, replica_groups=mesh['half'=2,'core'=2,'zq'=2,'zc'=4,'xa'=2,'xb'=2,'y'=4] {'zc','xb'}, dimensions={0} | all-to-all | bytes 393216 | tf_op jit(solution)/shard_map/all_to_all | solution.py:292
  83.5 0.1 copy.8
  83.5 0.8 reshape.11
  (6 shorter events, 0.1 us)
Async XLA Ops:
  0.8 10.2 %collective-permute-start = (bf16[16,1024]{1,0:T(8,128)(2,1)S(1)}, bf16[16,1024]{1,0:T(8,128)(2,1)S(1)}, u32[]{:S(2)}, u32[]{:S(2)}) collective-permute-start(bf16[16,1024]{1,0:T(8,128)(2,1)S(1)} %get-tuple-element.26.sent_ref), channel_id=1, source_target_pairs={{0,128},{128,0},{1,129},{129,1},{2,130},{130,2},{3,131},{131,3},{4... | collective-permute-start | bytes 98312 | tf_op jit(solution)/shard_map/ppermute | solution.py:217
  11.1 6.2 %collective-permute-start.2 = (bf16[16,1024]{1,0:T(8,128)(2,1)S(1)}, bf16[16,1024]{1,0:T(8,128)(2,1)S(1)}, u32[]{:S(2)}, u32[]{:S(2)}) collective-permute-start(bf16[16,1024]{1,0:T(8,128)(2,1)S(1)} %shard_map.73.after_ref.picked_ref), channel_id=1, source_target_pairs={{0,320},{16,336},{32,352},{48,368},{64,256},{80,272},{96,288},{112... | collective-permute-start | bytes 98312 | tf_op jit(solution)/shard_map/ppermute | solution.py:220
  16.3 1.0 %collective-permute-start.1 = (bf16[16,1024]{1,0:T(8,128)(2,1)S(1)}, bf16[16,1024]{1,0:T(8,128)(2,1)S(1)}, u32[]{:S(2)}, u32[]{:S(2)}) collective-permute-start(bf16[16,1024]{1,0:T(8,128)(2,1)S(1)} %get-tuple-element.16), channel_id=1, source_target_pairs={{256,384},{257,385},{258,386},{259,387},{260,388},{261,389},{262,3... | collective-permute-start | bytes 98312 | tf_op jit(solution)/shard_map/ppermute | solution.py:231
  18.0 16.9 %all-to-all-start = ((bf16[8,16,768]{2,1,0:T(8,128)(2,1)}), bf16[8,16,768]{2,1,0:T(8,128)(2,1)S(1)}, u32[]{:S(2)}, u32[]{:S(2)}) async-start(bf16[8,16,768]{2,1,0:T(8,128)(2,1)} %shard_map.75.after_ref), calls=%async_computation | async-start | bytes 393216 | tf_op jit(solution)/shard_map/all_to_all | solution.py:262
  23.9 0.9 %copy-start = (bf16[1,16,6144]{2,1,0:T(8,128)(2,1)S(1)}, bf16[1,16,6144]{2,1,0:T(8,128)(2,1)}, u32[]{:S(2)}) copy-start(bf16[1,16,6144]{2,1,0:T(8,128)(2,1)} %query_ref.1) | copy-start | bytes 589828
  25.1 5.4 %collective-permute-start.3 = (bf16[4,16,768]{2,1,0:T(8,128)(2,1)S(1)}, bf16[4,16,768]{2,1,0:T(8,128)(2,1)S(1)}, u32[]{:S(2)}, u32[]{:S(2)}) collective-permute-start(bf16[4,16,768]{2,1,0:T(8,128)(2,1)S(1)} %get-tuple-element.18), channel_id=1, source_target_pairs={{0,4},{4,0},{1,5},{5,1},{2,6},{6,2},{3,7},{7,3},{8,12},{12,8},{9,1... | collective-permute-start | bytes 294920 | tf_op jit(solution)/shard_map/ppermute | solution.py:252
  36.2 25.7 %all-to-all-start.1 = ((bf16[16,128,384]{2,1,0:T(8,128)(2,1)}), bf16[16,128,384]{2,1,0:T(8,128)(2,1)S(1)}, u32[]{:S(2)}, u32[]{:S(2)}) async-start(bf16[16,128,384]{2,1,0:T(8,128)(2,1)} %shard_map.80), calls=%async_computation.1 | async-start | bytes 3145728 | tf_op jit(solution)/shard_map/all_to_all | solution.py:264
  43.0 5.4 %collective-permute-start.4 = (bf16[2,2,16,768]{3,2,1,0:T(8,128)(2,1)S(1)}, bf16[2,2,16,768]{3,2,1,0:T(8,128)(2,1)S(1)}, u32[]{:S(2)}, u32[]{:S(2)}) collective-permute-start(bf16[2,2,16,768]{3,2,1,0:T(8,128)(2,1)S(1)} %get-tuple-element.20), channel_id=1, source_target_pairs={{0,16},{16,0},{32,48},{48,32},{1,17},{17,1},{33,49},{49,33},{2,18}... | collective-permute-start | bytes 294920 | tf_op jit(solution)/shard_map/ppermute | solution.py:256
  48.4 7.5 %collective-permute-start.5 = (bf16[2,2,16,768]{3,2,1,0:T(8,128)(2,1)S(1)}, bf16[2,2,16,768]{3,2,1,0:T(8,128)(2,1)S(1)}, u32[]{:S(2)}, u32[]{:S(2)}) collective-permute-start(bf16[2,2,16,768]{3,2,1,0:T(8,128)(2,1)S(1)} %get-tuple-element.22), channel_id=1, source_target_pairs={{0,32},{16,48},{32,0},{48,16},{1,33},{17,49},{33,1},{49,17},{2,34}... | collective-permute-start | bytes 294920 | tf_op jit(solution)/shard_map/ppermute | solution.py:258
  62.1 9.6 %copy-start.1 = (s32[4,4]{1,0:T(4,128)S(1)}, s32[4,4]{1,0:T(4,128)}, u32[]{:S(2)}) copy-start(s32[4,4]{1,0:T(4,128)} %mask_ref.1) | copy-start | bytes 196
  62.1 9.6 %collective-permute-start.6 = (bf16[16,128,128]{2,1,0:T(8,128)(2,1)S(1)}, bf16[16,128,128]{2,1,0:T(8,128)(2,1)S(1)}, u32[]{:S(2)}, u32[]{:S(2)}) collective-permute-start(bf16[16,128,128]{2,1,0:T(8,128)(2,1)S(1)} %shard_map.81), channel_id=1, source_target_pairs={{0,128},{128,0},{1,129},{129,1},{2,130},{130,2},{3,131},{131,3},{4... | collective-permute-start | bytes 1572872 | tf_op jit(solution)/shard_map/ppermute | solution.py:266

commit v7 on v6

--- a/solution.py
+++ b/solution.py
@@ -15,8 +15,10 @@
 GROUP = HEADS // KV_HEADS
 WIDE = GROUP * HEAD_DIM
 BASE = HEAD_DIM**-0.5 * math.log2(math.e)
+Z_ORDER = [3, 4, 5, 6, 7, 0, 1, 2]
+FIRST_ZC = 1
+SERVE_ORDER = [(i + 2 * FIRST_ZC) % 8 for i in range(8)]
 VMEM = pl.BlockSpec(memory_space=pltpu.VMEM)
-SMEM = pl.BlockSpec(memory_space=pltpu.SMEM)
 
 
 def head_rows(q_ref, first, count):
@@ -64,8 +66,12 @@
     rows = blocks * rows_each
     core = lax.axis_index("core")
     section = lax.axis_index("half") * 2 + core
-    finished = completing_ref[0]
-    seen = jnp.logical_and(section > finished, mask_ref[section, finished] == 1)
+    finished = jnp.broadcast_to(completing_ref[...], mask_ref.shape)
+    at_row = lax.broadcasted_iota(jnp.int32, mask_ref.shape, 0) == section
+    at_column = lax.broadcasted_iota(jnp.int32, mask_ref.shape, 1) == finished
+    visible = jnp.logical_and(mask_ref[...] == 1, section > finished)
+    hit = jnp.logical_and(jnp.logical_and(at_row, at_column), visible)
+    seen = jnp.max(jnp.where(hit, 1.0, 0.0)) > 0.5
 
     def store(first, total):
         out = total[:, :HEAD_DIM] / total[:, HEAD_DIM:]
@@ -106,7 +112,8 @@
     copies = []
     for z in range(KV_HEADS // 2):
         for i, (target, x) in enumerate(((keep_ref, xb), (send_ref, 1 - xb))):
-            at = pl.ds(pl.multiple_of((2 * z + x) * WIDE, WIDE), WIDE)
+            head = (z - FIRST_ZC) % 4 * 2 + x
+            at = pl.ds(pl.multiple_of(head * WIDE, WIDE), WIDE)
             copies.append(pltpu.make_async_copy(query_ref.at[0, :, at], target.at[z], sems.at[2 * z + i]))
     for copy in copies:
         copy.start()
@@ -122,8 +129,7 @@
             send_ref[x, high] = source[2 * high + 1 - low]
 
 
-def third_kernel(completing_ref, kept_ref, got_ref, keep_ref, send_ref):
-    del completing_ref
+def third_kernel(kept_ref, got_ref, keep_ref, send_ref):
     zc = lax.axis_index("zc")
     low, high = lax.rem(zc, 2), lax.div(zc, 2)
     for source, z in ((kept_ref, low), (got_ref, 1 - low)):
@@ -137,7 +143,8 @@
     for source, z in ((kept_ref, high), (got_ref, 1 - high)):
         for low in range(2):
             for x in range(2):
-                out_ref[4 * z + 2 * low + x] = source[low, x]
+                place = lax.rem(2 * z + low + 4 - FIRST_ZC, 4)
+                out_ref[2 * place + x] = source[low, x]
 
 
 def pair_kernel(near_ref, sent_ref, after_ref, out_ref, late_ref):
@@ -163,9 +170,11 @@
     for h in range(KV_HEADS):
         first = (h % 2) * 3 * HEAD_DIM
         near = pairs_ref[h // 2, :, (h % 2) * 2 * HEAD_DIM : (h % 2 + 1) * 2 * HEAD_DIM]
-        for z in (h // 2, h // 2 + KV_HEADS // 2):
-            out_ref[z, :, first : first + 2 * HEAD_DIM] = near
-            out_ref[z, :, first + 2 * HEAD_DIM : first + 3 * HEAD_DIM] = clean[:, h * HEAD_DIM : (h + 1) * HEAD_DIM]
+        place = (h // 2 + FIRST_ZC) % 4
+        for z in (place, place + 4):
+            i = Z_ORDER.index(z)
+            out_ref[i, :, first : first + 2 * HEAD_DIM] = near
+            out_ref[i, :, first + 2 * HEAD_DIM : first + 3 * HEAD_DIM] = clean[:, h * HEAD_DIM : (h + 1) * HEAD_DIM]
 
 
 def spread_kernel(served_ref, after_ref, out_ref):
@@ -212,7 +221,6 @@
     width = heads * HEAD_DIM
     core = lax.axis_index("core")
     mine = jnp.where(core == 0, clean_key[0], clean_value[0])
-    near = jnp.stack([key[0], value[0]])
     sent = jnp.where(core == 0, clean_value[0], clean_key[0])
     swapped = lax.ppermute(sent, ("half", "core"), [(0, 1), (1, 0)])
     finished = completing.reshape(1, 1)
@@ -220,6 +228,7 @@
     handed = lax.ppermute(
         picked, ("half",) + z_all, [(z, depth + (z + depth // 2) % depth) for z in range(depth)]
     )
+    near = jnp.stack([jnp.where(picked != picked, picked, a[0]) for a in (key, value)])
     pairs, late = call(
         pair_kernel,
         (shaped(heads // 2, tok, 4 * HEAD_DIM), shaped(tok, width)),
@@ -254,12 +263,12 @@
     keep, send = call(second_kernel, halves, [VMEM] * 2, keep, got)
     after_first = keep
     got = lax.ppermute(send, "zc", [(z, z ^ 1) for z in range(4)])
-    keep, send = call(third_kernel, halves, [SMEM] + [VMEM] * 2, completing, keep, got)
+    keep, send = call(third_kernel, halves, [VMEM] * 2, keep, got)
     got = lax.ppermute(send, "zc", [(z, z ^ 2) for z in range(4)])
     served = call(last_kernel, shaped(heads, tok, WIDE), [VMEM] * 2, keep, got)
 
 
-    kv = lax.all_to_all(kv, z_all, 0, 0, tiled=True)
+    kv = lax.all_to_all(kv, z_all, 0, 0, axis_index_groups=[Z_ORDER], tiled=True)
     kv = call(spread_kernel, shaped(plane, depth * tok, 3 * HEAD_DIM), [VMEM, anywhere], kv, after_first)
     kv = lax.all_to_all(kv, plane_axes, 0, 0, tiled=True)
     clean = call(clean_kernel, shaped(plane, depth * tok, HEAD_DIM), [VMEM, anywhere], kv, served)
@@ -278,8 +287,8 @@
     out = call(
         functools.partial(far_kernel, 3),
         shaped(heads, tok, WIDE),
-        [SMEM] * 2 + [VMEM] * 5,
-        completing,
+        [VMEM] * 7,
+        finished,
         span_mask,
         served,
         kv,
@@ -289,7 +298,7 @@
         cost=estimate(rows, n),
         mib=40,
     )
-    out = lax.all_to_all(out, served_by, 0, 0, tiled=True)
+    out = lax.all_to_all(out, served_by, 0, 0, axis_index_groups=[SERVE_ORDER], tiled=True)
     return jnp.transpose(out, (1, 0, 2)).reshape(1, tok, HEADS * HEAD_DIM)
 
 

time: 84.9 us -> 79 us (0.931)
  Pallas kernels: 7.05 us -> 4.73 us
  waiting for transfers between devices: 21.2 us -> 18.9 us
  local copies, waits for them, and re-layouts: 1.76 us -> 0.84 us
    pallas_call x10, Pallas kernels: 6.85 us -> 4.52 us  [call(): pl.pallas_call(kernel, out_shape=out_shape, in_specs=specs, out_specs=out...]
    all_to_all x1, waiting for transfers between devices: 4.46 us -> 2.13 us  [shards(): lax.all_to_all(kv, z_all, 0, 0, axis_index_groups=[Z_ORDER], tiled=True)]
    unnamed x4, local copies, waits for them, and re-layouts: 0.93 us -> 0.01 us
where the time goes in v7:
time: 79 us; the launch traced here: 78.4 us
  starting transfers between devices  42.9 us (54%)
  waiting for transfers between devices  18.9 us (24%)
  blocking collectives  8.59 us (11%)
  Pallas kernels  4.73 us (6%)
  other arithmetic  1.61 us (2%)
  local copies, waits for them, and re-layouts  0.84 us (1%)
  between operations  0.82 us (1%)
    ppermute x1, starting transfers between devices, shards(): swapped = lax.ppermute(sent, ('half', 'core'), [(0, 1), (1, 0)])  8.78 us
    all_to_all x1, blocking collectives, shards(): lax.all_to_all(out, served_by, 0, 0, axis_index_groups=[SERVE_ORDER], til...  8.59 us
    ppermute x1, starting transfers between devices, shards(): other = lax.ppermute(clean, 'core', [(0, 1), (1, 0)])  7.58 us
    all_to_all x1, starting transfers between devices, shards(): kv = lax.all_to_all(kv, plane_axes, 0, 0, tiled=True)  6.75 us
    all_to_all x1, starting transfers between devices, shards(): lax.all_to_all(kv, z_all, 0, 0, axis_index_groups=[Z_ORDER], tiled=True)  6.19 us
    all_to_all x1, waiting for transfers between devices, shards(): kv = lax.all_to_all(kv, plane_axes, 0, 0, tiled=True)  6.16 us
    ppermute x1, starting transfers between devices, shards(): lax.ppermute(picked, ('half',) + z_all, [(z, depth + (z + depth // 2) % d...  4.97 us
    pallas_call x10, Pallas kernels, call(): pl.pallas_call(kernel, out_shape=out_shape, in_specs=specs, out_specs=out...  4.52 us
  transfers between devices with their start and end apart: 9, of which 6 were waited for; matrix products, arithmetic and copies ran while one was open for 1% of the time, Pallas kernels for 3%

profile of v7, /device:TPU:1, one launch (start us, length us, event | category | flops | bytes accessed | tf_op | source)
XLA Modules:
  0.0 78.4 jit_solution(11092324327565583148)
XLA Ops:
  0.0 0.8 %select_bitcast_fusion = (bf16[16,1024]{1,0:T(8,128)(2,1)S(1)}, bf16[16,1024]{1,0:T(8,128)(2,1)S(1)}) fusion(bf16[1,16,1024]{2,1,0:T(8,128)(2,1)} %param.11, bf16[1,16,1024]{2,1,0:T(8,128)(2,1)} %param.10, pred[]{:T(512)S(6)} %eq.4), kind=kLoop, calls=%fused_computation.5 | loop fusion | flops 32768 | bytes 131073 | tf_op jit(solution)/shard_map/jit(_where)/select_n | solution.py:224
  0.8 8.8 %collective-permute-start = (bf16[16,1024]{1,0:T(8,128)(2,1)S(1)}, bf16[16,1024]{1,0:T(8,128)(2,1)S(1)}, u32[]{:S(2)}, u32[]{:S(2)}) collective-permute-start(bf16[16,1024]{1,0:T(8,128)(2,1)S(1)} %get-tuple-element.25.sent_ref), channel_id=1, source_target_pairs={{0,128},{128,0},{1,129},{129,1},{2,130},{130,2},{3,131},{131,3},{4... | collective-permute-start | bytes 98312 | tf_op jit(solution)/shard_map/ppermute | solution.py:225
  10.3 0.2 collective-permute-done.swapped_ref
  10.4 0.1 shard_map.73.after_ref.picked_ref
  10.5 5.0 %collective-permute-start.2 = (bf16[16,1024]{1,0:T(8,128)(2,1)S(1)}, bf16[16,1024]{1,0:T(8,128)(2,1)S(1)}, u32[]{:S(2)}, u32[]{:S(2)}) collective-permute-start(bf16[16,1024]{1,0:T(8,128)(2,1)S(1)} %shard_map.73.after_ref.picked_ref), channel_id=1, source_target_pairs={{0,320},{16,336},{32,352},{48,368},{64,256},{80,272},{96,288},{112... | collective-permute-start | bytes 98312 | tf_op jit(solution)/shard_map/ppermute | solution.py:228
  15.5 0.8 %fusion = (bf16[1,16,1024]{2,1,0:T(8,128)(2,1)S(1)}, bf16[1,16,1024]{2,1,0:T(8,128)(2,1)S(1)}) fusion(bf16[16,1024]{1,0:T(8,128)(2,1)S(1)} %shard_map.73.after_ref.picked_ref, bf16[1,16,1024]{2,1,0:T(8,128)(2,1)} %param.8, bf16[1,16,1024]{2,1,0:T(8,128)(2,1)} %param.9), kind=kLoop, calls=%fused_computation.3 | loop fusion | flops 49152 | bytes 163840 | tf_op jit(solution)/shard_map/stack | solution.py:231
  16.3 0.7 collective-permute-start.1
  17.0 0.0 collective-permute-done.2.handed_ref
  17.0 0.0 collective-permute-done.1.late_ref
  17.0 0.8 shard_map.75.after_ref
  17.8 6.2 %all-to-all-start = ((bf16[8,16,768]{2,1,0:T(8,128)(2,1)}), bf16[8,16,768]{2,1,0:T(8,128)(2,1)S(1)}, u32[]{:S(2)}, u32[]{:S(2)}) async-start(bf16[8,16,768]{2,1,0:T(8,128)(2,1)} %shard_map.75.after_ref), calls=%async_computation | async-start | bytes 393216 | tf_op jit(solution)/shard_map/all_to_all | solution.py:271
  24.0 0.0 copy-done
  24.0 0.2 shard_map.76
  24.2 3.1 %collective-permute-start.3 = (bf16[4,16,768]{2,1,0:T(8,128)(2,1)S(1)}, bf16[4,16,768]{2,1,0:T(8,128)(2,1)S(1)}, u32[]{:S(2)}, u32[]{:S(2)}) collective-permute-start(bf16[4,16,768]{2,1,0:T(8,128)(2,1)S(1)} %get-tuple-element.18), channel_id=1, source_target_pairs={{0,4},{4,0},{1,5},{5,1},{2,6},{6,2},{3,7},{7,3},{8,12},{12,8},{9,1... | collective-permute-start | bytes 294920 | tf_op jit(solution)/shard_map/ppermute | solution.py:261
  27.3 2.5 %collective-permute-done.3.got_ref = bf16[4,16,768]{2,1,0:T(8,128)(2,1)S(1)} collective-permute-done((bf16[4,16,768]{2,1,0:T(8,128)(2,1)S(1)}, bf16[4,16,768]{2,1,0:T(8,128)(2,1)S(1)}, u32[]{:S(2)}, u32[]{:S(2)}) %collective-permute-start.3) | collective-permute-done | bytes 98336 | tf_op jit(solution)/shard_map/ppermute | solution.py:261
  29.9 2.1 %all-to-all-done.served_ref = bf16[8,16,768]{2,1,0:T(8,128)(2,1)S(1)} async-done(((bf16[8,16,768]{2,1,0:T(8,128)(2,1)}), bf16[8,16,768]{2,1,0:T(8,128)(2,1)S(1)}, u32[]{:S(2)}, u32[]{:S(2)}) %all-to-all-start) | async-done | bytes 196640 | tf_op jit(solution)/shard_map/all_to_all | solution.py:271
  32.0 1.3 %shard_map.80 = bf16[16,128,384]{2,1,0:T(8,128)(2,1)} custom-call(bf16[8,16,768]{2,1,0:T(8,128)(2,1)S(1)} %all-to-all-done.served_ref, bf16[2,2,16,768]{3,2,1,0:T(8,128)(2,1)S(1)} %get-tuple-element.19.kept_ref.after_ref), custom_call_target="tpu_custom_call" | custom-call | tf_op jit(solution)/shard_map/pallas_call | solution.py:200
  33.3 6.8 %all-to-all-start.1 = ((bf16[16,128,384]{2,1,0:T(8,128)(2,1)}), bf16[16,128,384]{2,1,0:T(8,128)(2,1)S(1)}, u32[]{:S(2)}, u32[]{:S(2)}) async-start(bf16[16,128,384]{2,1,0:T(8,128)(2,1)} %shard_map.80), calls=%async_computation.1 | async-start | bytes 3145728 | tf_op jit(solution)/shard_map/all_to_all | solution.py:273
  40.1 1.9 %collective-permute-start.4 = (bf16[2,2,16,768]{3,2,1,0:T(8,128)(2,1)S(1)}, bf16[2,2,16,768]{3,2,1,0:T(8,128)(2,1)S(1)}, u32[]{:S(2)}, u32[]{:S(2)}) collective-permute-start(bf16[2,2,16,768]{3,2,1,0:T(8,128)(2,1)S(1)} %get-tuple-element.20), channel_id=1, source_target_pairs={{0,16},{16,0},{32,48},{48,32},{1,17},{17,1},{33,49},{49,33},{2,18}... | collective-permute-start | bytes 294920 | tf_op jit(solution)/shard_map/ppermute | solution.py:265
  42.0 3.4 %collective-permute-done.4.got_ref = bf16[2,2,16,768]{3,2,1,0:T(8,128)(2,1)S(1)} collective-permute-done((bf16[2,2,16,768]{3,2,1,0:T(8,128)(2,1)S(1)}, bf16[2,2,16,768]{3,2,1,0:T(8,128)(2,1)S(1)}, u32[]{:S(2)}, u32[]{:S(2)}) %collective-permute-start.4) | collective-permute-done | bytes 98336 | tf_op jit(solution)/shard_map/ppermute | solution.py:265
  45.5 3.0 %collective-permute-start.5 = (bf16[2,2,16,768]{3,2,1,0:T(8,128)(2,1)S(1)}, bf16[2,2,16,768]{3,2,1,0:T(8,128)(2,1)S(1)}, u32[]{:S(2)}, u32[]{:S(2)}) collective-permute-start(bf16[2,2,16,768]{3,2,1,0:T(8,128)(2,1)S(1)} %get-tuple-element.22), channel_id=1, source_target_pairs={{0,32},{16,48},{32,0},{48,16},{1,33},{17,49},{33,1},{49,17},{2,34}... | collective-permute-start | bytes 294920 | tf_op jit(solution)/shard_map/ppermute | solution.py:267
  48.4 4.4 %collective-permute-done.5.got_ref = bf16[2,2,16,768]{3,2,1,0:T(8,128)(2,1)S(1)} collective-permute-done((bf16[2,2,16,768]{3,2,1,0:T(8,128)(2,1)S(1)}, bf16[2,2,16,768]{3,2,1,0:T(8,128)(2,1)S(1)}, u32[]{:S(2)}, u32[]{:S(2)}) %collective-permute-start.5) | collective-permute-done | bytes 98336 | tf_op jit(solution)/shard_map/ppermute | solution.py:267
  52.9 6.2 %all-to-all-done.1.kv_ref = bf16[16,128,384]{2,1,0:T(8,128)(2,1)S(1)} async-done(((bf16[16,128,384]{2,1,0:T(8,128)(2,1)}), bf16[16,128,384]{2,1,0:T(8,128)(2,1)S(1)}, u32[]{:S(2)}, u32[]{:S(2)}) %all-to-all-start.1) | async-done | bytes 1572896 | tf_op jit(solution)/shard_map/all_to_all | solution.py:273
  59.1 0.1 shard_map.81
  59.2 0.0 copy-start.1
  59.2 7.6 %collective-permute-start.6 = (bf16[16,128,128]{2,1,0:T(8,128)(2,1)S(1)}, bf16[16,128,128]{2,1,0:T(8,128)(2,1)S(1)}, u32[]{:S(2)}, u32[]{:S(2)}) collective-permute-start(bf16[16,128,128]{2,1,0:T(8,128)(2,1)S(1)} %shard_map.81), channel_id=1, source_target_pairs={{0,128},{128,0},{1,129},{129,1},{2,130},{130,2},{3,131},{131,3},{4... | collective-permute-start | bytes 1572872 | tf_op jit(solution)/shard_map/ppermute | solution.py:275
  66.8 1.9 %shard_map.82 = (f32[768,256]{1,0:T(8,128)S(1)}, f32[768,128]{1,0:T(8,128)S(1)}) custom-call(bf16[8,16,768]{2,1,0:T(8,128)(2,1)S(1)} %shard_map.79.after_ref.q_ref, bf16[16,128,384]{2,1,0:T(8,128)(2,1)S(1)} %all-to-all-done.1.kv_ref), custom_call_target="tpu_custom_call" | custom-call | flops 805306368 | bytes 4194304 | tf_op jit(solution)/shard_map/pallas_call | solution.py:200
  68.7 0.0 collective-permute-done.6.other_ref
  68.7 0.3 shard_map.83
  69.0 8.6 %all_to_all.15 = bf16[8,16,768]{2,1,0:T(8,128)(2,1)S(1)} all-to-all(bf16[8,16,768]{2,1,0:T(8,128)(2,1)S(1)} %shard_map.83), channel_id=1, replica_groups={{16,20,32,36,48,52,0,4},{17,21,33,37,49,53,1,5},{18,22,34,38,50,54,2,6}..., dimensions={0} | all-to-all | bytes 393216 | tf_op jit(solution)/shard_map/all_to_all | solution.py:301
  77.6 0.1 copy.8
  77.7 0.8 reshape.11
  (7 shorter events, 0.1 us)
Async XLA Ops:
  0.0 24.0 %copy-start = (bf16[1,16,6144]{2,1,0:T(8,128)(2,1)S(1)}, bf16[1,16,6144]{2,1,0:T(8,128)(2,1)}, u32[]{:S(2)}) copy-start(bf16[1,16,6144]{2,1,0:T(8,128)(2,1)} %query_ref.1) | copy-start | bytes 589828
  0.8 9.6 %collective-permute-start = (bf16[16,1024]{1,0:T(8,128)(2,1)S(1)}, bf16[16,1024]{1,0:T(8,128)(2,1)S(1)}, u32[]{:S(2)}, u32[]{:S(2)}) collective-permute-start(bf16[16,1024]{1,0:T(8,128)(2,1)S(1)} %get-tuple-element.25.sent_ref), channel_id=1, source_target_pairs={{0,128},{128,0},{1,129},{129,1},{2,130},{130,2},{3,131},{131,3},{4... | collective-permute-start | bytes 98312 | tf_op jit(solution)/shard_map/ppermute | solution.py:225
  10.5 6.5 %collective-permute-start.2 = (bf16[16,1024]{1,0:T(8,128)(2,1)S(1)}, bf16[16,1024]{1,0:T(8,128)(2,1)S(1)}, u32[]{:S(2)}, u32[]{:S(2)}) collective-permute-start(bf16[16,1024]{1,0:T(8,128)(2,1)S(1)} %shard_map.73.after_ref.picked_ref), channel_id=1, source_target_pairs={{0,320},{16,336},{32,352},{48,368},{64,256},{80,272},{96,288},{112... | collective-permute-start | bytes 98312 | tf_op jit(solution)/shard_map/ppermute | solution.py:228
  16.3 0.7 collective-permute-start.1
  17.8 14.2 %all-to-all-start = ((bf16[8,16,768]{2,1,0:T(8,128)(2,1)}), bf16[8,16,768]{2,1,0:T(8,128)(2,1)S(1)}, u32[]{:S(2)}, u32[]{:S(2)}) async-start(bf16[8,16,768]{2,1,0:T(8,128)(2,1)} %shard_map.75.after_ref), calls=%async_computation | async-start | bytes 393216 | tf_op jit(solution)/shard_map/all_to_all | solution.py:271
  24.2 5.7 %collective-permute-start.3 = (bf16[4,16,768]{2,1,0:T(8,128)(2,1)S(1)}, bf16[4,16,768]{2,1,0:T(8,128)(2,1)S(1)}, u32[]{:S(2)}, u32[]{:S(2)}) collective-permute-start(bf16[4,16,768]{2,1,0:T(8,128)(2,1)S(1)} %get-tuple-element.18), channel_id=1, source_target_pairs={{0,4},{4,0},{1,5},{5,1},{2,6},{6,2},{3,7},{7,3},{8,12},{12,8},{9,1... | collective-permute-start | bytes 294920 | tf_op jit(solution)/shard_map/ppermute | solution.py:261
  33.3 25.8 %all-to-all-start.1 = ((bf16[16,128,384]{2,1,0:T(8,128)(2,1)}), bf16[16,128,384]{2,1,0:T(8,128)(2,1)S(1)}, u32[]{:S(2)}, u32[]{:S(2)}) async-start(bf16[16,128,384]{2,1,0:T(8,128)(2,1)} %shard_map.80), calls=%async_computation.1 | async-start | bytes 3145728 | tf_op jit(solution)/shard_map/all_to_all | solution.py:273
  40.1 5.4 %collective-permute-start.4 = (bf16[2,2,16,768]{3,2,1,0:T(8,128)(2,1)S(1)}, bf16[2,2,16,768]{3,2,1,0:T(8,128)(2,1)S(1)}, u32[]{:S(2)}, u32[]{:S(2)}) collective-permute-start(bf16[2,2,16,768]{3,2,1,0:T(8,128)(2,1)S(1)} %get-tuple-element.20), channel_id=1, source_target_pairs={{0,16},{16,0},{32,48},{48,32},{1,17},{17,1},{33,49},{49,33},{2,18}... | collective-permute-start | bytes 294920 | tf_op jit(solution)/shard_map/ppermute | solution.py:265
  45.5 7.4 %collective-permute-start.5 = (bf16[2,2,16,768]{3,2,1,0:T(8,128)(2,1)S(1)}, bf16[2,2,16,768]{3,2,1,0:T(8,128)(2,1)S(1)}, u32[]{:S(2)}, u32[]{:S(2)}) collective-permute-start(bf16[2,2,16,768]{3,2,1,0:T(8,128)(2,1)S(1)} %get-tuple-element.22), channel_id=1, source_target_pairs={{0,32},{16,48},{32,0},{48,16},{1,33},{17,49},{33,1},{49,17},{2,34}... | collective-permute-start | bytes 294920 | tf_op jit(solution)/shard_map/ppermute | solution.py:267
  59.2 9.6 %copy-start.1 = (s32[4,4]{1,0:T(4,128)S(1)}, s32[4,4]{1,0:T(4,128)}, u32[]{:S(2)}) copy-start(s32[4,4]{1,0:T(4,128)} %mask_ref.1) | copy-start | bytes 196
  59.2 9.5 %collective-permute-start.6 = (bf16[16,128,128]{2,1,0:T(8,128)(2,1)S(1)}, bf16[16,128,128]{2,1,0:T(8,128)(2,1)S(1)}, u32[]{:S(2)}, u32[]{:S(2)}) collective-permute-start(bf16[16,128,128]{2,1,0:T(8,128)(2,1)S(1)} %shard_map.81), channel_id=1, source_target_pairs={{0,128},{128,0},{1,129},{129,1},{2,130},{130,2},{3,131},{131,3},{4... | collective-permute-start | bytes 1572872 | tf_op jit(solution)/shard_map/ppermute | solution.py:275

commit v8 on v7

--- a/solution.py
+++ b/solution.py
@@ -58,6 +58,24 @@
         largest, sums = weigh(block, v_ones)
         sums_ref[at, :] = sums
         largest_ref[at, :] = jnp.broadcast_to(largest, (count * rows, HEAD_DIM))
+
+
+def alone_kernel(count, q_ref, kv_ref, out_ref):
+    n = kv_ref.shape[0] * kv_ref.shape[1]
+    blocks, rows_each = q_ref.shape[0], q_ref.shape[1]
+    rows = blocks * rows_each
+    k = kv_ref[:, :, :HEAD_DIM].reshape(n, HEAD_DIM)
+    v_ones = with_ones(kv_ref[:, :, HEAD_DIM : 2 * HEAD_DIM].reshape(n, HEAD_DIM))
+    firsts = range(0, GROUP, count)
+    scores = [scores_of(head_rows(q_ref, first, count), k) for first in firsts]
+    for first, block in zip(firsts, scores):
+        largest, sums = weigh(block, v_ones)
+        out = sums[:, :HEAD_DIM] / sums[:, HEAD_DIM:]
+        for i in range(count):
+            g = first + i
+            out_ref[:, :, g * HEAD_DIM : (g + 1) * HEAD_DIM] = (
+                out[i * rows : (i + 1) * rows].astype(out_ref.dtype).reshape(blocks, rows_each, HEAD_DIM)
+            )
 
 
 def far_kernel(count, completing_ref, mask_ref, q_ref, kv_ref, other_ref, sums_ref, largest_ref, out_ref):
@@ -181,9 +199,10 @@
     del after_ref
     rows = served_ref.shape[0] * served_ref.shape[1]
     each = 3 * HEAD_DIM
+    width = out_ref.shape[2]
     for i in range(out_ref.shape[0]):
         head = (i // 4) % 2
-        out_ref[i] = served_ref[:, :, head * each : (head + 1) * each].reshape(rows, each)
+        out_ref[i] = served_ref[:, :, head * each : head * each + width].reshape(rows, width)
 
 
 def clean_kernel(kv_ref, after_ref, out_ref):
@@ -261,43 +280,59 @@
     got = lax.ppermute(send, "xb", [(0, 1), (1, 0)])
     halves = (shaped(2, 2, tok, WIDE),) * 2
     keep, send = call(second_kernel, halves, [VMEM] * 2, keep, got)
-    after_first = keep
-    got = lax.ppermute(send, "zc", [(z, z ^ 1) for z in range(4)])
-    keep, send = call(third_kernel, halves, [VMEM] * 2, keep, got)
-    got = lax.ppermute(send, "zc", [(z, z ^ 2) for z in range(4)])
-    served = call(last_kernel, shaped(heads, tok, WIDE), [VMEM] * 2, keep, got)
-
-
     kv = lax.all_to_all(kv, z_all, 0, 0, axis_index_groups=[Z_ORDER], tiled=True)
-    kv = call(spread_kernel, shaped(plane, depth * tok, 3 * HEAD_DIM), [VMEM, anywhere], kv, after_first)
-    kv = lax.all_to_all(kv, plane_axes, 0, 0, tiled=True)
-    clean = call(clean_kernel, shaped(plane, depth * tok, HEAD_DIM), [VMEM, anywhere], kv, served)
-    other = lax.ppermute(clean, "core", [(0, 1), (1, 0)])
-
     rows, n = heads * tok * GROUP, plane * depth * tok
-    sums, largest = call(
-        functools.partial(own_kernel, 3),
-        (shaped(rows, 2 * HEAD_DIM, dtype=jnp.float32), shaped(rows, HEAD_DIM, dtype=jnp.float32)),
-        [VMEM] * 2,
-        served,
-        kv,
-        cost=estimate(rows, n),
-        mib=40,
-    )
-    out = call(
-        functools.partial(far_kernel, 3),
-        shaped(heads, tok, WIDE),
-        [VMEM] * 7,
-        finished,
-        span_mask,
-        served,
-        kv,
-        other,
-        sums,
-        largest,
-        cost=estimate(rows, n),
-        mib=40,
-    )
+
+    def gather(kv, keep, send, width):
+        own = call(spread_kernel, shaped(plane, depth * tok, width), [VMEM, anywhere], kv, keep)
+        own = lax.all_to_all(own, plane_axes, 0, 0, tiled=True)
+        got = lax.ppermute(send, "zc", [(z, z ^ 1) for z in range(4)])
+        keep, send = call(third_kernel, halves, [VMEM] * 2, keep, got)
+        got = lax.ppermute(send, "zc", [(z, z ^ 2) for z in range(4)])
+        return own, call(last_kernel, shaped(heads, tok, WIDE), [VMEM] * 2, keep, got)
+
+    def with_clean(kv, keep, send, finished, span_mask):
+        kv, served = gather(kv, keep, send, 3 * HEAD_DIM)
+        clean = call(clean_kernel, shaped(plane, depth * tok, HEAD_DIM), [VMEM, anywhere], kv, served)
+        other = lax.ppermute(clean, "core", [(0, 1), (1, 0)])
+        sums, largest = call(
+            functools.partial(own_kernel, 3),
+            (shaped(rows, 2 * HEAD_DIM, dtype=jnp.float32), shaped(rows, HEAD_DIM, dtype=jnp.float32)),
+            [VMEM] * 2,
+            served,
+            kv,
+            cost=estimate(rows, n),
+            mib=40,
+        )
+        return call(
+            functools.partial(far_kernel, 3),
+            shaped(heads, tok, WIDE),
+            [VMEM] * 7,
+            finished,
+            span_mask,
+            served,
+            kv,
+            other,
+            sums,
+            largest,
+            cost=estimate(rows, n),
+            mib=40,
+        )
+
+    def without(kv, keep, send, finished, span_mask):
+        kv, served = gather(kv, keep, send, 2 * HEAD_DIM)
+        return call(
+            functools.partial(alone_kernel, 3),
+            shaped(heads, tok, WIDE),
+            [VMEM] * 2,
+            served,
+            kv,
+            cost=estimate(rows, n),
+            mib=40,
+        )
+
+    may_see = 2 * lax.axis_index("half") + 1 > completing[0]
+    out = lax.cond(may_see, with_clean, without, kv, keep, send, finished, span_mask)
     out = lax.all_to_all(out, served_by, 0, 0, axis_index_groups=[SERVE_ORDER], tiled=True)
     return jnp.transpose(out, (1, 0, 2)).reshape(1, tok, HEADS * HEAD_DIM)
 

time: 79 us -> 73.6 us (0.932)
  the two profiles are of different devices: /device:TPU:1 before, /device:TPU:384 now
where the time goes in v8:
time: 73.6 us; the launch traced here: 73.1 us
  starting transfers between devices  31 us (42%)
  waiting for transfers between devices  20.5 us (28%)
  blocking collectives  11.1 us (15%)
  Pallas kernels  7.33 us (10%)
  other arithmetic  1.61 us (2%)
  local copies, waits for them, and re-layouts  0.84 us (1%)
  between operations  0.74 us (1%)
    all_to_all x1, blocking collectives, shards(): lax.all_to_all(out, served_by, 0, 0, axis_index_groups=[SERVE_ORDER], til...  11.1 us
    ppermute x1, waiting for transfers between devices, shards(): lax.ppermute(picked, ('half',) + z_all, [(z, depth + (z + depth // 2) % d...  7.38 us
    pallas_call x10, Pallas kernels, call(): pl.pallas_call(kernel, out_shape=out_shape, in_specs=specs, out_specs=out...  7.12 us
    all_to_all x1, starting transfers between devices, gather(): own = lax.all_to_all(own, plane_axes, 0, 0, tiled=True)  7.03 us
    ppermute x1, starting transfers between devices, gather(): got = lax.ppermute(send, 'zc', [(z, z ^ 2) for z in range(4)])  5.71 us
    all_to_all x1, starting transfers between devices, shards(): lax.all_to_all(kv, z_all, 0, 0, axis_index_groups=[Z_ORDER], tiled=True)  5.49 us
    all_to_all x1, waiting for transfers between devices, gather(): own = lax.all_to_all(own, plane_axes, 0, 0, tiled=True)  4.35 us
    ppermute x1, starting transfers between devices, gather(): got = lax.ppermute(send, 'zc', [(z, z ^ 1) for z in range(4)])  3.72 us
  transfers between devices with their start and end apart: 9, of which 6 were waited for; matrix products, arithmetic and copies ran while one was open for 1% of the time, Pallas kernels for 3%

profile of v8, /device:TPU:384, one launch (start us, length us, event | category | flops | bytes accessed | tf_op | source)
XLA Modules:
  0.0 73.1 jit_solution(18202819106326138122)
XLA Ops:
  0.0 0.8 %select_bitcast_fusion = (bf16[16,1024]{1,0:T(8,128)(2,1)S(1)}, bf16[16,1024]{1,0:T(8,128)(2,1)S(1)}) fusion(bf16[1,16,1024]{2,1,0:T(8,128)(2,1)} %param.13, bf16[1,16,1024]{2,1,0:T(8,128)(2,1)} %param.12, pred[]{:T(512)S(6)} %eq.4), kind=kLoop, calls=%fused_computation.5 | loop fusion | flops 32768 | bytes 131073 | tf_op jit(solution)/shard_map/jit(_where)/select_n | solution.py:243
  0.8 0.7 collective-permute-start.5
  2.1 0.0 collective-permute-done.5.swapped_ref
  2.1 0.1 shard_map.74.after_ref.picked_ref
  2.2 1.3 %collective-permute-start.7 = (bf16[16,1024]{1,0:T(8,128)(2,1)S(1)}, bf16[16,1024]{1,0:T(8,128)(2,1)S(1)}, u32[]{:S(2)}, u32[]{:S(2)}) collective-permute-start(bf16[16,1024]{1,0:T(8,128)(2,1)S(1)} %shard_map.74.after_ref.picked_ref), channel_id=1, source_target_pairs={{0,320},{16,336},{32,352},{48,368},{64,256},{80,272},{96,288},{112... | collective-permute-start | bytes 98312 | tf_op jit(solution)/shard_map/ppermute | solution.py:247
  3.5 0.8 %fusion = (bf16[1,16,1024]{2,1,0:T(8,128)(2,1)S(1)}, bf16[1,16,1024]{2,1,0:T(8,128)(2,1)S(1)}) fusion(bf16[16,1024]{1,0:T(8,128)(2,1)S(1)} %shard_map.74.after_ref.picked_ref, bf16[1,16,1024]{2,1,0:T(8,128)(2,1)} %param.10, bf16[1,16,1024]{2,1,0:T(8,128)(2,1)} %param.11), kind=kLoop, calls=%fused_computation.3 | loop fusion | flops 49152 | bytes 163840 | tf_op jit(solution)/shard_map/stack | solution.py:250
  4.3 1.7 %collective-permute-start.6 = (bf16[16,1024]{1,0:T(8,128)(2,1)S(1)}, bf16[16,1024]{1,0:T(8,128)(2,1)S(1)}, u32[]{:S(2)}, u32[]{:S(2)}) collective-permute-start(bf16[16,1024]{1,0:T(8,128)(2,1)S(1)} %get-tuple-element.45), channel_id=1, source_target_pairs={{256,384},{257,385},{258,386},{259,387},{260,388},{261,389},{262,3... | collective-permute-start | bytes 98312 | tf_op jit(solution)/shard_map/ppermute | solution.py:259
  6.1 7.4 %collective-permute-done.7.handed_ref = bf16[16,1024]{1,0:T(8,128)(2,1)S(1)} collective-permute-done((bf16[16,1024]{1,0:T(8,128)(2,1)S(1)}, bf16[16,1024]{1,0:T(8,128)(2,1)S(1)}, u32[]{:S(2)}, u32[]{:S(2)}) %collective-permute-start.7) | collective-permute-done | bytes 32800 | tf_op jit(solution)/shard_map/ppermute | solution.py:247
  13.5 0.0 collective-permute-done.6.late_ref
  13.5 0.8 %shard_map.76.after_ref = bf16[8,16,768]{2,1,0:T(8,128)(2,1)} custom-call(s32[1,1]{1,0:T(1,128)} %bitcast.17.completing_ref, bf16[4,16,512]{2,1,0:T(8,128)(2,1)S(1)} %get-tuple-element.44.pairs_ref, bf16[16,1024]{1,0:T(8,128)(2,1)S(1)} %shard_map.74.after_ref.picked_ref, bf16[16,1024]{1,0:T(8,128)(2,1)S(1)} %collective-permute-done.6.late_ref, ...), custom_call_target="tpu_custom_call" | custom-call | tf_op jit(solution)/shard_map/pallas_call | solution.py:219
  14.2 5.5 %all-to-all-start.2 = ((bf16[8,16,768]{2,1,0:T(8,128)(2,1)}), bf16[8,16,768]{2,1,0:T(8,128)(2,1)S(1)}, u32[]{:S(2)}, u32[]{:S(2)}) async-start(bf16[8,16,768]{2,1,0:T(8,128)(2,1)} %shard_map.76.after_ref), calls=%async_computation.2 | async-start | bytes 393216 | tf_op jit(solution)/shard_map/all_to_all | solution.py:283
  19.7 0.0 copy-done
  19.7 0.2 shard_map.77
  20.0 3.4 %collective-permute-start.8 = (bf16[4,16,768]{2,1,0:T(8,128)(2,1)S(1)}, bf16[4,16,768]{2,1,0:T(8,128)(2,1)S(1)}, u32[]{:S(2)}, u32[]{:S(2)}) collective-permute-start(bf16[4,16,768]{2,1,0:T(8,128)(2,1)S(1)} %get-tuple-element.47), channel_id=1, source_target_pairs={{0,4},{4,0},{1,5},{5,1},{2,6},{6,2},{3,7},{7,3},{8,12},{12,8},{9,1... | collective-permute-start | bytes 294920 | tf_op jit(solution)/shard_map/ppermute | solution.py:280
  23.4 3.1 %collective-permute-done.8.got_ref = bf16[4,16,768]{2,1,0:T(8,128)(2,1)S(1)} collective-permute-done((bf16[4,16,768]{2,1,0:T(8,128)(2,1)S(1)}, bf16[4,16,768]{2,1,0:T(8,128)(2,1)S(1)}, u32[]{:S(2)}, u32[]{:S(2)}) %collective-permute-start.8) | collective-permute-done | bytes 98336 | tf_op jit(solution)/shard_map/ppermute | solution.py:280
  26.5 0.2 all-to-all-done.2
  26.7 34.4 %conditional.1 = (bf16[8,16,768]{2,1,0:T(8,128)(2,1)S(1)}) conditional(s32[]{:T(128)} %convert_element_type.3, (bf16[2,2,16,768]{3,2,1,0:T(8,128)(2,1)S(1)}, bf16[2,2,16,768]{3,2,1,0:T(8,128)(2,1)S(1)}, bf16[8,16,768]{2,1,0:T(8,128)(2,1)S(1)}) %tuple.11, (bf16[2,2,16,768]{3,2,1,0:T(8,128)(2,1)S(1)}, bf16[2,2,16,768]{3,2,1,0:T(8,128)(2,1)S(1)}, ...), branch_computations={%region_0.1_spmd, %region_1.2_spmd} | conditional | flops 1610612736 | bytes 15990944 | solution.py:335
  26.7 1.3 %branch_1_fun.8 = bf16[16,128,384]{2,1,0:T(8,128)(2,1)} custom-call(bf16[8,16,768]{2,1,0:T(8,128)(2,1)S(1)} %get-tuple-element.35.served_ref, bf16[2,2,16,768]{3,2,1,0:T(8,128)(2,1)S(1)} %get-tuple-element.31.kept_ref.after_ref), custom_call_target="tpu_custom_call" | custom-call | tf_op jit(solution)/shard_map/cond/branch_1_fun/pallas_call | solution.py:219
  28.0 7.0 %all-to-all-start.1 = ((bf16[16,128,384]{2,1,0:T(8,128)(2,1)}), bf16[16,128,384]{2,1,0:T(8,128)(2,1)S(1)}, u32[]{:S(2)}, u32[]{:S(2)}) async-start(bf16[16,128,384]{2,1,0:T(8,128)(2,1)} %branch_1_fun.8), calls=%async_computation.1 | async-start | bytes 3145728 | tf_op jit(solution)/shard_map/cond/branch_1_fun/all_to_all | solution.py:288
  35.1 3.7 %collective-permute-start.2 = (bf16[2,2,16,768]{3,2,1,0:T(8,128)(2,1)S(1)}, bf16[2,2,16,768]{3,2,1,0:T(8,128)(2,1)S(1)}, u32[]{:S(2)}, u32[]{:S(2)}) collective-permute-start(bf16[2,2,16,768]{3,2,1,0:T(8,128)(2,1)S(1)} %get-tuple-element.32), channel_id=1, source_target_pairs={{0,16},{16,0},{32,48},{48,32},{1,17},{17,1},{33,49},{49,33},{2,18}... | collective-permute-start | bytes 294920 | tf_op jit(solution)/shard_map/cond/branch_1_fun/ppermute | solution.py:289
  38.8 2.8 %collective-permute-done.2.got_ref = bf16[2,2,16,768]{3,2,1,0:T(8,128)(2,1)S(1)} collective-permute-done((bf16[2,2,16,768]{3,2,1,0:T(8,128)(2,1)S(1)}, bf16[2,2,16,768]{3,2,1,0:T(8,128)(2,1)S(1)}, u32[]{:S(2)}, u32[]{:S(2)}) %collective-permute-start.2) | collective-permute-done | bytes 98336 | tf_op jit(solution)/shard_map/cond/branch_1_fun/ppermute | solution.py:289
  41.6 5.7 %collective-permute-start.3 = (bf16[2,2,16,768]{3,2,1,0:T(8,128)(2,1)S(1)}, bf16[2,2,16,768]{3,2,1,0:T(8,128)(2,1)S(1)}, u32[]{:S(2)}, u32[]{:S(2)}) collective-permute-start(bf16[2,2,16,768]{3,2,1,0:T(8,128)(2,1)S(1)} %get-tuple-element.34), channel_id=1, source_target_pairs={{0,32},{16,48},{32,0},{48,16},{1,33},{17,49},{33,1},{49,17},{2,34}... | collective-permute-start | bytes 294920 | tf_op jit(solution)/shard_map/cond/branch_1_fun/ppermute | solution.py:291
  47.3 2.6 %collective-permute-done.3.got_ref = bf16[2,2,16,768]{3,2,1,0:T(8,128)(2,1)S(1)} collective-permute-done((bf16[2,2,16,768]{3,2,1,0:T(8,128)(2,1)S(1)}, bf16[2,2,16,768]{3,2,1,0:T(8,128)(2,1)S(1)}, u32[]{:S(2)}, u32[]{:S(2)}) %collective-permute-start.3) | collective-permute-done | bytes 98336 | tf_op jit(solution)/shard_map/cond/branch_1_fun/ppermute | solution.py:291
  50.0 4.4 %all-to-all-done.1.kv_ref = bf16[16,128,384]{2,1,0:T(8,128)(2,1)S(1)} async-done(((bf16[16,128,384]{2,1,0:T(8,128)(2,1)}), bf16[16,128,384]{2,1,0:T(8,128)(2,1)S(1)}, u32[]{:S(2)}, u32[]{:S(2)}) %all-to-all-start.1) | async-done | bytes 1572896 | tf_op jit(solution)/shard_map/cond/branch_1_fun/all_to_all | solution.py:288
  54.3 0.1 branch_1_fun.9
  54.4 1.9 %collective-permute-start.4 = (bf16[16,128,128]{2,1,0:T(8,128)(2,1)S(1)}, bf16[16,128,128]{2,1,0:T(8,128)(2,1)S(1)}, u32[]{:S(2)}, u32[]{:S(2)}) collective-permute-start(bf16[16,128,128]{2,1,0:T(8,128)(2,1)S(1)} %branch_1_fun.9), channel_id=1, source_target_pairs={{0,128},{128,0},{1,129},{129,1},{2,130},{130,2},{3,131},{131,3},{4... | collective-permute-start | bytes 1572872 | tf_op jit(solution)/shard_map/cond/branch_1_fun/ppermute | solution.py:297
  56.3 1.9 %branch_1_fun.10 = (f32[768,256]{1,0:T(8,128)S(1)}, f32[768,128]{1,0:T(8,128)S(1)}) custom-call(bf16[8,16,768]{2,1,0:T(8,128)(2,1)S(1)} %branch_1_fun.7.after_ref.q_ref, bf16[16,128,384]{2,1,0:T(8,128)(2,1)S(1)} %all-to-all-done.1.kv_ref), custom_call_target="tpu_custom_call" | custom-call | flops 805306368 | bytes 4194304 | tf_op jit(solution)/shard_map/cond/branch_1_fun/pallas_call | solution.py:219
  58.3 0.0 collective-permute-done.4.other_ref
  58.3 2.9 %branch_1_fun.11 = bf16[8,16,768]{2,1,0:T(8,128)(2,1)S(1)} custom-call(s32[1,1]{1,0:T(1,128)} %get-tuple-element.29.completing_ref, s32[4,4]{1,0:T(4,128)S(1)} %get-tuple-element.51.mask_ref, bf16[8,16,768]{2,1,0:T(8,128)(2,1)S(1)} %branch_1_fun.7.after_ref.q_ref, bf16[16,128,384]{2,1,0:T(8,128)(2,1)S(1)} %all-to-all-done.1.kv_ref, ...), custom_call_target="tpu_custom_call" | custom-call | flops 805306368 | bytes 4194304 | tf_op jit(solution)/shard_map/cond/branch_1_fun/pallas_call | solution.py:219
  61.2 11.1 %all_to_all.18 = bf16[8,16,768]{2,1,0:T(8,128)(2,1)S(1)} all-to-all(bf16[8,16,768]{2,1,0:T(8,128)(2,1)S(1)} %get-tuple-element.56), channel_id=1, replica_groups={{16,20,32,36,48,52,0,4},{17,21,33,37,49,53,1,5},{18,22,34,38,50,54,2,6}..., dimensions={0} | all-to-all | bytes 393216 | tf_op jit(solution)/shard_map/all_to_all | solution.py:336
  72.2 0.1 copy.9
  72.3 0.8 %reshape.11 = bf16[1,16,6144]{2,1,0:T(8,128)(2,1)} reshape(bf16[16,8,768]{2,1,0:T(8,128)(2,1)S(1)} %copy.9) | data formatting | bytes 393216 | tf_op jit(solution)/shard_map/reshape | solution.py:337
  (8 shorter events, 0.1 us)
Async XLA Ops:
  0.0 19.7 %copy-start = (bf16[1,16,6144]{2,1,0:T(8,128)(2,1)S(1)}, bf16[1,16,6144]{2,1,0:T(8,128)(2,1)}, u32[]{:S(2)}) copy-start(bf16[1,16,6144]{2,1,0:T(8,128)(2,1)} %query_ref.1) | copy-start | bytes 589828
  0.0 26.7 %copy-start.1 = (s32[4,4]{1,0:T(4,128)S(1)}, s32[4,4]{1,0:T(4,128)}, u32[]{:S(2)}) copy-start(s32[4,4]{1,0:T(4,128)} %param.15) | copy-start | bytes 196
  0.8 1.3 %collective-permute-start.5 = (bf16[16,1024]{1,0:T(8,128)(2,1)S(1)}, bf16[16,1024]{1,0:T(8,128)(2,1)S(1)}, u32[]{:S(2)}, u32[]{:S(2)}) collective-permute-start(bf16[16,1024]{1,0:T(8,128)(2,1)S(1)} %get-tuple-element.52.sent_ref), channel_id=1, source_target_pairs={{0,128},{128,0},{1,129},{129,1},{2,130},{130,2},{3,131},{131,3},{4... | collective-permute-start | bytes 98312 | tf_op jit(solution)/shard_map/ppermute | solution.py:244
  2.2 11.2 %collective-permute-start.7 = (bf16[16,1024]{1,0:T(8,128)(2,1)S(1)}, bf16[16,1024]{1,0:T(8,128)(2,1)S(1)}, u32[]{:S(2)}, u32[]{:S(2)}) collective-permute-start(bf16[16,1024]{1,0:T(8,128)(2,1)S(1)} %shard_map.74.after_ref.picked_ref), channel_id=1, source_target_pairs={{0,320},{16,336},{32,352},{48,368},{64,256},{80,272},{96,288},{112... | collective-permute-start | bytes 98312 | tf_op jit(solution)/shard_map/ppermute | solution.py:247
  4.3 9.1 %collective-permute-start.6 = (bf16[16,1024]{1,0:T(8,128)(2,1)S(1)}, bf16[16,1024]{1,0:T(8,128)(2,1)S(1)}, u32[]{:S(2)}, u32[]{:S(2)}) collective-permute-start(bf16[16,1024]{1,0:T(8,128)(2,1)S(1)} %get-tuple-element.45), channel_id=1, source_target_pairs={{256,384},{257,385},{258,386},{259,387},{260,388},{261,389},{262,3... | collective-permute-start | bytes 98312 | tf_op jit(solution)/shard_map/ppermute | solution.py:259
  14.2 12.5 %all-to-all-start.2 = ((bf16[8,16,768]{2,1,0:T(8,128)(2,1)}), bf16[8,16,768]{2,1,0:T(8,128)(2,1)S(1)}, u32[]{:S(2)}, u32[]{:S(2)}) async-start(bf16[8,16,768]{2,1,0:T(8,128)(2,1)} %shard_map.76.after_ref), calls=%async_computation.2 | async-start | bytes 393216 | tf_op jit(solution)/shard_map/all_to_all | solution.py:283
  20.0 6.5 %collective-permute-start.8 = (bf16[4,16,768]{2,1,0:T(8,128)(2,1)S(1)}, bf16[4,16,768]{2,1,0:T(8,128)(2,1)S(1)}, u32[]{:S(2)}, u32[]{:S(2)}) collective-permute-start(bf16[4,16,768]{2,1,0:T(8,128)(2,1)S(1)} %get-tuple-element.47), channel_id=1, source_target_pairs={{0,4},{4,0},{1,5},{5,1},{2,6},{6,2},{3,7},{7,3},{8,12},{12,8},{9,1... | collective-permute-start | bytes 294920 | tf_op jit(solution)/shard_map/ppermute | solution.py:280
  28.0 26.3 %all-to-all-start.1 = ((bf16[16,128,384]{2,1,0:T(8,128)(2,1)}), bf16[16,128,384]{2,1,0:T(8,128)(2,1)S(1)}, u32[]{:S(2)}, u32[]{:S(2)}) async-start(bf16[16,128,384]{2,1,0:T(8,128)(2,1)} %branch_1_fun.8), calls=%async_computation.1 | async-start | bytes 3145728 | tf_op jit(solution)/shard_map/cond/branch_1_fun/all_to_all | solution.py:288
  35.1 6.5 %collective-permute-start.2 = (bf16[2,2,16,768]{3,2,1,0:T(8,128)(2,1)S(1)}, bf16[2,2,16,768]{3,2,1,0:T(8,128)(2,1)S(1)}, u32[]{:S(2)}, u32[]{:S(2)}) collective-permute-start(bf16[2,2,16,768]{3,2,1,0:T(8,128)(2,1)S(1)} %get-tuple-element.32), channel_id=1, source_target_pairs={{0,16},{16,0},{32,48},{48,32},{1,17},{17,1},{33,49},{49,33},{2,18}... | collective-permute-start | bytes 294920 | tf_op jit(solution)/shard_map/cond/branch_1_fun/ppermute | solution.py:289
  41.6 8.3 %collective-permute-start.3 = (bf16[2,2,16,768]{3,2,1,0:T(8,128)(2,1)S(1)}, bf16[2,2,16,768]{3,2,1,0:T(8,128)(2,1)S(1)}, u32[]{:S(2)}, u32[]{:S(2)}) collective-permute-start(bf16[2,2,16,768]{3,2,1,0:T(8,128)(2,1)S(1)} %get-tuple-element.34), channel_id=1, source_target_pairs={{0,32},{16,48},{32,0},{48,16},{1,33},{17,49},{33,1},{49,17},{2,34}... | collective-permute-start | bytes 294920 | tf_op jit(solution)/shard_map/cond/branch_1_fun/ppermute | solution.py:291
  54.4 3.9 %collective-permute-start.4 = (bf16[16,128,128]{2,1,0:T(8,128)(2,1)S(1)}, bf16[16,128,128]{2,1,0:T(8,128)(2,1)S(1)}, u32[]{:S(2)}, u32[]{:S(2)}) collective-permute-start(bf16[16,128,128]{2,1,0:T(8,128)(2,1)S(1)} %branch_1_fun.9), channel_id=1, source_target_pairs={{0,128},{128,0},{1,129},{129,1},{2,130},{130,2},{3,131},{131,3},{4... | collective-permute-start | bytes 1572872 | tf_op jit(solution)/shard_map/cond/branch_1_fun/ppermute | solution.py:297

commit v9 on v8

--- a/solution.py
+++ b/solution.py
@@ -165,9 +165,8 @@
                 out_ref[2 * place + x] = source[low, x]
 
 
-def pair_kernel(near_ref, sent_ref, after_ref, out_ref, late_ref):
+def pair_kernel(near_ref, after_ref, out_ref):
     del after_ref
-    late_ref[...] = sent_ref[...]
     for h in range(KV_HEADS):
         at = slice(h * HEAD_DIM, (h + 1) * HEAD_DIM)
         first = (h % 2) * 2 * HEAD_DIM
@@ -180,11 +179,8 @@
     out_ref[...] = jnp.where(jnp.broadcast_to(other, out_ref.shape), swapped_ref[...], mine_ref[...])
 
 
-def pack_keys_kernel(completing_ref, pairs_ref, picked_ref, late_ref, handed_ref, out_ref):
-    upper = lax.axis_index("half") == 1
-    handed = jnp.broadcast_to(jnp.where(upper, completing_ref[...], 2) < 2, handed_ref.shape)
-    late = jnp.logical_and(upper, lax.axis_index("core") == 1)
-    clean = jnp.where(handed, handed_ref[...], jnp.where(late, late_ref[...], picked_ref[...]))
+def pack_keys_kernel(axis, pairs_ref, mine_ref, got_ref, out_ref):
+    clean = jnp.where(lax.axis_index(axis) == 1, got_ref[...], mine_ref[...])
     for h in range(KV_HEADS):
         first = (h % 2) * 3 * HEAD_DIM
         near = pairs_ref[h // 2, :, (h % 2) * 2 * HEAD_DIM : (h % 2 + 1) * 2 * HEAD_DIM]
@@ -238,36 +234,33 @@
     anywhere = pl.BlockSpec(memory_space=pl.ANY)
 
     width = heads * HEAD_DIM
+    finished = completing.reshape(1, 1)
     core = lax.axis_index("core")
-    mine = jnp.where(core == 0, clean_key[0], clean_value[0])
-    sent = jnp.where(core == 0, clean_value[0], clean_key[0])
-    swapped = lax.ppermute(sent, ("half", "core"), [(0, 1), (1, 0)])
-    finished = completing.reshape(1, 1)
-    picked = call(pick_kernel, shaped(tok, width), [VMEM] * 3, finished, mine, swapped)
-    handed = lax.ppermute(
-        picked, ("half",) + z_all, [(z, depth + (z + depth // 2) % depth) for z in range(depth)]
-    )
-    near = jnp.stack([jnp.where(picked != picked, picked, a[0]) for a in (key, value)])
-    pairs, late = call(
-        pair_kernel,
-        (shaped(heads // 2, tok, 4 * HEAD_DIM), shaped(tok, width)),
-        [VMEM] * 2 + [anywhere],
-        near,
-        sent,
-        picked,
-    )
-    late = lax.ppermute(late, ("half", "core"), [(2, 3)])
-
-    kv = call(
-        pack_keys_kernel,
-        shaped(depth, tok, 6 * HEAD_DIM),
-        [VMEM] * 5,
-        finished,
-        pairs,
-        picked,
-        late,
-        handed,
-    )
+
+    def packed(axis, near, mine, got):
+        near = call(pair_kernel, shaped(heads // 2, tok, 4 * HEAD_DIM), [VMEM, anywhere], near, mine)
+        return call(
+            functools.partial(pack_keys_kernel, axis), shaped(depth, tok, 6 * HEAD_DIM), [VMEM] * 3, near, mine, got
+        )
+
+    def handed_over(key, value, clean_key, clean_value, finished):
+        mine = jnp.where(core == 0, clean_key[0], clean_value[0])
+        sent = jnp.where(core == 0, clean_value[0], clean_key[0])
+        swapped = lax.ppermute(sent, ("half", "core"), [(0, 1), (1, 0)])
+        picked = call(pick_kernel, shaped(tok, width), [VMEM] * 3, finished, mine, swapped)
+        handed = lax.ppermute(
+            picked, ("half",) + z_all, [(z, depth + (z + depth // 2) % depth) for z in range(depth)]
+        )
+        near = jnp.stack([jnp.where(picked != picked, picked, a[0]) for a in (key, value)])
+        return packed("half", near, picked, handed)
+
+    def kept(key, value, clean_key, clean_value, finished):
+        del finished
+        mine = jnp.where(core == 0, clean_key[0], clean_value[0])
+        got = lax.ppermute(clean_value[0], ("half", "core"), [(2, 3)])
+        return packed("core", jnp.stack([key[0], value[0]]), mine, got)
+
+    kv = lax.cond(completing[0] < 2, handed_over, kept, key, value, clean_key, clean_value, finished)
     part = heads // 2
     keep, send = pl.pallas_call(
         stage_kernel,

time: 73.6 us -> 81.5 us (1.11)
  the two profiles are of different devices: /device:TPU:384 before, /device:TPU:1 now
where the time goes in v9:
time: 81.5 us; the launch traced here: 80.9 us
  starting transfers between devices  41.6 us (51%)
  waiting for transfers between devices  19.8 us (24%)
  blocking collectives  8.38 us (10%)
  Pallas kernels  7.9 us (10%)
  other arithmetic  1.58 us (2%)
  local copies, waits for them, and re-layouts  0.84 us (1%)
    ppermute x1, starting transfers between devices, handed_over(): swapped = lax.ppermute(sent, ('half', 'core'), [(0, 1), (1, 0)])  8.78 us
    all_to_all x1, blocking collectives, shards(): lax.all_to_all(out, served_by, 0, 0, axis_index_groups=[SERVE_ORDER], til...  8.38 us
    pallas_call x10, Pallas kernels, call(): pl.pallas_call(kernel, out_shape=out_shape, in_specs=specs, out_specs=out...  7.7 us
    ppermute x1, starting transfers between devices, with_clean(): other = lax.ppermute(clean, 'core', [(0, 1), (1, 0)])  7.66 us
    all_to_all x1, starting transfers between devices, gather(): own = lax.all_to_all(own, plane_axes, 0, 0, tiled=True)  6.75 us
    all_to_all x1, starting transfers between devices, shards(): lax.all_to_all(kv, z_all, 0, 0, axis_index_groups=[Z_ORDER], tiled=True)  6.19 us
    all_to_all x1, waiting for transfers between devices, gather(): own = lax.all_to_all(own, plane_axes, 0, 0, tiled=True)  6.09 us
    ppermute x1, waiting for transfers between devices, gather(): got = lax.ppermute(send, 'zc', [(z, z ^ 2) for z in range(4)])  4.65 us
  transfers between devices with their start and end apart: 8, of which 7 were waited for; matrix products, arithmetic and copies ran while one was open for 1% of the time, Pallas kernels for 3%

profile of v9, /device:TPU:1, one launch (start us, length us, event | category | flops | bytes accessed | tf_op | source)
XLA Modules:
  0.0 80.9 jit_solution(477329155891820882)
XLA Ops:
  0.7 17.2 %conditional.2 = (bf16[8,16,768]{2,1,0:T(8,128)(2,1)}) conditional(s32[]{:T(128)} %convert_element_type.7, (bf16[1,16,1024]{2,1,0:T(8,128)(2,1)}, bf16[1,16,1024]{2,1,0:T(8,128)(2,1)}, s32[]{:T(128)}, bf16[1,16,1024]{2,1,0:T(8,128)(2,1)}, bf16[1,16,1024]{2,1,0:T(8,128)(2,1)}) %tuple.17, (s32[]{:T(128)}, bf16[1,16,1024]{2,1,0:T(8,128)(2,1)}, ...), branch_computations={%region_0.1_spmd, %region_1.2_spmd} | conditional | flops 114689 | bytes 688226 | solution.py:263
  0.7 0.8 select_bitcast_fusion
  1.5 8.8 %collective-permute-start.6 = (bf16[16,1024]{1,0:T(8,128)(2,1)S(1)}, bf16[16,1024]{1,0:T(8,128)(2,1)S(1)}, u32[]{:S(2)}, u32[]{:S(2)}) collective-permute-start(bf16[16,1024]{1,0:T(8,128)(2,1)S(1)} %get-tuple-element.84), channel_id=1, source_target_pairs={{0,128},{128,0},{1,129},{129,1},{2,130},{130,2},{3,131},{131,3},{4... | collective-permute-start | bytes 98312 | tf_op jit(solution)/shard_map/cond/branch_1_fun/ppermute | solution.py:249
  10.3 0.8 %collective-permute-done.6.swapped_ref = bf16[16,1024]{1,0:T(8,128)(2,1)S(1)} collective-permute-done((bf16[16,1024]{1,0:T(8,128)(2,1)S(1)}, bf16[16,1024]{1,0:T(8,128)(2,1)S(1)}, u32[]{:S(2)}, u32[]{:S(2)}) %collective-permute-start.6) | collective-permute-done | bytes 32800 | tf_op jit(solution)/shard_map/cond/branch_1_fun/ppermute | solution.py:249
  11.1 0.7 branch_1_fun.9.after_ref.mine_ref
  11.9 4.3 %collective-permute-start.7 = (bf16[16,1024]{1,0:T(8,128)(2,1)S(1)}, bf16[16,1024]{1,0:T(8,128)(2,1)S(1)}, u32[]{:S(2)}, u32[]{:S(2)}) collective-permute-start(bf16[16,1024]{1,0:T(8,128)(2,1)S(1)} %branch_1_fun.9.after_ref.mine_ref), channel_id=1, source_target_pairs={{0,320},{16,336},{32,352},{48,368},{64,256},{80,272},{96,288},{112... | collective-permute-start | bytes 98312 | tf_op jit(solution)/shard_map/cond/branch_1_fun/ppermute | solution.py:251
  16.2 0.8 fusion
  17.0 0.2 collective-permute-done.7.got_ref
  17.2 0.7 branch_1_fun.11
  17.9 6.2 %all-to-all-start.2 = ((bf16[8,16,768]{2,1,0:T(8,128)(2,1)}), bf16[8,16,768]{2,1,0:T(8,128)(2,1)S(1)}, u32[]{:S(2)}, u32[]{:S(2)}) async-start(bf16[8,16,768]{2,1,0:T(8,128)(2,1)} %get-tuple-element.88.after_ref), calls=%async_computation.2 | async-start | bytes 393216 | tf_op jit(solution)/shard_map/all_to_all | solution.py:276
  24.1 0.0 copy-done
  24.1 0.2 shard_map.74
  24.3 3.1 %collective-permute-start.8 = (bf16[4,16,768]{2,1,0:T(8,128)(2,1)S(1)}, bf16[4,16,768]{2,1,0:T(8,128)(2,1)S(1)}, u32[]{:S(2)}, u32[]{:S(2)}) collective-permute-start(bf16[4,16,768]{2,1,0:T(8,128)(2,1)S(1)} %get-tuple-element.79), channel_id=1, source_target_pairs={{0,4},{4,0},{1,5},{5,1},{2,6},{6,2},{3,7},{7,3},{8,12},{12,8},{9,1... | collective-permute-start | bytes 294920 | tf_op jit(solution)/shard_map/ppermute | solution.py:273
  27.4 2.5 %collective-permute-done.8.got_ref = bf16[4,16,768]{2,1,0:T(8,128)(2,1)S(1)} collective-permute-done((bf16[4,16,768]{2,1,0:T(8,128)(2,1)S(1)}, bf16[4,16,768]{2,1,0:T(8,128)(2,1)S(1)}, u32[]{:S(2)}, u32[]{:S(2)}) %collective-permute-start.8) | collective-permute-done | bytes 98336 | tf_op jit(solution)/shard_map/ppermute | solution.py:273
  30.0 2.1 %all-to-all-done.2 = bf16[8,16,768]{2,1,0:T(8,128)(2,1)S(1)} async-done(((bf16[8,16,768]{2,1,0:T(8,128)(2,1)}), bf16[8,16,768]{2,1,0:T(8,128)(2,1)S(1)}, u32[]{:S(2)}, u32[]{:S(2)}) %all-to-all-start.2) | async-done | bytes 196640 | tf_op jit(solution)/shard_map/all_to_all | solution.py:276
  32.1 0.0 copy-done.1
  32.1 39.6 %conditional.3 = (bf16[8,16,768]{2,1,0:T(8,128)(2,1)S(1)}) conditional(s32[]{:T(128)} %convert_element_type.6, (bf16[2,2,16,768]{3,2,1,0:T(8,128)(2,1)S(1)}, bf16[2,2,16,768]{3,2,1,0:T(8,128)(2,1)S(1)}, bf16[8,16,768]{2,1,0:T(8,128)(2,1)S(1)}) %tuple.19, (bf16[2,2,16,768]{3,2,1,0:T(8,128)(2,1)S(1)}, bf16[2,2,16,768]{3,2,1,0:T(8,128)(2,1)S(1)}, ...), branch_computations={%region_2.3_spmd, %region_3.4_spmd} | conditional | flops 1610612736 | bytes 15990944 | solution.py:328
  32.1 1.3 %branch_1_fun.14 = bf16[16,128,384]{2,1,0:T(8,128)(2,1)} custom-call(bf16[8,16,768]{2,1,0:T(8,128)(2,1)S(1)} %get-tuple-element.71.served_ref, bf16[2,2,16,768]{3,2,1,0:T(8,128)(2,1)S(1)} %get-tuple-element.67.kept_ref.after_ref), custom_call_target="tpu_custom_call" | custom-call | tf_op jit(solution)/shard_map/cond/branch_1_fun/pallas_call | solution.py:215
  33.4 6.8 %all-to-all-start.1 = ((bf16[16,128,384]{2,1,0:T(8,128)(2,1)}), bf16[16,128,384]{2,1,0:T(8,128)(2,1)S(1)}, u32[]{:S(2)}, u32[]{:S(2)}) async-start(bf16[16,128,384]{2,1,0:T(8,128)(2,1)} %branch_1_fun.14), calls=%async_computation.1 | async-start | bytes 3145728 | tf_op jit(solution)/shard_map/cond/branch_1_fun/all_to_all | solution.py:281
  40.2 1.9 %collective-permute-start.2 = (bf16[2,2,16,768]{3,2,1,0:T(8,128)(2,1)S(1)}, bf16[2,2,16,768]{3,2,1,0:T(8,128)(2,1)S(1)}, u32[]{:S(2)}, u32[]{:S(2)}) collective-permute-start(bf16[2,2,16,768]{3,2,1,0:T(8,128)(2,1)S(1)} %get-tuple-element.68), channel_id=1, source_target_pairs={{0,16},{16,0},{32,48},{48,32},{1,17},{17,1},{33,49},{49,33},{2,18}... | collective-permute-start | bytes 294920 | tf_op jit(solution)/shard_map/cond/branch_1_fun/ppermute | solution.py:282
  42.1 3.4 %collective-permute-done.2.got_ref = bf16[2,2,16,768]{3,2,1,0:T(8,128)(2,1)S(1)} collective-permute-done((bf16[2,2,16,768]{3,2,1,0:T(8,128)(2,1)S(1)}, bf16[2,2,16,768]{3,2,1,0:T(8,128)(2,1)S(1)}, u32[]{:S(2)}, u32[]{:S(2)}) %collective-permute-start.2) | collective-permute-done | bytes 98336 | tf_op jit(solution)/shard_map/cond/branch_1_fun/ppermute | solution.py:282
  45.5 2.8 %collective-permute-start.3 = (bf16[2,2,16,768]{3,2,1,0:T(8,128)(2,1)S(1)}, bf16[2,2,16,768]{3,2,1,0:T(8,128)(2,1)S(1)}, u32[]{:S(2)}, u32[]{:S(2)}) collective-permute-start(bf16[2,2,16,768]{3,2,1,0:T(8,128)(2,1)S(1)} %get-tuple-element.70), channel_id=1, source_target_pairs={{0,32},{16,48},{32,0},{48,16},{1,33},{17,49},{33,1},{49,17},{2,34}... | collective-permute-start | bytes 294920 | tf_op jit(solution)/shard_map/cond/branch_1_fun/ppermute | solution.py:284
  48.4 4.7 %collective-permute-done.3.got_ref = bf16[2,2,16,768]{3,2,1,0:T(8,128)(2,1)S(1)} collective-permute-done((bf16[2,2,16,768]{3,2,1,0:T(8,128)(2,1)S(1)}, bf16[2,2,16,768]{3,2,1,0:T(8,128)(2,1)S(1)}, u32[]{:S(2)}, u32[]{:S(2)}) %collective-permute-start.3) | collective-permute-done | bytes 98336 | tf_op jit(solution)/shard_map/cond/branch_1_fun/ppermute | solution.py:284
  53.1 6.1 %all-to-all-done.1.kv_ref = bf16[16,128,384]{2,1,0:T(8,128)(2,1)S(1)} async-done(((bf16[16,128,384]{2,1,0:T(8,128)(2,1)}), bf16[16,128,384]{2,1,0:T(8,128)(2,1)S(1)}, u32[]{:S(2)}, u32[]{:S(2)}) %all-to-all-start.1) | async-done | bytes 1572896 | tf_op jit(solution)/shard_map/cond/branch_1_fun/all_to_all | solution.py:281
  59.1 0.1 branch_1_fun.15
  59.2 7.7 %collective-permute-start.4 = (bf16[16,128,128]{2,1,0:T(8,128)(2,1)S(1)}, bf16[16,128,128]{2,1,0:T(8,128)(2,1)S(1)}, u32[]{:S(2)}, u32[]{:S(2)}) collective-permute-start(bf16[16,128,128]{2,1,0:T(8,128)(2,1)S(1)} %branch_1_fun.15), channel_id=1, source_target_pairs={{0,128},{128,0},{1,129},{129,1},{2,130},{130,2},{3,131},{131,3},{4... | collective-permute-start | bytes 1572872 | tf_op jit(solution)/shard_map/cond/branch_1_fun/ppermute | solution.py:290
  66.9 1.9 %branch_1_fun.16 = (f32[768,256]{1,0:T(8,128)S(1)}, f32[768,128]{1,0:T(8,128)S(1)}) custom-call(bf16[8,16,768]{2,1,0:T(8,128)(2,1)S(1)} %branch_1_fun.13.after_ref.q_ref, bf16[16,128,384]{2,1,0:T(8,128)(2,1)S(1)} %all-to-all-done.1.kv_ref), custom_call_target="tpu_custom_call" | custom-call | flops 805306368 | bytes 4194304 | tf_op jit(solution)/shard_map/cond/branch_1_fun/pallas_call | solution.py:215
  68.9 0.0 collective-permute-done.4.other_ref
  68.9 2.9 %branch_1_fun.17 = bf16[8,16,768]{2,1,0:T(8,128)(2,1)S(1)} custom-call(s32[1,1]{1,0:T(1,128)} %get-tuple-element.65.completing_ref, s32[4,4]{1,0:T(4,128)S(1)} %get-tuple-element.83.mask_ref, bf16[8,16,768]{2,1,0:T(8,128)(2,1)S(1)} %branch_1_fun.13.after_ref.q_ref, bf16[16,128,384]{2,1,0:T(8,128)(2,1)S(1)} %all-to-all-done.1.kv_ref, ...), custom_call_target="tpu_custom_call" | custom-call | flops 805306368 | bytes 4194304 | tf_op jit(solution)/shard_map/cond/branch_1_fun/pallas_call | solution.py:215
  71.7 8.4 %all_to_all.18 = bf16[8,16,768]{2,1,0:T(8,128)(2,1)S(1)} all-to-all(bf16[8,16,768]{2,1,0:T(8,128)(2,1)S(1)} %get-tuple-element.89), channel_id=1, replica_groups={{16,20,32,36,48,52,0,4},{17,21,33,37,49,53,1,5},{18,22,34,38,50,54,2,6}..., dimensions={0} | all-to-all | bytes 393216 | tf_op jit(solution)/shard_map/all_to_all | solution.py:329
  80.1 0.1 copy.9
  80.2 0.8 reshape.11
  (7 shorter events, 0.1 us)
Async XLA Ops:
  0.0 24.1 %copy-start = (bf16[1,16,6144]{2,1,0:T(8,128)(2,1)S(1)}, bf16[1,16,6144]{2,1,0:T(8,128)(2,1)}, u32[]{:S(2)}) copy-start(bf16[1,16,6144]{2,1,0:T(8,128)(2,1)} %query_ref.1) | copy-start | bytes 589828
  0.0 32.1 %copy-start.1 = (s32[4,4]{1,0:T(4,128)S(1)}, s32[4,4]{1,0:T(4,128)}, u32[]{:S(2)}) copy-start(s32[4,4]{1,0:T(4,128)} %param.17) | copy-start | bytes 196
  1.5 9.6 %collective-permute-start.6 = (bf16[16,1024]{1,0:T(8,128)(2,1)S(1)}, bf16[16,1024]{1,0:T(8,128)(2,1)S(1)}, u32[]{:S(2)}, u32[]{:S(2)}) collective-permute-start(bf16[16,1024]{1,0:T(8,128)(2,1)S(1)} %get-tuple-element.84), channel_id=1, source_target_pairs={{0,128},{128,0},{1,129},{129,1},{2,130},{130,2},{3,131},{131,3},{4... | collective-permute-start | bytes 98312 | tf_op jit(solution)/shard_map/cond/branch_1_fun/ppermute | solution.py:249
  11.9 5.3 %collective-permute-start.7 = (bf16[16,1024]{1,0:T(8,128)(2,1)S(1)}, bf16[16,1024]{1,0:T(8,128)(2,1)S(1)}, u32[]{:S(2)}, u32[]{:S(2)}) collective-permute-start(bf16[16,1024]{1,0:T(8,128)(2,1)S(1)} %branch_1_fun.9.after_ref.mine_ref), channel_id=1, source_target_pairs={{0,320},{16,336},{32,352},{48,368},{64,256},{80,272},{96,288},{112... | collective-permute-start | bytes 98312 | tf_op jit(solution)/shard_map/cond/branch_1_fun/ppermute | solution.py:251
  17.9 14.2 %all-to-all-start.2 = ((bf16[8,16,768]{2,1,0:T(8,128)(2,1)}), bf16[8,16,768]{2,1,0:T(8,128)(2,1)S(1)}, u32[]{:S(2)}, u32[]{:S(2)}) async-start(bf16[8,16,768]{2,1,0:T(8,128)(2,1)} %get-tuple-element.88.after_ref), calls=%async_computation.2 | async-start | bytes 393216 | tf_op jit(solution)/shard_map/all_to_all | solution.py:276
  24.3 5.7 %collective-permute-start.8 = (bf16[4,16,768]{2,1,0:T(8,128)(2,1)S(1)}, bf16[4,16,768]{2,1,0:T(8,128)(2,1)S(1)}, u32[]{:S(2)}, u32[]{:S(2)}) collective-permute-start(bf16[4,16,768]{2,1,0:T(8,128)(2,1)S(1)} %get-tuple-element.79), channel_id=1, source_target_pairs={{0,4},{4,0},{1,5},{5,1},{2,6},{6,2},{3,7},{7,3},{8,12},{12,8},{9,1... | collective-permute-start | bytes 294920 | tf_op jit(solution)/shard_map/ppermute | solution.py:273
  33.4 25.7 %all-to-all-start.1 = ((bf16[16,128,384]{2,1,0:T(8,128)(2,1)}), bf16[16,128,384]{2,1,0:T(8,128)(2,1)S(1)}, u32[]{:S(2)}, u32[]{:S(2)}) async-start(bf16[16,128,384]{2,1,0:T(8,128)(2,1)} %branch_1_fun.14), calls=%async_computation.1 | async-start | bytes 3145728 | tf_op jit(solution)/shard_map/cond/branch_1_fun/all_to_all | solution.py:281
  40.2 5.4 %collective-permute-start.2 = (bf16[2,2,16,768]{3,2,1,0:T(8,128)(2,1)S(1)}, bf16[2,2,16,768]{3,2,1,0:T(8,128)(2,1)S(1)}, u32[]{:S(2)}, u32[]{:S(2)}) collective-permute-start(bf16[2,2,16,768]{3,2,1,0:T(8,128)(2,1)S(1)} %get-tuple-element.68), channel_id=1, source_target_pairs={{0,16},{16,0},{32,48},{48,32},{1,17},{17,1},{33,49},{49,33},{2,18}... | collective-permute-start | bytes 294920 | tf_op jit(solution)/shard_map/cond/branch_1_fun/ppermute | solution.py:282
  45.5 7.5 %collective-permute-start.3 = (bf16[2,2,16,768]{3,2,1,0:T(8,128)(2,1)S(1)}, bf16[2,2,16,768]{3,2,1,0:T(8,128)(2,1)S(1)}, u32[]{:S(2)}, u32[]{:S(2)}) collective-permute-start(bf16[2,2,16,768]{3,2,1,0:T(8,128)(2,1)S(1)} %get-tuple-element.70), channel_id=1, source_target_pairs={{0,32},{16,48},{32,0},{48,16},{1,33},{17,49},{33,1},{49,17},{2,34}... | collective-permute-start | bytes 294920 | tf_op jit(solution)/shard_map/cond/branch_1_fun/ppermute | solution.py:284
  59.2 9.6 %collective-permute-start.4 = (bf16[16,128,128]{2,1,0:T(8,128)(2,1)S(1)}, bf16[16,128,128]{2,1,0:T(8,128)(2,1)S(1)}, u32[]{:S(2)}, u32[]{:S(2)}) collective-permute-start(bf16[16,128,128]{2,1,0:T(8,128)(2,1)S(1)} %branch_1_fun.15), channel_id=1, source_target_pairs={{0,128},{128,0},{1,129},{129,1},{2,130},{130,2},{3,131},{131,3},{4... | collective-permute-start | bytes 1572872 | tf_op jit(solution)/shard_map/cond/branch_1_fun/ppermute | solution.py:290
